TPU v7x, 256 devices: a whole 4x4x8 slice. The times are simulated.
256 devices in a mesh: space: 4 (over z_lo, core), tins: 4 (over y), tsink: 16 (over z_hi, x).
Axes of the slice: x: 4, y: 4, z: 8 (z_hi: 4, z_lo: 2; z = z_hi * 2 + z_lo), core: 2. Of those that a mesh axis runs over, the one named last changes fastest.
Arguments:
- eigvecs: float32 [4, 2, 3, 128, 16, 256], P('tins', None, None, 'tsink', 'space'), may hold values from -0.375 to 0.375
- links: float32 [4, 3, 2, 3, 3, 16, 256], P('tins', None, None, None, None, 'space'), may hold values from -3.5 to 3.5
- momenta: int32 [2, 3], replicated, may hold values from -2 to 2
- directions: int32 [3], replicated, may hold values from 0 to 2
- ins_time: int32 [4], P('tins'), may hold values from 0 to 3, as said below
- sink_time: int32 [16], P('tsink'), may hold values from 1 to 4
- sink_peramb: float32 [16, 4, 2, 512, 512], P('tsink', 'tins', None, 'space'), may hold values from -0.375 to 0.375
- source_peramb: float32 [4, 2, 512, 512], P('tins'), may hold values from -0.1875 to 0.1875
Outputs:
- gen_peramb: float32 [512, 16, 6, 2, 512], P('tins', 'tsink', None, None, 'space')
Inputs may be any that keep to these rules, and one draw needn't show every extreme that they name: `ins_time`: each lattice timeslice of the window appears in exactly one slot. `sink_time`: sink timeslices on the numbering of ins_time. `momenta`: momentum components in units of 2 pi / 16. `directions`: 0 is x, 1 is y, 2 is z.
All inputs are finite; a program needn't handle non-finite values.
Results may differ from a plain program's by a relative error of at most 0.0003.
Values sent between devices are 32-bit elements; how exact they have to be, the bound alone decides.
No kernel may reach another device: no remote copies, remote signals or barrier semaphores. Data moves between devices by JAX's collectives and lax.ppermute only.
A program may use at most 64 MiB of HBM per device.

v0:
```python
import math

import jax
import jax.numpy as jnp
from jax import lax
from jax.sharding import PartitionSpec as P

L = 16
NSPIN = 4


HIGHEST = lax.Precision.HIGHEST


def padded_2(cells, sides, width):
    for axis, dim in sides:
        count = lax.axis_size(axis)
        head = lax.slice_in_dim(cells, 0, width, axis=dim)
        tail = lax.slice_in_dim(cells, cells.shape[dim] - width, cells.shape[dim], axis=dim)
        cells = jnp.concatenate(
            [
                lax.ppermute(tail, axis, [(i, (i + 1) % count) for i in range(count)]),
                cells,
                lax.ppermute(head, axis, [((i + 1) % count, i) for i in range(count)]),
            ],
            axis=dim,
        )
    return cells


def from_behind(block, axis, distance):
    devices = range(lax.axis_size(axis))
    route = [((i - distance) % len(devices), i) for i in devices]
    return lax.ppermute(block, axis, route)


def plane_shift(source, axis_dir, step_sign, side_len):
    if axis_dir == 1:
        return jnp.roll(source, -step_sign * side_len, axis=-1)
    column = lax.broadcasted_iota(jnp.int32, (side_len * side_len,), 0) % side_len
    if step_sign == 1:
        return jnp.where(
            column == side_len - 1,
            jnp.roll(source, side_len - 1, axis=-1),
            jnp.roll(source, -1, axis=-1),
        )
    return jnp.where(
        column == 0, jnp.roll(source, 1 - side_len, axis=-1), jnp.roll(source, 1, axis=-1)
    )


def color_apply(link_mat, vector, adjoint):
    link_re, link_im = (link_mat[:, 0], link_mat[:, 1])
    vec_re, vec_im = (vector[:, 0], vector[:, 1])
    rows_real = []
    rows_imag = []
    for colour in range(3):
        sum_real = jnp.zeros_like(vec_re[:, 0])
        sum_imag = jnp.zeros_like(vec_re[:, 0])
        for inner in range(3):
            if adjoint:
                here_re = link_re[:, inner, colour][:, None]
                here_im = -link_im[:, inner, colour][:, None]
            else:
                here_re = link_re[:, colour, inner][:, None]
                here_im = link_im[:, colour, inner][:, None]
            sum_real = sum_real + here_re * vec_re[:, inner] - here_im * vec_im[:, inner]
            sum_imag = sum_imag + here_re * vec_im[:, inner] + here_im * vec_re[:, inner]
        rows_real.append(sum_real)
        rows_imag.append(sum_imag)
    return jnp.stack([jnp.stack(rows_real, axis=1), jnp.stack(rows_imag, axis=1)], axis=1)


def covariant(link_here, link_below, vec_above, vec_below):
    return color_apply(link_here, vec_above, False) - color_apply(link_below, vec_below, True)


def plane_derivs(vectors, link_all, side_len):
    result = []
    for axis_dir in range(2):
        link_here = link_all[:, axis_dir]
        vec_above = plane_shift(vectors, axis_dir, 1, side_len)
        vec_below = plane_shift(vectors, axis_dir, -1, side_len)
        link_below = plane_shift(link_here, axis_dir, -1, side_len)
        result.append(covariant(link_here, link_below, vec_above, vec_below))
    return result


def phase_factors(momenta, z_coord, side_len):
    site_index = lax.broadcasted_iota(jnp.int32, (side_len * side_len,), 0)
    x_coord = site_index % side_len
    y_coord = site_index // side_len
    product = (
        momenta[:, 0, None, None] * x_coord[None, None, :]
        + momenta[:, 1, None, None] * y_coord[None, None, :]
        + momenta[:, 2, None, None] * z_coord[None, :, None]
    )
    angles = 2.0 * math.pi / side_len * jnp.mod(product, side_len).astype(jnp.float32)
    return (jnp.cos(angles), jnp.sin(angles))


def phase_kets(derivative, directions, momenta, z_coord, side_len):
    onehot = (directions[:, None] == jnp.arange(3, dtype=jnp.int32)[None, :]).astype(jnp.float32)
    chosen = jnp.zeros((derivative.shape[1], onehot.shape[0]) + derivative.shape[2:], jnp.float32)
    for axis_dir in range(3):
        chosen = (
            chosen
            + onehot[None, :, axis_dir, None, None, None, None, None]
            * derivative[axis_dir][:, None]
        )
    cos_part, sine_part = phase_factors(momenta, z_coord, side_len)
    cos_part = cos_part[None, :, None, None, None, :, :]
    sine_part = sine_part[None, :, None, None, None, :, :]
    disp_real = chosen[:, None, :, 0]
    disp_imag = chosen[:, None, :, 1]
    wave_real = cos_part * disp_real + sine_part * disp_imag
    wave_imag = cos_part * disp_imag - sine_part * disp_real
    stacked = jnp.concatenate([wave_real, wave_imag], axis=3)
    shape_now = stacked.shape
    return stacked.reshape((shape_now[0], shape_now[1] * shape_now[2]) + shape_now[3:])


def elemental_part(bra_waves, ket_waves, pattern):
    swapped = jnp.concatenate([ket_waves[:, :, 3:], -ket_waves[:, :, :3]], axis=2)
    real_part = jnp.einsum(pattern, bra_waves, ket_waves, precision=HIGHEST)
    imag_part = jnp.einsum(pattern, bra_waves, swapped, precision=HIGHEST)
    return jnp.stack([real_part, imag_part], axis=2)


def left_product(row_block, elemental, weight):
    count_t = row_block.shape[0]
    row_count = row_block.shape[2]
    order_m = row_block.shape[3]
    split_rows = row_block.reshape(count_t, 2, row_count, NSPIN, order_m // NSPIN)
    rows_re, rows_im = (split_rows[:, 0], split_rows[:, 1])
    elem_re, elem_im = (elemental[:, :, 0], elemental[:, :, 1])

    def contract(first_op, second_op):
        return jnp.einsum("trsa,tqba->tqrsb", first_op, second_op, precision=HIGHEST)

    spin_sign = jnp.where(jnp.arange(NSPIN) < 2, 1.0, -1.0).astype(jnp.float32)
    factor = weight[:, None, None, None, None] * spin_sign[None, None, None, :, None]
    left_re = factor * (contract(rows_re, elem_re) - contract(rows_im, elem_im))
    left_im = factor * (contract(rows_re, elem_im) + contract(rows_im, elem_re))
    pairs = elemental.shape[1]
    return (
        left_re.reshape(count_t, pairs, row_count, order_m),
        left_im.reshape(count_t, pairs, row_count, order_m),
    )


def right_product(left_re, left_im, src_re, src_im):

    def contract(first_op, second_op):
        return jnp.einsum("tqrk,tkc->cqr", first_op, second_op, precision=HIGHEST)

    gen_re = contract(left_re, src_re) - contract(left_im, src_im)
    gen_im = contract(left_re, src_im) + contract(left_im, src_re)
    return jnp.stack([gen_re, gen_im], axis=2)


def on_device(eigvecs, links, momenta, directions, ins_time, sink_time, sink_peramb, source_peramb):
    z_depth = eigvecs.shape[4]
    count_t = eigvecs.shape[0]
    padded = padded_2(eigvecs, (("space", 4),), 1)
    low_plane = from_behind(links[:, 2, :, :, :, z_depth - 1 :, :], "space", 1)
    link_z = links[:, 2]
    link_below_z = jnp.concatenate([low_plane, link_z[:, :, :, :, : z_depth - 1]], axis=4)
    derivs = plane_derivs(eigvecs, links, L)
    derivs.append(
        covariant(link_z, link_below_z, padded[:, :, :, :, 2:], padded[:, :, :, :, :z_depth])
    )
    derivative = jnp.stack(derivs)
    z_coord = lax.axis_index("space") * z_depth + jnp.arange(z_depth, dtype=jnp.int32)
    ket_waves = phase_kets(derivative, directions, momenta, z_coord, L)
    bra_waves = eigvecs.reshape((count_t, 6) + eigvecs.shape[3:])
    partial_sum = elemental_part(
        lax.all_gather(bra_waves, "tsink", axis=2, tiled=True), ket_waves, "tkazp,tqkbzp->tqba"
    )
    summed = lax.psum(partial_sum, "space")
    elemental = lax.all_gather(summed, "tsink", axis=3, tiled=True)
    weight = (ins_time < sink_time[0]).astype(jnp.float32)
    left_re, left_im = left_product(sink_peramb[0], elemental, weight)
    source_re = source_peramb[:, 0]
    source_im = source_peramb[:, 1]
    generalized = lax.psum_scatter(
        right_product(left_re, left_im, source_re, source_im),
        "tins",
        scatter_dimension=0,
        tiled=True,
    )
    return generalized[:, None]


def solution(mesh):
    in_specs = (
        P("tins", None, None, "tsink", "space", None),
        P("tins", None, None, None, None, "space", None),
        P(),
        P(),
        P("tins"),
        P("tsink"),
        P("tsink", "tins", None, "space", None),
        P("tins", None, None, None),
    )
    out_specs = P("tins", "tsink", None, None, "space")
    return jax.shard_map(
        on_device, mesh=mesh, in_specs=in_specs, out_specs=out_specs, check_vma=False
    )
```

profile of v0, /device:TPU:1, one launch (start us, length us, event | category | flops | bytes accessed | tf_op | source)
XLA Modules:
  0.0 223.2 jit_solution(11165745261976049164)
XLA Ops:
  6.5 0.9 slice_bitcast_fusion.29
  7.5 3.1 %collective-permute-start.1 = (f32[1,2,3,3,1,256]{5,4,3,2,1,0:T(1,128)S(1)}, f32[1,2,3,3,1,256]{5,4,3,2,1,0:T(1,128)S(1)}, u32[]{:S(2)}, u32[]{:S(2)}) collective-permute-start(f32[1,2,3,3,1,256]{5,4,3,2,1,0:T(1,128)S(1)} %slice_bitcast_fusion.29), channel_id=1, source_target_pairs={{192,0},{0,64},{64,128},{128,192},{193,1},{1,65},{65,129},{129,193... | collective-permute-start | bytes 55304 | tf_op jit(solution)/shard_map/ppermute | solution.py:34
  10.6 1.1 fusion.86
  11.7 0.3 collective-permute-start
  12.0 1.5 collective-permute-start.2
  13.5 1.6 copy.21
  15.2 1.0 slice_bitcast_fusion.20
  16.2 0.1 slice.1067
  16.3 0.1 slice.1069
  16.4 0.2 fusion.81
  16.6 0.2 fusion.82
  16.8 0.1 fusion.80
  16.9 0.1 fusion.83
  17.1 0.2 fusion.85
  17.2 0.1 fusion.84
  17.4 0.1 maximum_select_fusion.2
  17.5 0.4 maximum_select_fusion
  18.0 0.1 slice.1127
  18.1 0.2 slice_reduce_fusion.2
  19.6 0.1 fusion.40
  19.8 0.2 fusion.30
  20.0 0.1 multiply_subtract_fusion.14
  20.0 0.1 multiply_subtract_fusion.13
  20.1 0.1 multiply_subtract_fusion.12
  20.2 0.1 multiply_subtract_fusion.17
  20.2 0.1 multiply_subtract_fusion.16
  20.3 0.1 multiply_subtract_fusion.15
  20.4 0.1 multiply_subtract_fusion.8
  20.4 0.1 maximum_subtract_fusion
  20.5 0.1 multiply_subtract_fusion.7
  20.6 0.1 multiply_subtract_fusion.6
  20.7 0.1 multiply_subtract_fusion.11
  20.7 0.1 multiply_subtract_fusion.10
  20.8 0.1 multiply_subtract_fusion.9
  20.9 0.1 maximum_subtract_fusion.1
  21.0 0.1 broadcast_multiply_fusion
  21.0 0.1 multiply_add_fusion.19
  21.1 0.2 fusion.74
  21.4 0.2 copy-done.2
  21.6 0.2 copy.22
  21.9 0.2 maximum_bitcast_fusion.8
  22.1 0.1 multiply_subtract_fusion.1
  22.2 0.1 multiply_subtract_fusion
  22.4 0.1 multiply_subtract_fusion.3
  22.4 0.1 maximum_subtract_fusion.2
  22.6 0.2 multiply_add_fusion
  22.9 0.3 fusion.24
  23.2 65.9 %all-gather.2.cloned.1.call-done = f32[1,6,128,4,256]{4,2,3,1,0:T(8,128)} async-done(((f32[1,6,8,4,256]{4,2,3,1,0:T(8,128)}), f32[1,6,128,4,256]{4,2,3,1,0:T(8,128)}) %all-gather.2.cloned.1.call-update) | async-done | bytes 3145744 | tf_op jit(solution)/shard_map/all_gather | solution.py:178
  89.1 5.4 %fusion.8 = f32[1,6,1,8,128]{4,3,1,2,0:T(8,128)S(1)} fusion(f32[1,6,128,4,256]{4,2,3,1,0:T(8,128)} %all-gather.2.cloned.1.call-done, f32[1,6,3,8,4,256]{5,3,4,2,1,0:T(8,128)S(1)} %get-tuple-element.10, f32[1,6,3,8,4,256]{5,3,4,2,1,0:T(8,128)S(1)} %get-tuple-element.8), kind=kOutput, calls=%fused_computation.15 | convolution fusion | flops 453279744 | bytes 4349952 | tf_op jit(solution)/shard_map/tkazp,tqkbzp->tqba/dot_general | solution.py:125
  94.5 3.3 %fusion.11 = f32[1,6,1,8,128]{4,3,1,2,0:T(8,128)S(1)} fusion(f32[1,6,128,4,256]{4,2,3,1,0:T(8,128)S(1)} %copy-done.5, f32[1,6,3,8,4,256]{5,3,4,2,1,0:T(8,128)S(1)} %get-tuple-element.9, f32[1,6,3,8,4,256]{5,3,4,2,1,0:T(8,128)S(1)} %get-tuple-element.10), kind=kOutput, calls=%fused_computation.16 | convolution fusion | flops 453279744 | bytes 4349952 | tf_op jit(solution)/shard_map/tkazp,tqkbzp->tqba/dot_general | solution.py:126
  97.9 10.8 %psum.7 = f32[1,6,2,8,128]{4,3,1,2,0:T(8,128)S(1)} all-reduce(f32[1,6,2,8,128]{4,3,1,2,0:T(8,128)S(1)} %pad_maximum_fusion.5), channel_id=1, replica_groups=mesh['space'=4,'tins'=4,'tsink'=16] {'space'}, use_global_device_ids=true, to_apply=%region_0.1 | all-reduce | flops 12288 | bytes 98304 | tf_op jit(solution)/shard_map/psum | solution.py:180
  108.7 42.5 %all_gather.7 = f32[1,6,2,128,128]{4,3,1,2,0:T(8,128)S(1)} all-gather(f32[1,6,2,8,128]{4,3,1,2,0:T(8,128)S(1)} %psum.7), channel_id=1, replica_groups=mesh['space'=4,'tins'=4,'tsink'=16] {'tsink'}, dimensions={3}, use_global_device_ids=true | all-gather | bytes 835584 | tf_op jit(solution)/shard_map/all_gather | solution.py:181
  151.2 1.4 fusion.27
  152.6 1.4 fusion.26
  154.0 1.5 bitcast_multiply_fusion.1
  155.5 0.1 copy-done.1
  155.6 2.7 %fusion.15 = f32[6,128,512]{2,1,0:T(8,128)S(1)} fusion(f32[6,128,512]{1,2,0:T(8,128)S(1)} %bitcast.422, f32[1,2,512,512]{3,2,1,0:T(8,128)S(1)} %copy-done.1), kind=kOutput, calls=%fused_computation.18 | convolution fusion | flops 2415919104 | bytes 4194304 | tf_op jit(solution)/shard_map/tqrk,tkc->cqr/dot_general | solution.py:155
  158.3 2.7 %fusion.17 = f32[6,128,512]{2,1,0:T(8,128)S(1)} fusion(f32[6,128,512]{1,2,0:T(8,128)S(1)} %bitcast.423, f32[1,2,512,512]{3,2,1,0:T(8,128)S(1)} %copy-done.1), kind=kOutput, calls=%fused_computation.20 | convolution fusion | flops 2415919104 | bytes 4194304 | tf_op jit(solution)/shard_map/tqrk,tkc->cqr/dot_general | solution.py:155
  161.0 1.5 bitcast_multiply_fusion
  162.4 2.9 %subtract_bitcast_fusion = f32[512,6,1,128]{0,3,1,2:T(8,128)S(1)} fusion(f32[6,128,512]{2,1,0:T(8,128)S(1)} %fusion.15, f32[6,128,512]{1,2,0:T(8,128)S(1)} %bitcast.420, f32[1,2,512,512]{3,2,1,0:T(8,128)S(1)} %copy-done.1), kind=kOutput, calls=%fused_computation.8 | convolution fusion | flops 2416312320 | bytes 5767168 | tf_op jit(solution)/shard_map/tqrk,tkc->cqr/dot_general | solution.py:155
  165.4 2.7 %add_bitcast_fusion = f32[512,6,1,128]{0,3,1,2:T(8,128)S(1)} fusion(f32[6,128,512]{2,1,0:T(8,128)S(1)} %fusion.17, f32[6,128,512]{1,2,0:T(8,128)S(1)} %bitcast.421, f32[1,2,512,512]{3,2,1,0:T(8,128)S(1)} %copy-done.1), kind=kOutput, calls=%fused_computation.7 | convolution fusion | flops 2416312320 | bytes 5767168 | tf_op jit(solution)/shard_map/tqrk,tkc->cqr/dot_general | solution.py:155
  168.1 1.9 pad_maximum_fusion
  170.1 44.2 %reduce-scatter.2.cloned.1.call-done = f32[128,6,2,128]{0,3,1,2:T(8,128)} async-done(((f32[512,6,2,128]{0,3,1,2:T(8,128)}), f32[128,6,2,128]{0,3,1,2:T(8,128)}) %reduce-scatter.2.cloned.1.call-update) | async-done | bytes 786448 | tf_op jit(solution)/shard_map/reduce_scatter | solution.py:186
  214.2 2.1 copy.29
  (51 shorter events, 0.8 us)
Async XLA Ops:
  6.5 9.9 %copy-start = (f32[1,2,3,8,4,256]{5,4,3,2,1,0:T(4,128)S(1)}, f32[1,2,3,8,4,256]{5,4,3,2,1,0:T(4,128)}, u32[]{:S(2)}) copy-start(f32[1,2,3,8,4,256]{5,4,3,2,1,0:T(4,128)} %param.8) | copy-start | bytes 589828
  6.5 82.6 %all-gather.2.cloned.1.call-start = ((), (), s32[]{:S(2)}) async-start(), calls=%async_computation.1 | async-start | bytes 3342336 | tf_op jit(solution)/shard_map/all_gather | solution.py:178
  7.5 14.3 %collective-permute-start.1 = (f32[1,2,3,3,1,256]{5,4,3,2,1,0:T(1,128)S(1)}, f32[1,2,3,3,1,256]{5,4,3,2,1,0:T(1,128)S(1)}, u32[]{:S(2)}, u32[]{:S(2)}) collective-permute-start(f32[1,2,3,3,1,256]{5,4,3,2,1,0:T(1,128)S(1)} %slice_bitcast_fusion.29), channel_id=1, source_target_pairs={{192,0},{0,64},{64,128},{128,192},{193,1},{1,65},{65,129},{129,193... | collective-permute-start | bytes 55304 | tf_op jit(solution)/shard_map/ppermute | solution.py:34
  11.7 10.1 %collective-permute-start = (f32[1,2,3,8,1,256]{5,4,3,2,1,0:T(1,128)S(1)}, f32[1,2,3,8,1,256]{5,4,3,2,1,0:T(1,128)S(1)}, u32[]{:S(2)}, u32[]{:S(2)}) collective-permute-start(f32[1,2,3,8,1,256]{5,4,3,2,1,0:T(1,128)S(1)} %get-tuple-element.79), channel_id=1, source_target_pairs={{64,0},{128,64},{192,128},{0,192},{65,1},{129,65},{193,129},{1,193... | collective-permute-start | bytes 147464 | tf_op jit(solution)/shard_map/ppermute | solution.py:24
  12.0 9.8 %collective-permute-start.2 = (f32[1,2,3,8,1,256]{5,4,3,2,1,0:T(1,128)S(1)}, f32[1,2,3,8,1,256]{5,4,3,2,1,0:T(1,128)S(1)}, u32[]{:S(2)}, u32[]{:S(2)}) collective-permute-start(f32[1,2,3,8,1,256]{5,4,3,2,1,0:T(1,128)S(1)} %get-tuple-element.78), channel_id=1, source_target_pairs={{0,64},{64,128},{128,192},{192,0},{1,65},{65,129},{129,193},{193,1... | collective-permute-start | bytes 147464 | tf_op jit(solution)/shard_map/ppermute | solution.py:22
  15.2 199.1 %reduce-scatter.2.cloned.1.call-start = ((), (), s32[]{:S(2)}) async-start(), calls=%async_computation.2 | async-start | bytes 3932160 | tf_op jit(solution)/shard_map/reduce_scatter | solution.py:186
  17.4 0.7 copy-start.3
  20.4 0.7 copy-start.4
  20.5 1.0 copy-start.2
  89.1 5.4 %copy-start.5 = (f32[1,6,128,4,256]{4,2,3,1,0:T(8,128)S(1)}, f32[1,6,128,4,256]{4,2,3,1,0:T(8,128)}, u32[]{:S(2)}) copy-start(f32[1,6,128,4,256]{4,2,3,1,0:T(8,128)} %all-gather.2.cloned.1.call-done) | copy-start | bytes 9437188
  154.0 1.6 copy-start.1
Sparse Core Ops, SparseCore 0:
  15.3 73.7 all-gather.1
  170.2 44.0 reduce-scatter.1
where the time goes:
time: 223 us
  waiting for transfers between devices  110 us (49%)
  blocking collectives  53.3 us (24%)
  matrix products  25.5 us (11%)
  between operations  15.3 us (7%)
  local copies, waits for them, and re-layouts  8.92 us (4%)
  other arithmetic  5.1 us (2%)
  starting transfers between devices  4.97 us (2%)
    all_gather x1, waiting for transfers between devices, on_device(): lax.all_gather(bra_waves, 'tsink', axis=2, tiled=True)  65.9 us
    reduce_scatter x1, waiting for transfers between devices, on_device(): lax.psum_scatter(right_product(left_re, left_im, source_re, source_im), '...  44.2 us
    all_gather x1, blocking collectives, on_device(): elemental = lax.all_gather(summed, 'tsink', axis=3, tiled=True)  42.5 us
    dot_general x4, matrix products, contract(): return jnp.einsum('tqrk,tkc->cqr', first_op, second_op, precision=HIGHEST)  11 us
    psum x1, blocking collectives, on_device(): summed = lax.psum(partial_sum, 'space')  10.8 us
    dot_general x4, matrix products, contract(): jnp.einsum('trsa,tqba->tqrsb', first_op, second_op, precision=HIGHEST)  5.76 us
    dot_general x1, matrix products, elemental_part(): real_part = jnp.einsum(pattern, bra_waves, ket_waves, precision=HIGHEST)  5.37 us
  transfers between devices with their start and end apart: 5, of which 2 were waited for; matrix products, arithmetic and copies ran while one was open for 4% of the time, Pallas kernels for 0%

commit v1 on v0

v1 whole, which is shorter than its diff:
```python
import functools
import math

import jax
import jax.numpy as jnp
from jax import lax
from jax.experimental import pallas as pl
from jax.experimental.pallas import tpu as pltpu
from jax.sharding import PartitionSpec as P

L = 16
NSPIN = 4
F32 = jnp.float32
BF16 = jnp.bfloat16
VMEM = pl.BlockSpec(memory_space=pltpu.VMEM)
SMEM = pl.BlockSpec(memory_space=pltpu.SMEM)


def params(mib):
    return pltpu.CompilerParams(vmem_limit_bytes=mib * 2**20)


def halves(value):
    high = value.astype(BF16)
    return high, (value - high.astype(F32)).astype(BF16)


def dot_three(first, second, dims):
    dot = functools.partial(
        lax.dot_general, dimension_numbers=(dims, ((), ())), preferred_element_type=F32
    )
    return dot(first[0], second[0]) + (dot(first[0], second[1]) + dot(first[1], second[0]))


def colour_product(link, vector, adjoint):
    out = []
    for colour in range(3):
        real = imag = None
        for inner in range(3):
            v_re, v_im = vector[inner], vector[3 + inner]
            if adjoint:
                u_re, u_im = link(inner, colour)
                terms = (u_re * v_re + u_im * v_im, u_re * v_im - u_im * v_re)
            else:
                u_re, u_im = link(colour, inner)
                terms = (u_re * v_re - u_im * v_im, u_re * v_im + u_im * v_re)
            real = terms[0] if real is None else real + terms[0]
            imag = terms[1] if imag is None else imag + terms[1]
        out.append((real, imag))
    return [pair[0] for pair in out] + [pair[1] for pair in out]


def shift_x(value, step, column):
    if step == 1:
        return jnp.where(
            column == L - 1, pltpu.roll(value, L - 1, 1), pltpu.roll(value, 127, 1)
        )
    return jnp.where(column == 0, pltpu.roll(value, 128 - L + 1, 1), pltpu.roll(value, 1, 1))


def shift_y(low, high, step, lane):
    if step == 1:
        low, high = pltpu.roll(low, 128 - L, 1), pltpu.roll(high, 128 - L, 1)
        own = lane < 128 - L
    else:
        low, high = pltpu.roll(low, L, 1), pltpu.roll(high, L, 1)
        own = lane >= L
    return jnp.where(own, low, high), jnp.where(own, high, low)


def elemental_kernel(place, *refs):
    bras, kets = refs[0:4], refs[4:8]
    links_xy, links_z, phase, turn, out, waves, phased, total, combined = refs[8:]
    space, z_hi, x_pos = place[0], place[1], place[2]
    lane = lax.broadcasted_iota(jnp.int32, (8, 128), 1)
    column = lane % L
    total[...] = jnp.zeros_like(total)

    def plane(z, carry):
        for block in range(4):
            row = pl.multiple_of(((x_pos + 4 - block) % 4) * 8, 8)
            bra = bras[block]

            def vec(z_at, half):
                lanes = slice(half * 128, half * 128 + 128)
                return [bra[z_at, comp, :, lanes] for comp in range(6)]

            here = [vec(z + 1, half) for half in range(2)]

            def store(axis, sign, values):
                base = (axis * 2 + sign) * 32
                for half in range(2):
                    for comp in range(6):
                        start = comp * 256 + half * 128
                        waves[pl.ds(base + row, 8), start : start + 128] = values[half][comp]

            for axis in range(3):

                def link(ref, z_at, first, half):
                    lanes = slice(half * 128, half * 128 + 128)

                    def get(a, b):
                        real = ref[z_at, first + a * 3 + b : first + a * 3 + b + 1, lanes]
                        imag = ref[z_at, first + 9 + a * 3 + b : first + 10 + a * 3 + b, lanes]
                        return real, imag

                    return get

                if axis < 2:
                    use = [link(links_xy, z, axis * 18, half) for half in range(2)]
                    below = use
                else:
                    use = [link(links_z, z + 1, 0, half) for half in range(2)]
                    below = [link(links_z, z, 0, half) for half in range(2)]
                if axis == 0:
                    above = [[shift_x(v, 1, column) for v in here[h]] for h in range(2)]
                elif axis == 1:
                    pairs = [shift_y(a, b, 1, lane) for a, b in zip(here[0], here[1])]
                    above = [[pair[h] for pair in pairs] for h in range(2)]
                else:
                    above = [vec(z + 2, half) for half in range(2)]
                store(axis, 0, [colour_product(use[h], above[h], False) for h in range(2)])
                source = here if axis < 2 else [vec(z, half) for half in range(2)]
                back = [colour_product(below[h], source[h], True) for h in range(2)]
                if axis == 0:
                    back = [[shift_x(v, -1, column) for v in back[h]] for h in range(2)]
                elif axis == 1:
                    pairs = [shift_y(a, b, -1, lane) for a, b in zip(back[0], back[1])]
                    back = [[pair[h] for pair in pairs] for h in range(2)]
                store(axis, 1, back)

        for block in range(4):
            row = pl.multiple_of(((z_hi + 4 - block) % 4) * 8, 8)
            ket = kets[block]
            for mom in range(2):
                cos = phase[z, mom * 2 : mom * 2 + 1, :]
                sin = phase[z, mom * 2 + 1 : mom * 2 + 2, :]
                for colour in range(3):
                    v_re, v_im = ket[z, colour], ket[z, 3 + colour]
                    w_re = cos * v_re + sin * v_im
                    w_im = cos * v_im - sin * v_re
                    first = slice(colour * 256, colour * 256 + 256)
                    second = slice(768 + colour * 256, 1024 + colour * 256)
                    phased[pl.ds(mom * 64 + row, 8), first] = w_re
                    phased[pl.ds(mom * 64 + row, 8), second] = w_im
                    phased[pl.ds(mom * 64 + 32 + row, 8), first] = w_im
                    phased[pl.ds(mom * 64 + 32 + row, 8), second] = -w_re
        total[...] += dot_three(halves(waves[...]), halves(phased[...]), ((1,), (1,)))
        return carry

    lax.fori_loop(0, 4, plane, 0)

    for block in range(6):
        combined[block] = total[block * 32 : block * 32 + 32, :]
    wide = lax.broadcasted_iota(jnp.int32, (32, 128), 1)
    is_real = wide % 64 < 32
    for pair in range(3):
        axis = place[3 + pair]
        ahead, back = combined[axis * 2], combined[axis * 2 + 1]
        added = ahead + back
        swapped = jnp.where(is_real, pltpu.roll(added, 96, 1), pltpu.roll(added, 32, 1))
        value = turn[0, pair : pair + 1, :] * (back - ahead) + turn[1, pair : pair + 1, :] * swapped
        for group in range(4):
            out[space ^ group, pair] = value[group * 8 : group * 8 + 8, :]


def elemental_blocks(place, bras, kets, links_xy, links_z, phase, turn):
    return pl.pallas_call(
        elemental_kernel,
        out_shape=jax.ShapeDtypeStruct((4, 3, 8, 128), F32),
        in_specs=[SMEM] + [VMEM] * 12,
        out_specs=VMEM,
        scratch_shapes=[
            pltpu.VMEM((192, 1536), F32),
            pltpu.VMEM((128, 1536), F32),
            pltpu.VMEM((192, 128), F32),
            pltpu.VMEM((6, 32, 128), F32),
        ],
        compiler_params=params(24),
        cost_estimate=pl.CostEstimate(flops=10**9, bytes_accessed=3 * 10**6, transcendentals=0),
        name="elementals",
    )(place, *bras, *kets, links_xy, links_z, phase, turn)


def prepare_kernel(weight, source, sink, src_hi, src_lo, sink_hi, sink_lo):
    for part in range(2):
        for spin in range(NSPIN):
            rows = [
                source[part, spin * 128 + i * 32 + j * 8 : spin * 128 + i * 32 + j * 8 + 8, :]
                for j in range(4)
                for i in range(4)
            ]
            turned = jnp.concatenate(rows, axis=0).T
            high, low = halves(turned)
            for block in range(4):
                sign = 1 if part == 0 else -1
                cols = slice(block * 128, block * 128 + 128)
                same = slice(part * 512 + spin * 128, part * 512 + spin * 128 + 128)
                other = slice((1 - part) * 512 + spin * 128, (1 - part) * 512 + spin * 128 + 128)
                src_hi[block, 0:128, same] = sign * high[cols]
                src_lo[block, 0:128, same] = sign * low[cols]
                src_hi[block, 128:256, other] = high[cols]
                src_lo[block, 128:256, other] = low[cols]
    for part in range(2):
        for spin in range(NSPIN):
            sign = 1.0 if spin < 2 else -1.0
            turned = sink[part, :, spin * 128 : spin * 128 + 128].T * (sign * weight[0])
            high, low = halves(turned)
            sink_hi[part * 128 : part * 128 + 128, spin * 128 : spin * 128 + 128] = high
            sink_lo[part * 128 : part * 128 + 128, spin * 128 : spin * 128 + 128] = low


def prepare(weight, source, sink):
    src = jax.ShapeDtypeStruct((4, 256, 1024), BF16)
    snk = jax.ShapeDtypeStruct((256, 512), BF16)
    return pl.pallas_call(
        prepare_kernel,
        out_shape=(src, src, snk, snk),
        in_specs=[SMEM, VMEM, VMEM],
        out_specs=(VMEM,) * 4,
        compiler_params=params(24),
        cost_estimate=pl.CostEstimate(flops=10**8, bytes_accessed=8 * 10**6, transcendentals=0),
        name="prepare",
    )(weight, source, sink)


def left_kernel(elem, sink_hi, sink_lo, left_hi, left_lo):
    for pair in range(3):
        rows_all = []
        for x_pos in range(4):
            tiles = [elem[p, i * 4 + x_pos, pair] for i in range(4) for p in range(4)]
            turned = jnp.concatenate(tiles, axis=0).T
            swapped = jnp.concatenate(
                [-turned[32:64], turned[0:32], -turned[96:128], turned[64:96]], axis=0
            )
            rows_all.append(jnp.concatenate([turned, swapped], axis=1))
        value = dot_three(
            halves(jnp.concatenate(rows_all, axis=0)), (sink_hi[...], sink_lo[...]), ((1,), (0,))
        )
        high, low = halves(value)
        for x_pos in range(4):
            for mom in range(2):
                for part in range(2):
                    start = x_pos * 128 + mom * 64 + part * 32
                    for spin in range(NSPIN):
                        place = part * 512 + spin * 128 + x_pos * 32
                        lanes = slice((mom * 3 + pair) * 128, (mom * 3 + pair) * 128 + 128)
                        cols = slice(spin * 128, spin * 128 + 128)
                        left_hi[place : place + 32, lanes] = high[start : start + 32, cols]
                        left_lo[place : place + 32, lanes] = low[start : start + 32, cols]


def left_product(elem, sink_hi, sink_lo):
    shape = jax.ShapeDtypeStruct((1024, 768), BF16)
    return pl.pallas_call(
        left_kernel,
        out_shape=(shape, shape),
        in_specs=[VMEM] * 3,
        out_specs=(VMEM,) * 2,
        compiler_params=params(24),
        cost_estimate=pl.CostEstimate(flops=10**9, bytes_accessed=4 * 10**6, transcendentals=0),
        name="left",
    )(elem, sink_hi, sink_lo)


def right_kernel(block, src_hi, src_lo, left_hi, left_lo, out_re, out_im):
    value = dot_three(
        (src_hi[0], src_lo[0]), (left_hi[...], left_lo[...]), ((1,), (0,))
    )
    out_re[...] = value[0:128]
    out_im[...] = value[128:256]


def right_product(block, src_hi, src_lo, left_hi, left_lo):
    shape = jax.ShapeDtypeStruct((128, 768), F32)
    spec = pl.BlockSpec((1, 256, 1024), lambda i, ref: (ref[0], 0, 0))
    whole = pl.BlockSpec((1024, 768), lambda i, ref: (0, 0))
    result = pl.BlockSpec((128, 768), lambda i, ref: (0, 0))
    return pl.pallas_call(
        right_kernel,
        out_shape=(shape, shape),
        grid_spec=pltpu.PrefetchScalarGridSpec(
            num_scalar_prefetch=1,
            grid=(1,),
            in_specs=[spec, spec, whole, whole],
            out_specs=(result, result),
        ),
        compiler_params=params(24),
        cost_estimate=pl.CostEstimate(flops=10**9, bytes_accessed=5 * 10**6, transcendentals=0),
        name="right",
    )(block, src_hi, src_lo, left_hi, left_lo)


def final_kernel(*refs):
    out = refs[6]
    for part in range(2):
        value = refs[part][...] + (refs[2 + part][...] + refs[4 + part][...])
        for pair in range(6):
            out[:, pair, part, :] = value[:, pair * 128 : pair * 128 + 128]


def final_sum(*terms):
    return pl.pallas_call(
        final_kernel,
        out_shape=jax.ShapeDtypeStruct((128, 6, 2, 128), F32),
        in_specs=[VMEM] * 6,
        out_specs=VMEM,
        compiler_params=params(16),
        name="final",
    )(*terms)


def ring(count, step):
    return [(i, (i + step) % count) for i in range(count)]


def along_x(step):
    return [(i * 4 + j, i * 4 + (j + step) % 4) for i in range(4) for j in range(4)]


def along_z(step):
    return [(i * 4 + j, ((i + step) % 4) * 4 + j) for i in range(4) for j in range(4)]


def phase_planes(momenta, z_coord):
    site = lax.broadcasted_iota(jnp.int32, (L * L,), 0)
    product = (
        momenta[None, :, 0, None] * (site % L)[None, None, :]
        + momenta[None, :, 1, None] * (site // L)[None, None, :]
        + momenta[None, :, 2, None] * z_coord[:, None, None]
    )
    angles = 2.0 * math.pi / L * jnp.mod(product, L).astype(F32)
    return jnp.stack([jnp.cos(angles), jnp.sin(angles)], axis=2).reshape(-1, 4, L * L)


def step_phases(momenta, directions):
    steps = jnp.stack([momenta[:, directions[e]] for e in range(3)], axis=0)
    angles = 2.0 * math.pi / L * jnp.mod(steps, L).astype(F32)
    cos, sin = jnp.cos(angles), jnp.sin(angles)
    cos = jnp.broadcast_to(cos[:, :, None, None], (3, 2, 2, 32))
    signs = jnp.array([-1.0, 1.0], F32)[None, None, :, None]
    sin = jnp.broadcast_to(sin[:, :, None, None] * signs, (3, 2, 2, 32))
    return jnp.stack([cos.reshape(3, 128), sin.reshape(3, 128)])


def on_device(eigvecs, links, momenta, directions, ins_time, sink_time, sink_peramb, source_peramb):
    depth = eigvecs.shape[4]
    space, tins, tsink = (lax.axis_index(name) for name in ("space", "tins", "tsink"))

    own = jnp.transpose(eigvecs[0].reshape(6, 8, depth, 256), (2, 0, 1, 3))
    planes = jnp.transpose(links[0].reshape(3, 18, depth, 256), (2, 0, 1, 3))
    links_xy = planes[:, :2].reshape(depth, 36, 256)
    top = jnp.concatenate([own[depth - 1].reshape(48, 256), planes[depth - 1, 2]], axis=0)
    top = lax.ppermute(top, "space", ring(4, 1))
    above = lax.ppermute(own[0], "space", ring(4, -1))
    links_z = jnp.concatenate([top[None, 48:], planes[:, 2]], axis=0)
    kets = [own] + [lax.ppermute(own, "tsink", along_z(step)) for step in (1, 2, 3)]
    bra = jnp.concatenate([top[None, :48].reshape(1, 6, 8, 256), own, above[None]], axis=0)
    bras = [bra] + [lax.ppermute(bra, "tsink", along_x(step)) for step in (1, 2, 3)]

    weight = (ins_time < sink_time[0]).astype(F32)
    src_hi, src_lo, sink_hi, sink_lo = prepare(weight, source_peramb[0], sink_peramb[0, 0])

    phase = phase_planes(momenta, space * depth + jnp.arange(depth, dtype=jnp.int32))
    turn = step_phases(momenta, directions)
    place = jnp.concatenate(
        [jnp.stack([space, tsink // 4, tsink % 4]).astype(jnp.int32), directions]
    )
    blocks = elemental_blocks(place, bras, kets, links_xy, links_z, phase, turn)
    summed = blocks[0]
    for other in (2, 3, 1):
        summed = summed + lax.ppermute(blocks[other], "space", [(i, i ^ other) for i in range(4)])
    copies = jnp.broadcast_to(summed[None], (16,) + summed.shape)
    group = lax.all_to_all(copies, "tsink", 0, 0, tiled=True)
    elem = lax.all_gather(group, "space", axis=0, tiled=False)

    left_hi, left_lo = left_product(elem, sink_hi, sink_lo)

    def right(offset):
        block = ((tins + offset) % 4).astype(jnp.int32)[None]
        return right_product(block, src_hi, src_lo, left_hi, left_lo)

    def up(value):
        return lax.ppermute(value, "tins", ring(4, 1))

    def down(value):
        return lax.ppermute(value, "tins", ring(4, -1))

    far_re, far_im = right(2)
    from_below, from_above = up(far_re), down(far_im)
    next_re, next_im = right(1)
    below_im = up(next_im)
    prev_re, prev_im = right(3)
    above_re = down(prev_re)
    own_re, own_im = right(0)
    below_re = up(next_re + from_below)
    above_im = down(prev_im + from_above)
    return final_sum(own_re, own_im, below_re, below_im, above_re, above_im)[:, None]


def solution(mesh):
    in_specs = (
        P("tins", None, None, "tsink", "space", None),
        P("tins", None, None, None, None, "space", None),
        P(),
        P(),
        P("tins"),
        P("tsink"),
        P("tsink", "tins", None, "space", None),
        P("tins", None, None, None),
    )
    out_specs = P("tins", "tsink", None, None, "space")
    return jax.shard_map(
        on_device, mesh=mesh, in_specs=in_specs, out_specs=out_specs, check_vma=False
    )
```

time: 223 us -> 124 us (0.56)
  waiting for transfers between devices: 110 us -> 30.4 us
  blocking collectives: 53.3 us -> 11.3 us
  starting transfers between devices: 4.97 us -> 34.6 us
  matrix products: 25.5 us -> 0 us
  Pallas kernels: 0 us -> 18.1 us
  local copies, waits for them, and re-layouts: 8.92 us -> 17.4 us
  between operations: 15.3 us -> 7.31 us
    all_gather x1 -> x0, waiting for transfers between devices: 65.9 us -> none  [on_device(): lax.all_gather(bra_waves, 'tsink', axis=2, tiled=True)]
    reduce_scatter x1 -> x0, waiting for transfers between devices: 44.2 us -> none  [on_device(): lax.psum_scatter(right_product(left_re, left_im, source_re, source_im), '...]
    all_gather x1, blocking collectives: 42.5 us -> 11.3 us  [on_device(): elem = lax.all_gather(group, 'space', axis=0, tiled=False)]
    ppermute x3 -> x17, waiting for transfers between devices: 0.01 us -> 25.8 us  [the longest x3 11.8 us: on_device(): lax.ppermute(bra, 'tsink', along_x(step))]
    dot_general x10 -> x0, matrix products: 25.5 us -> none  [the longest x4 11 us: contract(): return jnp.einsum('tqrk,tkc->cqr', first_op, second_op, precision=HIGHEST)]
    ppermute x3 -> x17, starting transfers between devices: 4.93 us -> 29.7 us  [the longest x3 11.4 us: on_device(): lax.ppermute(own, 'tsink', along_z(step))]
    pallas_call x0 -> x8, Pallas kernels: none -> 18.1 us  [the longest x4 7.74 us: right_product(): pl.pallas_call(right_kernel, out_shape=(shape, shape), grid_spec=pltpu.Pr...]
    psum x1 -> x0, blocking collectives: 10.8 us -> none  [on_device(): summed = lax.psum(partial_sum, 'space')]
  transfers between devices with their start and end apart: 5 -> 18, of which waited for: 2 -> 8; matrix products, arithmetic and copies ran while one was open for 4% -> 7% of each run, Pallas kernels for 0% -> 5%
where the time goes in v1:
time: 124 us; the launch traced here: 123 us
  starting transfers between devices  34.6 us (28%)
  waiting for transfers between devices  30.4 us (25%)
  Pallas kernels  18.1 us (15%)
  local copies, waits for them, and re-layouts  17.4 us (14%)
  blocking collectives  11.3 us (9%)
  between operations  7.31 us (6%)
  other arithmetic  4.18 us (3%)
    unnamed x29, local copies, waits for them, and re-layouts  12.8 us
    ppermute x3, waiting for transfers between devices, on_device(): lax.ppermute(bra, 'tsink', along_x(step))  11.8 us
    ppermute x3, starting transfers between devices, on_device(): lax.ppermute(own, 'tsink', along_z(step))  11.4 us
    all_gather x1, blocking collectives, on_device(): elem = lax.all_gather(group, 'space', axis=0, tiled=False)  11.3 us
    ppermute x3, starting transfers between devices, down(): return lax.ppermute(value, 'tins', ring(4, -1))  8.1 us
    pallas_call x4, Pallas kernels, right_product(): pl.pallas_call(right_kernel, out_shape=(shape, shape), grid_spec=pltpu.Pr...  7.74 us
    pallas_call x1, Pallas kernels, elemental_blocks(): pl.pallas_call(elemental_kernel, out_shape=jax.ShapeDtypeStruct((4, 3, 8,...  5.59 us
    ppermute x3, waiting for transfers between devices, up(): return lax.ppermute(value, 'tins', ring(4, 1))  5.22 us
  transfers between devices with their start and end apart: 18, of which 8 were waited for; matrix products, arithmetic and copies ran while one was open for 7% of the time, Pallas kernels for 5%

profile of v1, /device:TPU:1, one launch (start us, length us, event | category | flops | bytes accessed | tf_op | source)
XLA Modules:
  0.0 123.3 jit_solution(10973119647253791353)
XLA Ops:
  0.0 1.0 copy.23
  1.0 3.9 %collective-permute-start.5 = (f32[4,6,8,256]{3,2,1,0:T(8,128)S(1)}, f32[4,6,8,256]{3,2,1,0:T(8,128)S(1)}, u32[]{:S(2)}, u32[]{:S(2)}) collective-permute-start(f32[4,6,8,256]{3,2,1,0:T(8,128)S(1)} %bitcast.56), channel_id=1, source_target_pairs={{0,4},{1,5},{2,6},{3,7},{4,8},{5,9},{6,10},{7,11},{8,12},{9,13},{1... | collective-permute-start | bytes 589832 | tf_op jit(solution)/shard_map/ppermute | solution.py:357
  4.9 5.1 %collective-permute-start.6 = (f32[4,6,8,256]{3,2,1,0:T(8,128)S(1)}, f32[4,6,8,256]{3,2,1,0:T(8,128)S(1)}, u32[]{:S(2)}, u32[]{:S(2)}) collective-permute-start(f32[4,6,8,256]{3,2,1,0:T(8,128)S(1)} %bitcast.57), channel_id=1, source_target_pairs={{0,8},{1,9},{2,10},{3,11},{4,12},{5,13},{6,14},{7,15},{8,0},{9,1},... | collective-permute-start | bytes 589832 | tf_op jit(solution)/shard_map/ppermute | solution.py:357
  10.0 2.4 %collective-permute-start.7 = (f32[4,6,8,256]{3,2,1,0:T(8,128)S(1)}, f32[4,6,8,256]{3,2,1,0:T(8,128)S(1)}, u32[]{:S(2)}, u32[]{:S(2)}) collective-permute-start(f32[4,6,8,256]{3,2,1,0:T(8,128)S(1)} %bitcast.58), channel_id=1, source_target_pairs={{0,12},{1,13},{2,14},{3,15},{4,0},{5,1},{6,2},{7,3},{8,4},{9,5},{1... | collective-permute-start | bytes 589832 | tf_op jit(solution)/shard_map/ppermute | solution.py:357
  12.4 1.0 copy.31
  13.4 2.2 %collective-permute-start = (f32[66,256]{1,0:T(8,128)S(1)}, f32[66,256]{1,0:T(8,128)S(1)}, u32[]{:S(2)}, u32[]{:S(2)}) collective-permute-start(f32[66,256]{1,0:T(8,128)S(1)} %pad_maximum_fusion.2), channel_id=1, source_target_pairs={{0,64},{64,128},{128,192},{192,0},{1,65},{65,129},{129,193},{193,1... | collective-permute-start | bytes 202760 | tf_op jit(solution)/shard_map/ppermute | solution.py:354
  15.6 0.0 collective-permute-start.1
  15.6 1.4 %fusion.14 = (s32[1]{0:T(128)}, s32[1]{0:T(128)}, s32[1]{0:T(128)}) fusion(s32[3]{0:T(128)} %param.12), kind=kLoop, calls=%fused_computation.54 | loop fusion | bytes 24 | tf_op jit(solution)/shard_map/slice | solution.py:337
  22.8 1.2 dynamic-slice_reduce_fusion.2
  23.9 0.1 broadcast_multiply_fusion.1
  24.0 0.1 multiply_add_fusion
  24.1 0.2 fusion.7
  24.3 0.1 fusion.13
  24.3 0.1 broadcast_multiply_fusion
  24.4 0.1 broadcast_in_dim.47
  24.5 0.1 stack_reshape.7
  24.6 0.1 broadcast_in_dim.46
  24.6 0.1 stack_reshape.6
  24.7 0.1 copy.25
  24.9 0.1 pad_add_fusion.place
  25.0 4.8 %collective-permute-done.1 = f32[6,8,256]{2,1,0:T(8,128)S(1)} collective-permute-done((f32[6,8,256]{2,1,0:T(8,128)S(1)}, f32[6,8,256]{2,1,0:T(8,128)S(1)}, u32[]{:S(2)}, u32[]{:S(2)}) %collective-permute-start.1) | collective-permute-done | bytes 49184 | tf_op jit(solution)/shard_map/ppermute | solution.py:355
  29.8 1.3 %collective-permute-start.2 = (f32[6,6,8,256]{3,2,1,0:T(8,128)S(1)}, f32[6,6,8,256]{3,2,1,0:T(8,128)S(1)}, u32[]{:S(2)}, u32[]{:S(2)}) collective-permute-start(f32[6,6,8,256]{3,2,1,0:T(8,128)S(1)} %pad_maximum_fusion.refs_0_), channel_id=1, source_target_pairs={{0,1},{1,2},{2,3},{3,0},{4,5},{5,6},{6,7},{7,4},{8,9},{9,10},{10,1... | collective-permute-start | bytes 884744 | tf_op jit(solution)/shard_map/ppermute | solution.py:359
  31.1 2.5 %collective-permute-start.3 = (f32[6,6,8,256]{3,2,1,0:T(8,128)S(1)}, f32[6,6,8,256]{3,2,1,0:T(8,128)S(1)}, u32[]{:S(2)}, u32[]{:S(2)}) collective-permute-start(f32[6,6,8,256]{3,2,1,0:T(8,128)S(1)} %pad_maximum_fusion.refs_0_), channel_id=1, source_target_pairs={{0,2},{1,3},{2,0},{3,1},{4,6},{5,7},{6,4},{7,5},{8,10},{9,11},{10,... | collective-permute-start | bytes 884744 | tf_op jit(solution)/shard_map/ppermute | solution.py:359
  33.5 0.0 collective-permute-done.5.refs_5_
  33.5 1.2 collective-permute-start.4
  34.7 0.0 collective-permute-done.7.refs_7_
  34.7 4.5 %collective-permute-done.2.refs_1_ = f32[6,6,8,256]{3,2,1,0:T(8,128)S(1)} collective-permute-done((f32[6,6,8,256]{3,2,1,0:T(8,128)S(1)}, f32[6,6,8,256]{3,2,1,0:T(8,128)S(1)}, u32[]{:S(2)}, u32[]{:S(2)}) %collective-permute-start.2) | collective-permute-done | bytes 294944 | tf_op jit(solution)/shard_map/ppermute | solution.py:359
  39.2 7.3 %collective-permute-done.3.refs_2_ = f32[6,6,8,256]{3,2,1,0:T(8,128)S(1)} collective-permute-done((f32[6,6,8,256]{3,2,1,0:T(8,128)S(1)}, f32[6,6,8,256]{3,2,1,0:T(8,128)S(1)}, u32[]{:S(2)}, u32[]{:S(2)}) %collective-permute-start.3) | collective-permute-done | bytes 294944 | tf_op jit(solution)/shard_map/ppermute | solution.py:359
  46.5 0.0 collective-permute-done.4.refs_3_
  46.5 5.6 %elementals.1 = f32[4,3,8,128]{3,2,1,0:T(8,128)S(1)} custom-call(s32[6]{0:T(128)S(1)} %pad_add_fusion.place, f32[6,6,8,256]{3,2,1,0:T(8,128)S(1)} %pad_maximum_fusion.refs_0_, f32[6,6,8,256]{3,2,1,0:T(8,128)S(1)} %collective-permute-done.2.refs_1_, f32[6,6,8,256]{3,2,1,0:T(8,128)S(1)} %collective-permute-done.3.refs_2_, ...), custom_call_target="tpu_custom_call" | custom-call | flops 1000000000 | bytes 3000000 | tf_op jit(solution)/shard_map/elementals/pallas_call | solution.py:168
  52.2 1.3 %collective-permute-start.10 = (f32[3,8,128]{2,1,0:T(8,128)S(1)}, f32[3,8,128]{2,1,0:T(8,128)S(1)}, u32[]{:S(2)}, u32[]{:S(2)}) collective-permute-start(f32[3,8,128]{2,1,0:T(8,128)S(1)} %get-tuple-element.42), channel_id=1, source_target_pairs={{0,64},{64,0},{128,192},{192,128},{1,65},{65,1},{129,193},{193,129... | collective-permute-start | bytes 36872 | tf_op jit(solution)/shard_map/ppermute | solution.py:372
  53.5 0.0 collective-permute-start.8
  53.5 1.7 %collective-permute-start.9 = (f32[3,8,128]{2,1,0:T(8,128)S(1)}, f32[3,8,128]{2,1,0:T(8,128)S(1)}, u32[]{:S(2)}, u32[]{:S(2)}) collective-permute-start(f32[3,8,128]{2,1,0:T(8,128)S(1)} %get-tuple-element.43), channel_id=1, source_target_pairs={{0,192},{64,128},{128,64},{192,0},{1,193},{65,129},{129,65},{193,1... | collective-permute-start | bytes 36872 | tf_op jit(solution)/shard_map/ppermute | solution.py:372
  55.2 0.8 collective-permute-done.8
  56.1 0.8 collective-permute-done.9
  56.9 0.7 broadcast_in_dim.48
  57.6 4.9 %all-to-all-start = ((f32[16,3,8,128]{3,2,1,0:T(8,128)}), f32[16,3,8,128]{3,2,1,0:T(8,128)S(1)}, u32[]{:S(2)}, u32[]{:S(2)}) async-start(f32[16,3,8,128]{3,2,1,0:T(8,128)} %broadcast_in_dim.48), calls=%async_computation | async-start | bytes 393216 | tf_op jit(solution)/shard_map/all_to_all | solution.py:374
  63.8 0.0 copy-start.10
  63.8 1.6 %copy-done.10 = f32[1,2,512,512]{3,2,1,0:T(8,128)S(1)} copy-done((f32[1,2,512,512]{3,2,1,0:T(8,128)S(1)}, f32[1,2,512,512]{3,2,1,0:T(8,128)}, u32[]{:S(2)}) %copy-start.10) | copy-done | bytes 2097176
  65.4 0.8 prepare.1
  66.2 1.3 %copy-done = bf16[4,256,1024]{2,1,0:T(8,128)(2,1)} copy-done((bf16[4,256,1024]{2,1,0:T(8,128)(2,1)}, bf16[4,256,1024]{2,1,0:T(8,128)(2,1)S(1)}, u32[]{:S(2)}) %copy-start) | copy-done | bytes 2097176
  67.5 4.7 %all-to-all-done = f32[16,3,8,128]{3,2,1,0:T(8,128)S(1)} async-done(((f32[16,3,8,128]{3,2,1,0:T(8,128)}), f32[16,3,8,128]{3,2,1,0:T(8,128)S(1)}, u32[]{:S(2)}, u32[]{:S(2)}) %all-to-all-start) | async-done | bytes 196640 | tf_op jit(solution)/shard_map/all_to_all | solution.py:374
  72.2 11.3 %all-gather = f32[64,3,8,128]{3,2,1,0:T(8,128)S(1)} all-gather(f32[16,3,8,128]{3,2,1,0:T(8,128)S(1)} %all-to-all-done), channel_id=2, replica_groups=mesh['space'=4,'tins'=4,'tsink'=16] {'space'}, dimensions={0}, use_global_device_ids=true | all-gather | bytes 983040 | tf_op jit(solution)/shard_map/all_gather | solution.py:375
  83.5 1.7 %left.1 = (bf16[1024,768]{1,0:T(8,128)(2,1)S(1)}, bf16[1024,768]{1,0:T(8,128)(2,1)S(1)}) custom-call(f32[4,16,3,8,128]{4,3,2,1,0:T(8,128)S(1)} %bitcast.62, bf16[256,512]{1,0:T(8,128)(2,1)S(1)} %get-tuple-element.21.sink_hi, bf16[256,512]{1,0:T(8,128)(2,1)S(1)} %get-tuple-element.22.sink_lo), custom_call_target="tpu_custom_call" | custom-call | flops 1000000000 | bytes 4000000 | tf_op jit(solution)/shard_map/left/pallas_call | solution.py:255
  85.2 2.1 %right.6 = (f32[128,768]{1,0:T(8,128)}, f32[128,768]{1,0:T(8,128)S(1)}) custom-call(s32[1]{0:T(128)} %bitcast.29.block, bf16[4,256,1024]{2,1,0:T(8,128)(2,1)S(1)} %get-tuple-element.19.src_hi, bf16[4,256,1024]{2,1,0:T(8,128)(2,1)S(1)} %copy-done.1, bf16[1024,768]{1,0:T(8,128)(2,1)S(1)} %get-tuple-element.23.left_hi, ...), custom_call_target="tpu_custom_call" | custom-call | flops 1000000000 | bytes 5000000 | tf_op jit(solution)/shard_map/right/pallas_call | solution.py:279
  87.3 2.7 %collective-permute-start.15 = (f32[128,768]{1,0:T(8,128)S(1)}, f32[128,768]{1,0:T(8,128)}, u32[]{:S(2)}, u32[]{:S(2)}) collective-permute-start(f32[128,768]{1,0:T(8,128)S(1)} %get-tuple-element.32), channel_id=1, source_target_pairs={{0,48},{16,0},{32,16},{48,32},{1,49},{17,1},{33,17},{49,33},{2,50}... | collective-permute-start | bytes 1179656 | tf_op jit(solution)/shard_map/ppermute | solution.py:387
  90.1 0.0 collective-permute-start.11
  90.1 1.6 %copy-done.2 = bf16[4,256,1024]{2,1,0:T(8,128)(2,1)S(1)} copy-done((bf16[4,256,1024]{2,1,0:T(8,128)(2,1)S(1)}, bf16[4,256,1024]{2,1,0:T(8,128)(2,1)}, u32[]{:S(2)}) %copy-start.2) | copy-done | bytes 2097176
  91.7 1.4 %copy-done.5 = bf16[1024,768]{1,0:T(8,128)(2,1)S(1)} copy-done((bf16[1024,768]{1,0:T(8,128)(2,1)S(1)}, bf16[1024,768]{1,0:T(8,128)(2,1)}, u32[]{:S(2)}) %copy-start.5) | copy-done | bytes 1572888
  93.1 1.4 %copy-done.8 = bf16[1024,768]{1,0:T(8,128)(2,1)S(1)} copy-done((bf16[1024,768]{1,0:T(8,128)(2,1)S(1)}, bf16[1024,768]{1,0:T(8,128)(2,1)}, u32[]{:S(2)}) %copy-start.8) | copy-done | bytes 1572888
  94.5 2.1 %right.7 = (f32[128,768]{1,0:T(8,128)}, f32[128,768]{1,0:T(8,128)S(1)}) custom-call(s32[1]{0:T(128)} %bitcast.30.block, bf16[4,256,1024]{2,1,0:T(8,128)(2,1)S(1)} %get-tuple-element.19.src_hi, bf16[4,256,1024]{2,1,0:T(8,128)(2,1)S(1)} %copy-done.2, bf16[1024,768]{1,0:T(8,128)(2,1)S(1)} %copy-done.5, bf16[1024,768]{1,0:T(8,128)(2,1)S(1)} %copy-done.8), custom_call_target="tpu_custom_call" | custom-call | flops 1000000000 | bytes 5000000 | tf_op jit(solution)/shard_map/right/pallas_call | solution.py:279
  96.6 2.7 %collective-permute-start.14 = (f32[128,768]{1,0:T(8,128)}, f32[128,768]{1,0:T(8,128)S(1)}, u32[]{:S(2)}, u32[]{:S(2)}) collective-permute-start(f32[128,768]{1,0:T(8,128)} %get-tuple-element.30), channel_id=1, source_target_pairs={{0,48},{16,0},{32,16},{48,32},{1,49},{17,1},{33,17},{49,33},{2,50}... | collective-permute-start | bytes 1179656 | tf_op jit(solution)/shard_map/ppermute | solution.py:387
  99.3 2.1 %right.5 = (f32[128,768]{1,0:T(8,128)S(1)}, f32[128,768]{1,0:T(8,128)}) custom-call(s32[1]{0:T(128)} %bitcast.28.block, bf16[4,256,1024]{2,1,0:T(8,128)(2,1)S(1)} %get-tuple-element.19.src_hi, bf16[4,256,1024]{2,1,0:T(8,128)(2,1)S(1)} %copy-done.2, bf16[1024,768]{1,0:T(8,128)(2,1)S(1)} %copy-done.5, bf16[1024,768]{1,0:T(8,128)(2,1)S(1)} %copy-done.8), custom_call_target="tpu_custom_call" | custom-call | flops 1000000000 | bytes 5000000 | tf_op jit(solution)/shard_map/right/pallas_call | solution.py:279
  101.4 0.0 collective-permute-start.13
  101.4 1.8 %add.161 = f32[128,768]{1,0:T(8,128)} add(f32[128,768]{1,0:T(8,128)S(1)} %get-tuple-element.31, f32[128,768]{1,0:T(8,128)} %collective-permute-done.15) | non-fusion elementwise | flops 98304 | bytes 1179648 | tf_op jit(solution)/shard_map/add | solution.py:397
  103.2 2.7 %collective-permute-start.16 = (f32[128,768]{1,0:T(8,128)}, f32[128,768]{1,0:T(8,128)S(1)}, u32[]{:S(2)}, u32[]{:S(2)}) collective-permute-start(f32[128,768]{1,0:T(8,128)} %add.161), channel_id=1, source_target_pairs={{0,48},{16,0},{32,16},{48,32},{1,49},{17,1},{33,17},{49,33},{2,50}... | collective-permute-start | bytes 1179656 | tf_op jit(solution)/shard_map/ppermute | solution.py:387
  105.9 1.8 %add.158 = f32[128,768]{1,0:T(8,128)} add(f32[128,768]{1,0:T(8,128)S(1)} %get-tuple-element.27, f32[128,768]{1,0:T(8,128)} %collective-permute-done.11) | non-fusion elementwise | flops 98304 | bytes 1179648 | tf_op jit(solution)/shard_map/add | solution.py:396
  107.7 1.6 %copy-done.3 = bf16[4,256,1024]{2,1,0:T(8,128)(2,1)S(1)} copy-done((bf16[4,256,1024]{2,1,0:T(8,128)(2,1)S(1)}, bf16[4,256,1024]{2,1,0:T(8,128)(2,1)}, u32[]{:S(2)}) %copy-start.3) | copy-done | bytes 2097176
  109.3 1.4 %copy-done.6 = bf16[1024,768]{1,0:T(8,128)(2,1)S(1)} copy-done((bf16[1024,768]{1,0:T(8,128)(2,1)S(1)}, bf16[1024,768]{1,0:T(8,128)(2,1)}, u32[]{:S(2)}) %copy-start.6) | copy-done | bytes 1572888
  110.7 1.4 %copy-done.9 = bf16[1024,768]{1,0:T(8,128)(2,1)S(1)} copy-done((bf16[1024,768]{1,0:T(8,128)(2,1)S(1)}, bf16[1024,768]{1,0:T(8,128)(2,1)}, u32[]{:S(2)}) %copy-start.9) | copy-done | bytes 1572888
  112.1 1.4 %right.4 = (f32[128,768]{1,0:T(8,128)S(1)}, f32[128,768]{1,0:T(8,128)S(1)}) custom-call(s32[1]{0:T(128)} %bitcast.block, bf16[4,256,1024]{2,1,0:T(8,128)(2,1)S(1)} %get-tuple-element.19.src_hi, bf16[4,256,1024]{2,1,0:T(8,128)(2,1)S(1)} %copy-done.3, bf16[1024,768]{1,0:T(8,128)(2,1)S(1)} %copy-done.6, bf16[1024,768]{1,0:T(8,128)(2,1)S(1)} %copy-done.9), custom_call_target="tpu_custom_call" | custom-call | flops 1000000000 | bytes 5000000 | tf_op jit(solution)/shard_map/right/pallas_call | solution.py:279
  113.5 2.2 %collective-permute-done.16.refs_5_ = f32[128,768]{1,0:T(8,128)S(1)} collective-permute-done((f32[128,768]{1,0:T(8,128)}, f32[128,768]{1,0:T(8,128)S(1)}, u32[]{:S(2)}, u32[]{:S(2)}) %collective-permute-start.16) | collective-permute-done | bytes 393248 | tf_op jit(solution)/shard_map/ppermute | solution.py:387
  115.7 5.2 %collective-permute-done.12.refs_2_ = f32[128,768]{1,0:T(8,128)} collective-permute-done((f32[128,768]{1,0:T(8,128)}, f32[128,768]{1,0:T(8,128)}, u32[]{:S(2)}, u32[]{:S(2)}) %collective-permute-start.12) | collective-permute-done | bytes 393248 | tf_op jit(solution)/shard_map/ppermute | solution.py:384
  121.0 2.3 %final.1 = f32[128,6,2,128]{3,2,1,0:T(2,128)} custom-call(f32[128,768]{1,0:T(8,128)S(1)} %get-tuple-element.25.refs_0_, f32[128,768]{1,0:T(8,128)S(1)} %get-tuple-element.26.refs_1_, f32[128,768]{1,0:T(8,128)} %collective-permute-done.12.refs_2_, f32[128,768]{1,0:T(8,128)S(1)} %collective-permute-done.13.refs_3_, ...), custom_call_target="tpu_custom_call" | custom-call | tf_op jit(solution)/shard_map/final/pallas_call | solution.py:303
  (44 shorter events, 0.2 us)
Async XLA Ops:
  0.0 24.3 %copy-start.13 = (f32[2]{0:T(128)S(1)}, f32[2]{0:T(128)}, u32[]{:S(2)}) copy-start(f32[2]{0:T(128)} %constant.107.clone) | copy-start | bytes 28
  0.0 24.9 %copy-start.12 = (s32[3]{0:T(128)S(1)}, s32[3]{0:T(128)}, u32[]{:S(2)}) copy-start(s32[3]{0:T(128)} %param.12) | copy-start | bytes 40
  1.0 32.5 %collective-permute-start.5 = (f32[4,6,8,256]{3,2,1,0:T(8,128)S(1)}, f32[4,6,8,256]{3,2,1,0:T(8,128)S(1)}, u32[]{:S(2)}, u32[]{:S(2)}) collective-permute-start(f32[4,6,8,256]{3,2,1,0:T(8,128)S(1)} %bitcast.56), channel_id=1, source_target_pairs={{0,4},{1,5},{2,6},{3,7},{4,8},{5,9},{6,10},{7,11},{8,12},{9,13},{1... | collective-permute-start | bytes 589832 | tf_op jit(solution)/shard_map/ppermute | solution.py:357
  4.9 29.8 %collective-permute-start.6 = (f32[4,6,8,256]{3,2,1,0:T(8,128)S(1)}, f32[4,6,8,256]{3,2,1,0:T(8,128)S(1)}, u32[]{:S(2)}, u32[]{:S(2)}) collective-permute-start(f32[4,6,8,256]{3,2,1,0:T(8,128)S(1)} %bitcast.57), channel_id=1, source_target_pairs={{0,8},{1,9},{2,10},{3,11},{4,12},{5,13},{6,14},{7,15},{8,0},{9,1},... | collective-permute-start | bytes 589832 | tf_op jit(solution)/shard_map/ppermute | solution.py:357
  10.0 24.7 %collective-permute-start.7 = (f32[4,6,8,256]{3,2,1,0:T(8,128)S(1)}, f32[4,6,8,256]{3,2,1,0:T(8,128)S(1)}, u32[]{:S(2)}, u32[]{:S(2)}) collective-permute-start(f32[4,6,8,256]{3,2,1,0:T(8,128)S(1)} %bitcast.58), channel_id=1, source_target_pairs={{0,12},{1,13},{2,14},{3,15},{4,0},{5,1},{6,2},{7,3},{8,4},{9,5},{1... | collective-permute-start | bytes 589832 | tf_op jit(solution)/shard_map/ppermute | solution.py:357
  13.4 11.5 %collective-permute-start = (f32[66,256]{1,0:T(8,128)S(1)}, f32[66,256]{1,0:T(8,128)S(1)}, u32[]{:S(2)}, u32[]{:S(2)}) collective-permute-start(f32[66,256]{1,0:T(8,128)S(1)} %pad_maximum_fusion.2), channel_id=1, source_target_pairs={{0,64},{64,128},{128,192},{192,0},{1,65},{65,129},{129,193},{193,1... | collective-permute-start | bytes 202760 | tf_op jit(solution)/shard_map/ppermute | solution.py:354
  15.6 14.1 %collective-permute-start.1 = (f32[6,8,256]{2,1,0:T(8,128)S(1)}, f32[6,8,256]{2,1,0:T(8,128)S(1)}, u32[]{:S(2)}, u32[]{:S(2)}) collective-permute-start(f32[6,8,256]{2,1,0:T(8,128)S(1)} %get-tuple-element.40), channel_id=1, source_target_pairs={{0,192},{64,0},{128,64},{192,128},{1,193},{65,1},{129,65},{193,129... | collective-permute-start | bytes 147464 | tf_op jit(solution)/shard_map/ppermute | solution.py:355
  29.8 9.5 %collective-permute-start.2 = (f32[6,6,8,256]{3,2,1,0:T(8,128)S(1)}, f32[6,6,8,256]{3,2,1,0:T(8,128)S(1)}, u32[]{:S(2)}, u32[]{:S(2)}) collective-permute-start(f32[6,6,8,256]{3,2,1,0:T(8,128)S(1)} %pad_maximum_fusion.refs_0_), channel_id=1, source_target_pairs={{0,1},{1,2},{2,3},{3,0},{4,5},{5,6},{6,7},{7,4},{8,9},{9,10},{10,1... | collective-permute-start | bytes 884744 | tf_op jit(solution)/shard_map/ppermute | solution.py:359
  31.1 15.5 %collective-permute-start.3 = (f32[6,6,8,256]{3,2,1,0:T(8,128)S(1)}, f32[6,6,8,256]{3,2,1,0:T(8,128)S(1)}, u32[]{:S(2)}, u32[]{:S(2)}) collective-permute-start(f32[6,6,8,256]{3,2,1,0:T(8,128)S(1)} %pad_maximum_fusion.refs_0_), channel_id=1, source_target_pairs={{0,2},{1,3},{2,0},{3,1},{4,6},{5,7},{6,4},{7,5},{8,10},{9,11},{10,... | collective-permute-start | bytes 884744 | tf_op jit(solution)/shard_map/ppermute | solution.py:359
  33.5 13.0 %collective-permute-start.4 = (f32[6,6,8,256]{3,2,1,0:T(8,128)S(1)}, f32[6,6,8,256]{3,2,1,0:T(8,128)S(1)}, u32[]{:S(2)}, u32[]{:S(2)}) collective-permute-start(f32[6,6,8,256]{3,2,1,0:T(8,128)S(1)} %pad_maximum_fusion.refs_0_), channel_id=1, source_target_pairs={{0,3},{1,0},{2,1},{3,2},{4,7},{5,4},{6,5},{7,6},{8,11},{9,8},{10,9... | collective-permute-start | bytes 884744 | tf_op jit(solution)/shard_map/ppermute | solution.py:359
  34.7 29.1 %copy-start.11 = (f32[1,1,2,128,512]{4,3,2,1,0:T(8,128)S(1)}, f32[1,1,2,128,512]{4,3,2,1,0:T(8,128)}, u32[]{:S(2)}) copy-start(f32[1,1,2,128,512]{4,3,2,1,0:T(8,128)} %param.15) | copy-start | bytes 1572868
  52.2 3.1 %collective-permute-start.10 = (f32[3,8,128]{2,1,0:T(8,128)S(1)}, f32[3,8,128]{2,1,0:T(8,128)S(1)}, u32[]{:S(2)}, u32[]{:S(2)}) collective-permute-start(f32[3,8,128]{2,1,0:T(8,128)S(1)} %get-tuple-element.42), channel_id=1, source_target_pairs={{0,64},{64,0},{128,192},{192,128},{1,65},{65,1},{129,193},{193,129... | collective-permute-start | bytes 36872 | tf_op jit(solution)/shard_map/ppermute | solution.py:372
  53.5 2.6 %collective-permute-start.8 = (f32[3,8,128]{2,1,0:T(8,128)S(1)}, f32[3,8,128]{2,1,0:T(8,128)S(1)}, u32[]{:S(2)}, u32[]{:S(2)}) collective-permute-start(f32[3,8,128]{2,1,0:T(8,128)S(1)} %get-tuple-element.41), channel_id=1, source_target_pairs={{0,128},{64,192},{128,0},{192,64},{1,129},{65,193},{129,1},{193,65... | collective-permute-start | bytes 36872 | tf_op jit(solution)/shard_map/ppermute | solution.py:372
  53.5 3.4 %collective-permute-start.9 = (f32[3,8,128]{2,1,0:T(8,128)S(1)}, f32[3,8,128]{2,1,0:T(8,128)S(1)}, u32[]{:S(2)}, u32[]{:S(2)}) collective-permute-start(f32[3,8,128]{2,1,0:T(8,128)S(1)} %get-tuple-element.43), channel_id=1, source_target_pairs={{0,192},{64,128},{128,64},{192,0},{1,193},{65,129},{129,65},{193,1... | collective-permute-start | bytes 36872 | tf_op jit(solution)/shard_map/ppermute | solution.py:372
  57.6 14.6 %all-to-all-start = ((f32[16,3,8,128]{3,2,1,0:T(8,128)}), f32[16,3,8,128]{3,2,1,0:T(8,128)S(1)}, u32[]{:S(2)}, u32[]{:S(2)}) async-start(f32[16,3,8,128]{3,2,1,0:T(8,128)} %broadcast_in_dim.48), calls=%async_computation | async-start | bytes 393216 | tf_op jit(solution)/shard_map/all_to_all | solution.py:374
  63.8 1.6 %copy-start.10 = (f32[1,2,512,512]{3,2,1,0:T(8,128)S(1)}, f32[1,2,512,512]{3,2,1,0:T(8,128)}, u32[]{:S(2)}) copy-start(f32[1,2,512,512]{3,2,1,0:T(8,128)} %param.16) | copy-start | bytes 6291460
  66.2 1.3 %copy-start = (bf16[4,256,1024]{2,1,0:T(8,128)(2,1)}, bf16[4,256,1024]{2,1,0:T(8,128)(2,1)S(1)}, u32[]{:S(2)}) copy-start(bf16[4,256,1024]{2,1,0:T(8,128)(2,1)S(1)} %get-tuple-element.20.src_lo) | copy-start | bytes 6291460
  83.5 1.7 %copy-start.1 = (bf16[4,256,1024]{2,1,0:T(8,128)(2,1)S(1)}, bf16[4,256,1024]{2,1,0:T(8,128)(2,1)}, u32[]{:S(2)}) copy-start(bf16[4,256,1024]{2,1,0:T(8,128)(2,1)} %copy-done) | copy-start | bytes 6291460
  85.2 2.2 %copy-start.4 = (bf16[1024,768]{1,0:T(8,128)(2,1)}, bf16[1024,768]{1,0:T(8,128)(2,1)S(1)}, u32[]{:S(2)}) copy-start(bf16[1024,768]{1,0:T(8,128)(2,1)S(1)} %get-tuple-element.23.left_hi) | copy-start | bytes 4718596
  85.2 2.1 %copy-start.7 = (bf16[1024,768]{1,0:T(8,128)(2,1)}, bf16[1024,768]{1,0:T(8,128)(2,1)S(1)}, u32[]{:S(2)}) copy-start(bf16[1024,768]{1,0:T(8,128)(2,1)S(1)} %get-tuple-element.24.left_lo) | copy-start | bytes 4718596
  87.3 14.1 %collective-permute-start.15 = (f32[128,768]{1,0:T(8,128)S(1)}, f32[128,768]{1,0:T(8,128)}, u32[]{:S(2)}, u32[]{:S(2)}) collective-permute-start(f32[128,768]{1,0:T(8,128)S(1)} %get-tuple-element.32), channel_id=1, source_target_pairs={{0,48},{16,0},{32,16},{48,32},{1,49},{17,1},{33,17},{49,33},{2,50}... | collective-permute-start | bytes 1179656 | tf_op jit(solution)/shard_map/ppermute | solution.py:387
  90.1 15.8 %collective-permute-start.11 = (f32[128,768]{1,0:T(8,128)}, f32[128,768]{1,0:T(8,128)}, u32[]{:S(2)}, u32[]{:S(2)}) collective-permute-start(f32[128,768]{1,0:T(8,128)} %get-tuple-element.28), channel_id=1, source_target_pairs={{0,16},{16,32},{32,48},{48,0},{1,17},{17,33},{33,49},{49,1},{2,18}... | collective-permute-start | bytes 1179656 | tf_op jit(solution)/shard_map/ppermute | solution.py:384
  90.1 1.6 %copy-start.2 = (bf16[4,256,1024]{2,1,0:T(8,128)(2,1)S(1)}, bf16[4,256,1024]{2,1,0:T(8,128)(2,1)}, u32[]{:S(2)}) copy-start(bf16[4,256,1024]{2,1,0:T(8,128)(2,1)} %copy-done) | copy-start | bytes 6291460
  91.7 1.4 %copy-start.5 = (bf16[1024,768]{1,0:T(8,128)(2,1)S(1)}, bf16[1024,768]{1,0:T(8,128)(2,1)}, u32[]{:S(2)}) copy-start(bf16[1024,768]{1,0:T(8,128)(2,1)} %copy-done.4) | copy-start | bytes 4718596
  93.1 1.4 %copy-start.8 = (bf16[1024,768]{1,0:T(8,128)(2,1)S(1)}, bf16[1024,768]{1,0:T(8,128)(2,1)}, u32[]{:S(2)}) copy-start(bf16[1024,768]{1,0:T(8,128)(2,1)} %copy-done.7) | copy-start | bytes 4718596
  96.6 16.9 %collective-permute-start.14 = (f32[128,768]{1,0:T(8,128)}, f32[128,768]{1,0:T(8,128)S(1)}, u32[]{:S(2)}, u32[]{:S(2)}) collective-permute-start(f32[128,768]{1,0:T(8,128)} %get-tuple-element.30), channel_id=1, source_target_pairs={{0,48},{16,0},{32,16},{48,32},{1,49},{17,1},{33,17},{49,33},{2,50}... | collective-permute-start | bytes 1179656 | tf_op jit(solution)/shard_map/ppermute | solution.py:387
  101.4 12.1 %collective-permute-start.13 = (f32[128,768]{1,0:T(8,128)}, f32[128,768]{1,0:T(8,128)S(1)}, u32[]{:S(2)}, u32[]{:S(2)}) collective-permute-start(f32[128,768]{1,0:T(8,128)} %get-tuple-element.29), channel_id=1, source_target_pairs={{0,16},{16,32},{32,48},{48,0},{1,17},{17,33},{33,49},{49,1},{2,18}... | collective-permute-start | bytes 1179656 | tf_op jit(solution)/shard_map/ppermute | solution.py:384
  103.2 12.6 %collective-permute-start.16 = (f32[128,768]{1,0:T(8,128)}, f32[128,768]{1,0:T(8,128)S(1)}, u32[]{:S(2)}, u32[]{:S(2)}) collective-permute-start(f32[128,768]{1,0:T(8,128)} %add.161), channel_id=1, source_target_pairs={{0,48},{16,0},{32,16},{48,32},{1,49},{17,1},{33,17},{49,33},{2,50}... | collective-permute-start | bytes 1179656 | tf_op jit(solution)/shard_map/ppermute | solution.py:387
  107.7 13.3 %collective-permute-start.12 = (f32[128,768]{1,0:T(8,128)}, f32[128,768]{1,0:T(8,128)}, u32[]{:S(2)}, u32[]{:S(2)}) collective-permute-start(f32[128,768]{1,0:T(8,128)} %add.158), channel_id=1, source_target_pairs={{0,16},{16,32},{32,48},{48,0},{1,17},{17,33},{33,49},{49,1},{2,18}... | collective-permute-start | bytes 1179656 | tf_op jit(solution)/shard_map/ppermute | solution.py:384
  107.7 1.6 %copy-start.3 = (bf16[4,256,1024]{2,1,0:T(8,128)(2,1)S(1)}, bf16[4,256,1024]{2,1,0:T(8,128)(2,1)}, u32[]{:S(2)}) copy-start(bf16[4,256,1024]{2,1,0:T(8,128)(2,1)} %copy-done) | copy-start | bytes 6291460
  109.3 1.4 %copy-start.6 = (bf16[1024,768]{1,0:T(8,128)(2,1)S(1)}, bf16[1024,768]{1,0:T(8,128)(2,1)}, u32[]{:S(2)}) copy-start(bf16[1024,768]{1,0:T(8,128)(2,1)} %copy-done.4) | copy-start | bytes 4718596
  110.7 1.4 %copy-start.9 = (bf16[1024,768]{1,0:T(8,128)(2,1)S(1)}, bf16[1024,768]{1,0:T(8,128)(2,1)}, u32[]{:S(2)}) copy-start(bf16[1024,768]{1,0:T(8,128)(2,1)} %copy-done.7) | copy-start | bytes 4718596

commit v2 on v1

v2 whole, which is shorter than its diff:
```python
import functools
import math

import jax
import jax.numpy as jnp
from jax import lax
from jax.experimental import pallas as pl
from jax.experimental.pallas import tpu as pltpu
from jax.sharding import PartitionSpec as P

L = 16
NSPIN = 4
F32 = jnp.float32
BF16 = jnp.bfloat16
VMEM = pl.BlockSpec(memory_space=pltpu.VMEM)
SMEM = pl.BlockSpec(memory_space=pltpu.SMEM)


def params(mib):
    return pltpu.CompilerParams(vmem_limit_bytes=mib * 2**20)


def halves(value):
    high = value.astype(BF16)
    return high, (value - high.astype(F32)).astype(BF16)


def dot_three(first, second, dims):
    dot = functools.partial(
        lax.dot_general, dimension_numbers=(dims, ((), ())), preferred_element_type=F32
    )
    return dot(first[0], second[0]) + (dot(first[0], second[1]) + dot(first[1], second[0]))


def colour_product(link, vector, adjoint):
    out = []
    for colour in range(3):
        real = imag = None
        for inner in range(3):
            v_re, v_im = vector[inner], vector[3 + inner]
            if adjoint:
                u_re, u_im = link(inner, colour)
                terms = (u_re * v_re + u_im * v_im, u_re * v_im - u_im * v_re)
            else:
                u_re, u_im = link(colour, inner)
                terms = (u_re * v_re - u_im * v_im, u_re * v_im + u_im * v_re)
            real = terms[0] if real is None else real + terms[0]
            imag = terms[1] if imag is None else imag + terms[1]
        out.append((real, imag))
    return [pair[0] for pair in out] + [pair[1] for pair in out]


def shift_x(value, step, column):
    if step == 1:
        return jnp.where(
            column == L - 1, pltpu.roll(value, L - 1, 1), pltpu.roll(value, 127, 1)
        )
    return jnp.where(column == 0, pltpu.roll(value, 128 - L + 1, 1), pltpu.roll(value, 1, 1))


def shift_y(low, high, step, lane):
    if step == 1:
        low, high = pltpu.roll(low, 128 - L, 1), pltpu.roll(high, 128 - L, 1)
        own = lane < 128 - L
    else:
        low, high = pltpu.roll(low, L, 1), pltpu.roll(high, L, 1)
        own = lane >= L
    return jnp.where(own, low, high), jnp.where(own, high, low)


def z_place():
    return lax.shift_right_logical(lax.axis_index("tsink").astype(jnp.int32), 2)


def x_place():
    return lax.axis_index("tsink").astype(jnp.int32) & 3


def block_readers(refs):
    def whole(ref):
        return lambda z, comp, lanes: ref[comp // 3, z, comp % 3, :, lanes]

    def pair(real, imag):
        return lambda z, comp, lanes: (real, imag)[comp // 3][z, comp % 3, :, lanes]

    return [whole(refs[0]), whole(refs[1]), pair(refs[2], refs[3]), whole(refs[4])]


def elemental_kernel(directions, *refs):
    bras, kets = block_readers(refs[0:5]), block_readers(refs[5:10])
    links, low_links, phase, turn, out, waves, phased, total, combined = refs[10:]
    space, z_hi, x_pos = lax.axis_index("space"), z_place(), x_place()
    lane = lax.broadcasted_iota(jnp.int32, (8, 128), 1)
    column = lane % L
    total[...] = jnp.zeros_like(total)

    for z in range(4):
        for block in range(4):
            row = pl.multiple_of(((x_pos + 4 - block) % 4) * 8, 8)
            bra = bras[block]

            def vec(z_at, half):
                lanes = slice(half * 128, half * 128 + 128)
                return [bra(z_at, comp, lanes) for comp in range(6)]

            here = [vec(z + 1, half) for half in range(2)]

            def store(axis, sign, values):
                base = (axis * 2 + sign) * 32
                for half in range(2):
                    for comp in range(6):
                        start = comp * 256 + half * 128
                        waves[pl.ds(base + row, 8), start : start + 128] = values[half][comp]

            for axis in range(3):

                def link(half, shifted):
                    lanes = slice(half * 128, half * 128 + 128)

                    def row(index):
                        if not shifted:
                            return links[axis * 18 + index, z : z + 1, lanes]
                        if z == 0:
                            return low_links[48 + index : 49 + index, lanes]
                        return links[axis * 18 + index, z - 1 : z, lanes]

                    return lambda a, b: (row(a * 3 + b), row(9 + a * 3 + b))

                use = [link(half, False) for half in range(2)]
                below = [link(half, axis == 2) for half in range(2)]
                if axis == 0:
                    above = [[shift_x(v, 1, column) for v in here[h]] for h in range(2)]
                elif axis == 1:
                    pairs = [shift_y(a, b, 1, lane) for a, b in zip(here[0], here[1])]
                    above = [[pair[h] for pair in pairs] for h in range(2)]
                else:
                    above = [vec(z + 2, half) for half in range(2)]
                store(axis, 0, [colour_product(use[h], above[h], False) for h in range(2)])
                source = here if axis < 2 else [vec(z, half) for half in range(2)]
                back = [colour_product(below[h], source[h], True) for h in range(2)]
                if axis == 0:
                    back = [[shift_x(v, -1, column) for v in back[h]] for h in range(2)]
                elif axis == 1:
                    pairs = [shift_y(a, b, -1, lane) for a, b in zip(back[0], back[1])]
                    back = [[pair[h] for pair in pairs] for h in range(2)]
                store(axis, 1, back)

        for block in range(4):
            row = pl.multiple_of(((z_hi + 4 - block) % 4) * 8, 8)
            ket = kets[block]
            for mom in range(2):
                cos = phase[mom * 2, z : z + 1, :]
                sin = phase[mom * 2 + 1, z : z + 1, :]
                for colour in range(3):
                    v_re, v_im = ket(z, colour, slice(0, 256)), ket(z, 3 + colour, slice(0, 256))
                    w_re = cos * v_re + sin * v_im
                    w_im = cos * v_im - sin * v_re
                    first = slice(colour * 256, colour * 256 + 256)
                    second = slice(768 + colour * 256, 1024 + colour * 256)
                    phased[pl.ds(mom * 64 + row, 8), first] = w_re
                    phased[pl.ds(mom * 64 + row, 8), second] = w_im
                    phased[pl.ds(mom * 64 + 32 + row, 8), first] = w_im
                    phased[pl.ds(mom * 64 + 32 + row, 8), second] = -w_re
        total[...] += dot_three(halves(waves[...]), halves(phased[...]), ((1,), (1,)))

    for block in range(6):
        combined[block] = total[block * 32 : block * 32 + 32, :]
    wide = lax.broadcasted_iota(jnp.int32, (32, 128), 1)
    is_real = wide % 64 < 32
    for pair in range(3):
        axis = directions[pair]
        ahead, back = combined[axis * 2], combined[axis * 2 + 1]
        added = ahead + back
        swapped = jnp.where(is_real, pltpu.roll(added, 96, 1), pltpu.roll(added, 32, 1))
        value = turn[0, pair, 0:1] * (back - ahead) + turn[1, pair, 0:1] * swapped
        for group in range(4):
            out[(space % 2) ^ (group % 2), group // 2, pair] = value[group * 8 : group * 8 + 8, :]


def elemental_blocks(directions, bras, kets, links, low_links, phase, turn):
    return pl.pallas_call(
        elemental_kernel,
        out_shape=jax.ShapeDtypeStruct((2, 2, 3, 8, 128), F32),
        in_specs=[SMEM] + [VMEM] * 14,
        out_specs=VMEM,
        scratch_shapes=[
            pltpu.VMEM((192, 1536), F32),
            pltpu.VMEM((128, 1536), F32),
            pltpu.VMEM((192, 128), F32),
            pltpu.VMEM((6, 32, 128), F32),
        ],
        compiler_params=params(24),
        cost_estimate=pl.CostEstimate(flops=10**9, bytes_accessed=3 * 10**6, transcendentals=0),
        name="elementals",
    )(directions, *bras, *kets, links, low_links, phase, turn)


def prepare_kernel(ins_time, sink_time, momenta, directions, source, sink, far_hi, far_lo, near_hi,
                   near_lo, own_hi, own_lo, sink_hi, sink_lo, phase, turn, turned):
    tins = lax.axis_index("tins").astype(jnp.int32)
    weight = jnp.where(ins_time[0] < sink_time[0], 1.0, 0.0)
    site = lax.broadcasted_iota(jnp.int32, (4, L * L), 1)
    z_at = lax.axis_index("space").astype(jnp.int32) * 4 + lax.broadcasted_iota(jnp.int32, (4, L * L), 0)
    for mom in range(2):
        product = momenta[mom, 0] * (site & 15) + momenta[mom, 1] * (site >> 4) + momenta[mom, 2] * z_at
        angles = 2.0 * math.pi / L * (product & 15).astype(F32)
        phase[2 * mom] = jnp.cos(angles)
        phase[2 * mom + 1] = jnp.sin(angles)
    lane = lax.broadcasted_iota(jnp.int32, (8, 128), 1)
    for pair in range(3):
        axis = directions[pair]
        step = jnp.where(lane < 64, momenta[0, axis], momenta[1, axis])
        angles = 2.0 * math.pi / L * (step & 15).astype(F32)
        turn[0, pair] = jnp.cos(angles)
        turn[1, pair] = jnp.where(lane % 64 < 32, -jnp.sin(angles), jnp.sin(angles))
    slots = (
        (2, far_hi, far_lo, 0),
        (1, near_hi, near_lo, 0),
        (3, near_hi, near_lo, 256),
        (0, own_hi, own_lo, 0),
    )
    for part in range(2):
        for spin in range(NSPIN):
            rows = [
                source[part, spin * 128 + i * 32 + j * 8 : spin * 128 + i * 32 + j * 8 + 8, :]
                for j in range(4)
                for i in range(4)
            ]
            turned[...] = jnp.concatenate(rows, axis=0).T
            sign = 1 if part == 0 else -1
            same = slice(part * 512 + spin * 128, part * 512 + spin * 128 + 128)
            other = slice((1 - part) * 512 + spin * 128, (1 - part) * 512 + spin * 128 + 128)
            for offset, to_hi, to_lo, top in slots:
                block = pl.multiple_of(((tins + offset) & 3) * 128, 128)
                high, low = halves(turned[pl.ds(block, 128), :])
                to_hi[top : top + 128, same] = sign * high
                to_lo[top : top + 128, same] = sign * low
                to_hi[top + 128 : top + 256, other] = high
                to_lo[top + 128 : top + 256, other] = low
    for part in range(2):
        for spin in range(NSPIN):
            sign = 1.0 if spin < 2 else -1.0
            value = sink[part, :, spin * 128 : spin * 128 + 128].T * (sign * weight)
            high, low = halves(value)
            sink_hi[part * 128 : part * 128 + 128, spin * 128 : spin * 128 + 128] = high
            sink_lo[part * 128 : part * 128 + 128, spin * 128 : spin * 128 + 128] = low


def prepare(ins_time, sink_time, momenta, directions, source, sink):
    one = jax.ShapeDtypeStruct((256, 1024), BF16)
    two = jax.ShapeDtypeStruct((512, 1024), BF16)
    snk = jax.ShapeDtypeStruct((256, 512), BF16)
    phases = (
        jax.ShapeDtypeStruct((4, 4, 256), F32),
        jax.ShapeDtypeStruct((2, 3, 8, 128), F32),
    )
    return pl.pallas_call(
        prepare_kernel,
        out_shape=(one, one, two, two, one, one, snk, snk) + phases,
        in_specs=[SMEM] * 4 + [VMEM] * 2,
        out_specs=(VMEM,) * 10,
        scratch_shapes=[pltpu.VMEM((512, 128), F32)],
        compiler_params=params(12),
        cost_estimate=pl.CostEstimate(flops=10**8, bytes_accessed=8 * 10**6, transcendentals=0),
        name="prepare",
    )(ins_time, sink_time, momenta, directions, source, sink)


def left_kernel(mine, others, sink_hi, sink_lo, src_hi, src_lo, left_hi, left_lo, out_re, out_im):
    core, z_hi, x_at = lax.axis_index("space") & 1, z_place(), x_place()
    for pair in range(3):
        rows_all = []
        for x_pos in range(4):
            from_x = (x_at - x_pos) & 3
            tiles = []
            for i in range(4):
                from_z = (z_hi - i) & 3
                for group in range(2):
                    own = mine[from_x, from_z, group, pair]
                    other = others[from_x, from_z, group, pair]
                    tiles.append(jnp.where(core == 0, own, other))
                    tiles.append(jnp.where(core == 0, other, own))
            turned = jnp.concatenate(tiles, axis=0).T
            swapped = jnp.concatenate(
                [-turned[32:64], turned[0:32], -turned[96:128], turned[64:96]], axis=0
            )
            rows_all.append(jnp.concatenate([turned, swapped], axis=1))
        value = dot_three(
            halves(jnp.concatenate(rows_all, axis=0)), (sink_hi[...], sink_lo[...]), ((1,), (0,))
        )
        high, low = halves(value)
        for x_pos in range(4):
            for mom in range(2):
                for part in range(2):
                    start = x_pos * 128 + mom * 64 + part * 32
                    for spin in range(NSPIN):
                        at = part * 512 + spin * 128 + x_pos * 32
                        lanes = slice((mom * 3 + pair) * 128, (mom * 3 + pair) * 128 + 128)
                        cols = slice(spin * 128, spin * 128 + 128)
                        left_hi[at : at + 32, lanes] = high[start : start + 32, cols]
                        left_lo[at : at + 32, lanes] = low[start : start + 32, cols]
    right_kernel(src_hi, src_lo, left_hi, left_lo, out_re, out_im)


def left_product(mine, others, sink_hi, sink_lo, src_hi, src_lo):
    shape = jax.ShapeDtypeStruct((1024, 768), BF16)
    result = jax.ShapeDtypeStruct((128, 768), F32)
    return pl.pallas_call(
        left_kernel,
        out_shape=(shape, shape, result, result),
        in_specs=[VMEM] * 6,
        out_specs=(VMEM,) * 4,
        compiler_params=params(16),
        cost_estimate=pl.CostEstimate(flops=10**9, bytes_accessed=4 * 10**6, transcendentals=0),
        name="left",
    )(mine, others, sink_hi, sink_lo, src_hi, src_lo)


def right_kernel(src_hi, src_lo, left_hi, left_lo, *outs):
    for block in range(len(outs) // 2):
        rows = slice(block * 256, block * 256 + 256)
        value = dot_three(
            (src_hi[rows, :], src_lo[rows, :]), (left_hi[...], left_lo[...]), ((1,), (0,))
        )
        outs[2 * block][...] = value[0:128]
        outs[2 * block + 1][...] = value[128:256]


def right_product(src_hi, src_lo, left_hi, left_lo):
    count = 2 * (src_hi.shape[0] // 256)
    return pl.pallas_call(
        right_kernel,
        out_shape=(jax.ShapeDtypeStruct((128, 768), F32),) * count,
        in_specs=[VMEM] * 4,
        out_specs=(VMEM,) * count,
        compiler_params=params(16),
        cost_estimate=pl.CostEstimate(flops=10**9, bytes_accessed=5 * 10**6, transcendentals=0),
        name="right",
    )(src_hi, src_lo, left_hi, left_lo)


def relay_kernel(first, second, third, fourth, out_one, out_two):
    out_one[...] = first[...] + second[...]
    out_two[...] = third[...] + fourth[...]


def relay_sums(*terms):
    shape = jax.ShapeDtypeStruct((128, 768), F32)
    return pl.pallas_call(
        relay_kernel,
        out_shape=(shape, shape),
        in_specs=[VMEM] * 4,
        out_specs=(VMEM,) * 2,
        compiler_params=params(8),
        name="relay",
    )(*terms)


def final_kernel(*refs):
    out = refs[6]
    for part in range(2):
        value = refs[part][...] + (refs[2 + part][...] + refs[4 + part][...])
        for pair in range(6):
            out[:, pair, part, :] = value[:, pair * 128 : pair * 128 + 128]


def final_sum(*terms):
    return pl.pallas_call(
        final_kernel,
        out_shape=jax.ShapeDtypeStruct((128, 6, 2, 128), F32),
        in_specs=[VMEM] * 6,
        out_specs=VMEM,
        compiler_params=params(8),
        name="final",
    )(*terms)


def ring(count, step):
    return [(i, (i + step) % count) for i in range(count)]


def along_x(step):
    return [(i * 4 + j, i * 4 + (j + step) % 4) for i in range(4) for j in range(4)]


def along_z(step):
    return [(i * 4 + j, ((i + step) % 4) * 4 + j) for i in range(4) for j in range(4)]


def gathered(block, along):
    behind = lax.ppermute(block, "tsink", along(1))
    ahead = lax.ppermute(block, "tsink", along(-1))
    real = lax.ppermute(behind[0], "tsink", along(1))
    imag = lax.ppermute(ahead[1], "tsink", along(-1))
    return [block, behind, real, imag, ahead]


def on_device(eigvecs, links, momenta, directions, ins_time, sink_time, sink_peramb, source_peramb):
    depth = eigvecs.shape[4]
    own = lax.optimization_barrier(jnp.transpose(eigvecs[0], (0, 3, 1, 2, 4)))
    links = links[0].reshape(54, depth, 256)
    top = jnp.concatenate([own[:, depth - 1].reshape(48, 256), links[36:, depth - 1]], axis=0)
    top = lax.ppermute(top, "space", ring(4, 1))
    above = lax.ppermute(own[:, 0], "space", ring(4, -1))
    kets = gathered(own, along_z)
    below = top[:48].reshape(2, 1, 3, 8, 256)
    bras = gathered(jnp.concatenate([below, own, above[:, None]], axis=1), along_x)

    sources = prepare(
        ins_time, sink_time, momenta, directions, source_peramb[0], sink_peramb[0, 0]
    )
    far_hi, far_lo, near_hi, near_lo, own_hi, own_lo, sink_hi, sink_lo, phase, turn = sources

    blocks = elemental_blocks(directions, bras, kets, links, top, phase, turn)
    core_pairs = [(i, i ^ 1) for i in range(4)]
    chip_pairs = [(i, i ^ 2) for i in range(4)]
    summed = blocks[0] + lax.ppermute(blocks[1], "space", core_pairs)
    summed = summed + lax.ppermute(summed, "space", chip_pairs)
    for along in (along_z, along_x):
        summed = jnp.stack([summed] + [lax.ppermute(summed, "tsink", along(d)) for d in (1, 2, 3)])
    others = lax.ppermute(summed, "space", core_pairs)

    left_hi, left_lo, far_re, far_im = left_product(
        summed, others, sink_hi, sink_lo, far_hi, far_lo
    )

    def up(value):
        return lax.ppermute(value, "tins", ring(4, 1))

    def down(value):
        return lax.ppermute(value, "tins", ring(4, -1))

    from_below, from_above = up(far_re), down(far_im)
    next_re, next_im, prev_re, prev_im = right_product(near_hi, near_lo, left_hi, left_lo)
    below_im, above_re = up(next_im), down(prev_re)
    own_re, own_im = right_product(own_hi, own_lo, left_hi, left_lo)
    next_re, prev_im = relay_sums(next_re, from_below, prev_im, from_above)
    below_re, above_im = up(next_re), down(prev_im)
    return final_sum(own_re, own_im, below_re, below_im, above_re, above_im)[:, None]


def solution(mesh):
    in_specs = (
        P("tins", None, None, "tsink", "space", None),
        P("tins", None, None, None, None, "space", None),
        P(),
        P(),
        P("tins"),
        P("tsink"),
        P("tsink", "tins", None, "space", None),
        P("tins", None, None, None),
    )
    out_specs = P("tins", "tsink", None, None, "space")
    return jax.shard_map(
        on_device, mesh=mesh, in_specs=in_specs, out_specs=out_specs, check_vma=False
    )
```

time: 124 us -> 100 us (0.81)
  local copies, waits for them, and re-layouts: 17.4 us -> 3.14 us
  starting transfers between devices: 34.6 us -> 48.3 us
  blocking collectives: 11.3 us -> 0 us
  between operations: 7.31 us -> 1.55 us
  other arithmetic: 4.18 us -> 0.08 us
  Pallas kernels: 18.1 us -> 16 us
    ppermute x10 -> x18, starting transfers between devices: 19.4 us -> 36.8 us  [the longest x6 9.34 us: on_device(): lax.ppermute(summed, 'tsink', along(d))]
    all_gather x1 -> x0, blocking collectives: 11.3 us -> none  [on_device(): elem = lax.all_gather(group, 'space', axis=0, tiled=False)]
    ppermute x3, waiting for transfers between devices: 5.22 us -> 16.1 us  [up(): return lax.ppermute(value, 'tins', ring(4, 1))]
    unnamed x29 -> x12, local copies, waits for them, and re-layouts: 12.8 us -> 2.03 us
    all_to_all x1 -> x0, starting transfers between devices: 4.89 us -> none  [on_device(): group = lax.all_to_all(copies, 'tsink', 0, 0, tiled=True)]
    all_to_all x1 -> x0, waiting for transfers between devices: 4.65 us -> none  [on_device(): group = lax.all_to_all(copies, 'tsink', 0, 0, tiled=True)]
    add x5 -> x2, other arithmetic: 3.68 us -> 0.01 us  [the longest x1 0.01 us: on_device(): summed = blocks[0] + lax.ppermute(blocks[1], 'space', core_pairs)]
    ppermute x10 -> x18, waiting for transfers between devices: 18.3 us -> 14.8 us  [the longest x6 6.99 us: on_device(): lax.ppermute(summed, 'tsink', along(d))]
  transfers between devices with their start and end apart: 18 -> 25, of which waited for: 8 -> 13; matrix products, arithmetic and copies ran while one was open for 7% -> 0% of each run, Pallas kernels for 5% -> 6%
where the time goes in v2:
time: 100 us
  starting transfers between devices  48.3 us (48%)
  waiting for transfers between devices  30.9 us (31%)
  Pallas kernels  16 us (16%)
  local copies, waits for them, and re-layouts  3.14 us (3%)
  between operations  1.55 us (2%)
    ppermute x3, waiting for transfers between devices, up(): return lax.ppermute(value, 'tins', ring(4, 1))  16.1 us
    ppermute x6, starting transfers between devices, on_device(): lax.ppermute(summed, 'tsink', along(d))  9.34 us
    ppermute x2, starting transfers between devices, gathered(): ahead = lax.ppermute(block, 'tsink', along(-1))  7.38 us
    ppermute x2, starting transfers between devices, gathered(): imag = lax.ppermute(ahead[1], 'tsink', along(-1))  7.08 us
    ppermute x6, waiting for transfers between devices, on_device(): lax.ppermute(summed, 'tsink', along(d))  6.99 us
    ppermute x3, starting transfers between devices, down(): return lax.ppermute(value, 'tins', ring(4, -1))  5.94 us
    pallas_call x1, Pallas kernels, elemental_blocks(): pl.pallas_call(elemental_kernel, out_shape=jax.ShapeDtypeStruct((2, 2, 3,...  5.33 us
    ppermute x1, starting transfers between devices, on_device(): others = lax.ppermute(summed, 'space', core_pairs)  4.93 us
  transfers between devices with their start and end apart: 25, of which 13 were waited for; matrix products, arithmetic and copies ran while one was open for 0% of the time, Pallas kernels for 6%

profile of v2, /device:TPU:1, one launch (start us, length us, event | category | flops | bytes accessed | tf_op | source)
XLA Modules:
  0.0 100.0 jit_solution(8209447710099119212)
XLA Ops:
  0.0 1.1 %slice.41 = f32[18,1,256]{2,1,0:T(1,128)S(1)} slice(f32[54,4,256]{2,1,0:T(4,128)} %bitcast.53), slice={[36:54], [3:4], [0:256]} | slice | bytes 36864 | tf_op jit(solution)/shard_map/slice | solution.py:402
  1.1 1.0 copy.24
  2.1 3.1 %collective-permute-start = (f32[66,256]{1,0:T(8,128)S(1)}, f32[66,256]{1,0:T(8,128)S(1)}, u32[]{:S(2)}, u32[]{:S(2)}) collective-permute-start(f32[66,256]{1,0:T(8,128)S(1)} %pad_maximum_fusion.3), channel_id=1, source_target_pairs={{0,64},{64,128},{128,192},{192,0},{1,65},{65,129},{129,193},{193,1... | collective-permute-start | bytes 202760 | tf_op jit(solution)/shard_map/ppermute | solution.py:403
  5.2 0.3 collective-permute-start.1
  5.5 4.8 %collective-permute-start.8 = (f32[2,4,3,8,256]{4,3,2,1,0:T(8,128)S(1)}, f32[2,4,3,8,256]{4,3,2,1,0:T(8,128)S(1)}, u32[]{:S(2)}, u32[]{:S(2)}) collective-permute-start(f32[2,4,3,8,256]{4,3,2,1,0:T(8,128)S(1)} %bitcast.48), channel_id=1, source_target_pairs={{0,12},{1,13},{2,14},{3,15},{4,0},{5,1},{6,2},{7,3},{8,4},{9,5},{1... | collective-permute-start | bytes 589832 | tf_op jit(solution)/shard_map/ppermute | solution.py:392
  10.3 0.0 collective-permute-done.refs_11_
  10.3 0.0 collective-permute-done.1
  10.4 2.6 %collective-permute-start.4 = (f32[2,6,3,8,256]{4,3,2,1,0:T(8,128)S(1)}, f32[2,6,3,8,256]{4,3,2,1,0:T(8,128)S(1)}, u32[]{:S(2)}, u32[]{:S(2)}) collective-permute-start(f32[2,6,3,8,256]{4,3,2,1,0:T(8,128)S(1)} %pad_maximum_fusion.1.refs_0_), channel_id=1, source_target_pairs={{0,3},{1,0},{2,1},{3,2},{4,7},{5,4},{6,5},{7,6},{8,11},{9,8},{10,9... | collective-permute-start | bytes 884744 | tf_op jit(solution)/shard_map/ppermute | solution.py:392
  12.9 2.0 %collective-permute-start.6 = (f32[2,4,3,8,256]{4,3,2,1,0:T(8,128)S(1)}, f32[2,4,3,8,256]{4,3,2,1,0:T(8,128)S(1)}, u32[]{:S(2)}, u32[]{:S(2)}) collective-permute-start(f32[2,4,3,8,256]{4,3,2,1,0:T(8,128)S(1)} %bitcast.50), channel_id=1, source_target_pairs={{0,4},{1,5},{2,6},{3,7},{4,8},{5,9},{6,10},{7,11},{8,12},{9,13},{1... | collective-permute-start | bytes 589832 | tf_op jit(solution)/shard_map/ppermute | solution.py:391
  14.9 0.0 collective-permute-start.2
  14.9 1.0 %collective-permute-done.8.refs_9_ = f32[2,4,3,8,256]{4,3,2,1,0:T(8,128)S(1)} collective-permute-done((f32[2,4,3,8,256]{4,3,2,1,0:T(8,128)S(1)}, f32[2,4,3,8,256]{4,3,2,1,0:T(8,128)S(1)}, u32[]{:S(2)}, u32[]{:S(2)}) %collective-permute-start.8) | collective-permute-done | bytes 196640 | tf_op jit(solution)/shard_map/ppermute | solution.py:392
  15.9 4.6 %collective-permute-start.9 = (f32[4,3,8,256]{3,2,1,0:T(8,128)S(1)}, f32[4,3,8,256]{3,2,1,0:T(8,128)S(1)}, u32[]{:S(2)}, u32[]{:S(2)}) collective-permute-start(f32[4,3,8,256]{3,2,1,0:T(8,128)S(1)} %slice_bitcast_fusion.2), channel_id=1, source_target_pairs={{0,12},{1,13},{2,14},{3,15},{4,0},{5,1},{6,2},{7,3},{8,4},{9,5},{1... | collective-permute-start | bytes 294920 | tf_op jit(solution)/shard_map/ppermute | solution.py:394
  20.4 0.0 collective-permute-done.4.refs_4_
  20.5 0.0 copy-start.2
  20.5 2.5 %collective-permute-start.5 = (f32[6,3,8,256]{3,2,1,0:T(8,128)S(1)}, f32[6,3,8,256]{3,2,1,0:T(8,128)S(1)}, u32[]{:S(2)}, u32[]{:S(2)}) collective-permute-start(f32[6,3,8,256]{3,2,1,0:T(8,128)S(1)} %slice_bitcast_fusion), channel_id=1, source_target_pairs={{0,3},{1,0},{2,1},{3,2},{4,7},{5,4},{6,5},{7,6},{8,11},{9,8},{10,9... | collective-permute-start | bytes 442376 | tf_op jit(solution)/shard_map/ppermute | solution.py:394
  23.0 1.9 %collective-permute-done.2.refs_1_ = f32[2,6,3,8,256]{4,3,2,1,0:T(8,128)S(1)} collective-permute-done((f32[2,6,3,8,256]{4,3,2,1,0:T(8,128)S(1)}, f32[2,6,3,8,256]{4,3,2,1,0:T(8,128)S(1)}, u32[]{:S(2)}, u32[]{:S(2)}) %collective-permute-start.2) | collective-permute-done | bytes 294944 | tf_op jit(solution)/shard_map/ppermute | solution.py:391
  24.9 0.1 collective-permute-start.3
  25.0 0.0 collective-permute-done.6.refs_6_
  25.1 3.5 %collective-permute-start.7 = (f32[4,3,8,256]{3,2,1,0:T(8,128)S(1)}, f32[4,3,8,256]{3,2,1,0:T(8,128)S(1)}, u32[]{:S(2)}, u32[]{:S(2)}) collective-permute-start(f32[4,3,8,256]{3,2,1,0:T(8,128)S(1)} %slice_bitcast_fusion.3), channel_id=1, source_target_pairs={{0,4},{1,5},{2,6},{3,7},{4,8},{5,9},{6,10},{7,11},{8,12},{9,13},{1... | collective-permute-start | bytes 294920 | tf_op jit(solution)/shard_map/ppermute | solution.py:393
  29.9 0.0 copy-done.4
  29.9 0.0 copy-start.1
  29.9 1.0 %copy-done.1 = f32[1,1,2,128,512]{4,3,2,1,0:T(8,128)S(1)} copy-done((f32[1,1,2,128,512]{4,3,2,1,0:T(8,128)S(1)}, f32[1,1,2,128,512]{4,3,2,1,0:T(8,128)}, u32[]{:S(2)}) %copy-start.1) | copy-done | bytes 524312
  31.0 1.9 %prepare.1 = (bf16[256,1024]{1,0:T(8,128)(2,1)S(1)}, bf16[256,1024]{1,0:T(8,128)(2,1)S(1)}, bf16[512,1024]{1,0:T(8,128)(2,1)S(1)}, bf16[512,1024]{1,0:T(8,128)(2...) custom-call(s32[1]{0:T(128)S(6)} %copy.26.ins_time, ...), custom_call_target="tpu_custom_call" | custom-call | flops 100000000 | bytes 8000000 | tf_op jit(solution)/shard_map/prepare/pallas_call | solution.py:257
  32.9 0.0 collective-permute-done.9.refs_8_
  32.9 0.0 collective-permute-done.7.refs_7_
  32.9 0.0 collective-permute-done.5.refs_3_
  32.9 0.0 collective-permute-done.3.refs_2_
  32.9 0.0 copy-done.2
  33.0 5.3 %elementals.1 = f32[2,2,3,8,128]{4,3,2,1,0:T(8,128)S(1)} custom-call(s32[3]{0:T(128)S(1)} %copy-done.4, f32[2,6,3,8,256]{4,3,2,1,0:T(8,128)S(1)} %pad_maximum_fusion.1.refs_0_, f32[2,6,3,8,256]{4,3,2,1,0:T(8,128)S(1)} %collective-permute-done.2.refs_1_, f32[6,3,8,256]{3,2,1,0:T(8,128)S(1)} %collective-permute-done.3.refs_2_, ...), custom_call_target="tpu_custom_call" | custom-call | flops 1000000000 | bytes 3000000 | tf_op jit(solution)/shard_map/elementals/pallas_call | solution.py:181
  38.3 2.2 %collective-permute-start.10 = (f32[2,3,8,128]{3,2,1,0:T(8,128)S(1)}, f32[2,3,8,128]{3,2,1,0:T(8,128)S(1)}, u32[]{:S(2)}, u32[]{:S(2)}) collective-permute-start(f32[2,3,8,128]{3,2,1,0:T(8,128)S(1)} %slice_bitcast_fusion.5), channel_id=1, source_target_pairs={{0,64},{64,0},{128,192},{192,128},{1,65},{65,1},{129,193},{193,129... | collective-permute-start | bytes 73736 | tf_op jit(solution)/shard_map/ppermute | solution.py:417
  40.5 0.8 collective-permute-done.10
  41.4 0.0 collective-permute-start.11
  41.4 2.7 %collective-permute-done.11 = f32[2,3,8,128]{3,2,1,0:T(8,128)S(1)} collective-permute-done((f32[2,3,8,128]{3,2,1,0:T(8,128)S(1)}, f32[2,3,8,128]{3,2,1,0:T(8,128)S(1)}, u32[]{:S(2)}, u32[]{:S(2)}) %collective-permute-start.11) | collective-permute-done | bytes 24608 | tf_op jit(solution)/shard_map/ppermute | solution.py:418
  44.1 0.7 collective-permute-start.14
  44.8 3.7 %collective-permute-start.13 = (f32[2,3,8,128]{3,2,1,0:T(8,128)S(1)}, f32[2,3,8,128]{3,2,1,0:T(8,128)S(1)}, u32[]{:S(2)}, u32[]{:S(2)}) collective-permute-start(f32[2,3,8,128]{3,2,1,0:T(8,128)S(1)} %add.7), channel_id=1, source_target_pairs={{0,8},{1,9},{2,10},{3,11},{4,12},{5,13},{6,14},{7,15},{8,0},{9,1},... | collective-permute-start | bytes 73736 | tf_op jit(solution)/shard_map/ppermute | solution.py:420
  48.5 1.2 %collective-permute-start.12 = (f32[2,3,8,128]{3,2,1,0:T(8,128)S(1)}, f32[2,3,8,128]{3,2,1,0:T(8,128)S(1)}, u32[]{:S(2)}, u32[]{:S(2)}) collective-permute-start(f32[2,3,8,128]{3,2,1,0:T(8,128)S(1)} %add.7), channel_id=1, source_target_pairs={{0,4},{1,5},{2,6},{3,7},{4,8},{5,9},{6,10},{7,11},{8,12},{9,13},{1... | collective-permute-start | bytes 73736 | tf_op jit(solution)/shard_map/ppermute | solution.py:420
  49.7 0.0 collective-permute-done.14
  49.7 1.7 %collective-permute-done.13 = f32[2,3,8,128]{3,2,1,0:T(8,128)S(1)} collective-permute-done((f32[2,3,8,128]{3,2,1,0:T(8,128)S(1)}, f32[2,3,8,128]{3,2,1,0:T(8,128)S(1)}, u32[]{:S(2)}, u32[]{:S(2)}) %collective-permute-start.13) | collective-permute-done | bytes 24608 | tf_op jit(solution)/shard_map/ppermute | solution.py:420
  51.4 2.4 %collective-permute-done.12 = f32[2,3,8,128]{3,2,1,0:T(8,128)S(1)} collective-permute-done((f32[2,3,8,128]{3,2,1,0:T(8,128)S(1)}, f32[2,3,8,128]{3,2,1,0:T(8,128)S(1)}, u32[]{:S(2)}, u32[]{:S(2)}) %collective-permute-start.12) | collective-permute-done | bytes 24608 | tf_op jit(solution)/shard_map/ppermute | solution.py:420
  53.7 1.0 %collective-permute-start.16 = (f32[4,2,3,8,128]{4,3,2,1,0:T(8,128)S(1)}, f32[4,2,3,8,128]{4,3,2,1,0:T(8,128)S(1)}, u32[]{:S(2)}, u32[]{:S(2)}) collective-permute-start(f32[4,2,3,8,128]{4,3,2,1,0:T(8,128)S(1)} %get-tuple-element.52), channel_id=1, source_target_pairs={{0,2},{1,3},{2,0},{3,1},{4,6},{5,7},{6,4},{7,5},{8,10},{9,11},{10,... | collective-permute-start | bytes 294920 | tf_op jit(solution)/shard_map/ppermute | solution.py:420
  54.8 2.2 %collective-permute-start.15 = (f32[4,2,3,8,128]{4,3,2,1,0:T(8,128)S(1)}, f32[4,2,3,8,128]{4,3,2,1,0:T(8,128)S(1)}, u32[]{:S(2)}, u32[]{:S(2)}) collective-permute-start(f32[4,2,3,8,128]{4,3,2,1,0:T(8,128)S(1)} %get-tuple-element.52), channel_id=1, source_target_pairs={{0,1},{1,2},{2,3},{3,0},{4,5},{5,6},{6,7},{7,4},{8,9},{9,10},{10,1... | collective-permute-start | bytes 294920 | tf_op jit(solution)/shard_map/ppermute | solution.py:420
  56.9 0.5 collective-permute-start.17
  57.4 1.4 %collective-permute-done.16 = f32[4,2,3,8,128]{4,3,2,1,0:T(8,128)S(1)} collective-permute-done((f32[4,2,3,8,128]{4,3,2,1,0:T(8,128)S(1)}, f32[4,2,3,8,128]{4,3,2,1,0:T(8,128)S(1)}, u32[]{:S(2)}, u32[]{:S(2)}) %collective-permute-start.16) | collective-permute-done | bytes 98336 | tf_op jit(solution)/shard_map/ppermute | solution.py:420
  58.8 1.0 %collective-permute-done.15 = f32[4,2,3,8,128]{4,3,2,1,0:T(8,128)S(1)} collective-permute-done((f32[4,2,3,8,128]{4,3,2,1,0:T(8,128)S(1)}, f32[4,2,3,8,128]{4,3,2,1,0:T(8,128)S(1)}, u32[]{:S(2)}, u32[]{:S(2)}) %collective-permute-start.15) | collective-permute-done | bytes 98336 | tf_op jit(solution)/shard_map/ppermute | solution.py:420
  59.9 0.6 collective-permute-done.17
  60.4 4.9 %collective-permute-start.18 = (f32[4,4,2,3,8,128]{5,4,3,2,1,0:T(8,128)S(1)}, f32[4,4,2,3,8,128]{5,4,3,2,1,0:T(8,128)S(1)}, u32[]{:S(2)}, u32[]{:S(2)}) collective-permute-start(f32[4,4,2,3,8,128]{5,4,3,2,1,0:T(8,128)S(1)} %pad_maximum_fusion.mine), channel_id=1, source_target_pairs={{0,64},{64,0},{128,192},{192,128},{1,65},{65,1},{129,193},{193,129... | collective-permute-start | bytes 1179656 | tf_op jit(solution)/shard_map/ppermute | solution.py:421
  65.4 1.3 %collective-permute-done.18.others = f32[4,4,2,3,8,128]{5,4,3,2,1,0:T(8,128)S(1)} collective-permute-done((f32[4,4,2,3,8,128]{5,4,3,2,1,0:T(8,128)S(1)}, f32[4,4,2,3,8,128]{5,4,3,2,1,0:T(8,128)S(1)}, u32[]{:S(2)}, u32[]{:S(2)}) %collective-permute-start.18) | collective-permute-done | bytes 393248 | tf_op jit(solution)/shard_map/ppermute | solution.py:421
  66.7 3.4 %left.1 = (bf16[1024,768]{1,0:T(8,128)(2,1)S(1)}, bf16[1024,768]{1,0:T(8,128)(2,1)S(1)}, f32[128,768]{1,0:T(8,128)S(1)}, f32[128,768]{1,0:T(8,128)S(1)}) custom-call(f32[4,4,2,3,8,128]{5,4,3,2,1,0:T(8,128)S(1)} %pad_maximum_fusion.mine, f32[4,4,2,3,8,128]{5,4,3,2,1,0:T(8,128)S(1)} %collective-permute-done.18.others, ...), custom_call_target="tpu_custom_call" | custom-call | flops 1000000000 | bytes 4000000 | tf_op jit(solution)/shard_map/left/pallas_call | solution.py:308
  70.1 1.4 %collective-permute-start.19 = (f32[128,768]{1,0:T(8,128)S(1)}, f32[128,768]{1,0:T(8,128)S(1)}, u32[]{:S(2)}, u32[]{:S(2)}) collective-permute-start(f32[128,768]{1,0:T(8,128)S(1)} %get-tuple-element.42), channel_id=1, source_target_pairs={{0,16},{16,32},{32,48},{48,0},{1,17},{17,33},{33,49},{49,1},{2,18}... | collective-permute-start | bytes 1179656 | tf_op jit(solution)/shard_map/ppermute | solution.py:428
  71.5 1.5 %collective-permute-start.20 = (f32[128,768]{1,0:T(8,128)S(1)}, f32[128,768]{1,0:T(8,128)S(1)}, u32[]{:S(2)}, u32[]{:S(2)}) collective-permute-start(f32[128,768]{1,0:T(8,128)S(1)} %get-tuple-element.44), channel_id=1, source_target_pairs={{0,48},{16,0},{32,16},{48,32},{1,49},{17,1},{33,17},{49,33},{2,50}... | collective-permute-start | bytes 1179656 | tf_op jit(solution)/shard_map/ppermute | solution.py:431
  73.0 2.6 %right.3 = (f32[128,768]{1,0:T(8,128)S(1)}, f32[128,768]{1,0:T(8,128)S(1)}, f32[128,768]{1,0:T(8,128)S(1)}, f32[128,768]{1,0:T(8,128)S(1)}) custom-call(bf16[512,1024]{1,0:T(8,128)(2,1)S(1)} %get-tuple-element.39.src_hi, bf16[512,1024]{1,0:T(8,128)(2,1)S(1)} %get-tuple-element.40.src_lo, bf16[1024,768]{1,0:T(8,128)(2,1)S(1)} %get-tuple-element.35.left_hi, ...), custom_call_target="tpu_custom_call" | custom-call | flops 1000000000 | bytes 5000000 | tf_op jit(solution)/shard_map/right/pallas_call | solution.py:331
  75.6 0.1 collective-permute-start.22
  75.7 2.7 %collective-permute-start.23 = (f32[128,768]{1,0:T(8,128)S(1)}, f32[128,768]{1,0:T(8,128)S(1)}, u32[]{:S(2)}, u32[]{:S(2)}) collective-permute-start(f32[128,768]{1,0:T(8,128)S(1)} %get-tuple-element.47), channel_id=1, source_target_pairs={{0,48},{16,0},{32,16},{48,32},{1,49},{17,1},{33,17},{49,33},{2,50}... | collective-permute-start | bytes 1179656 | tf_op jit(solution)/shard_map/ppermute | solution.py:431
  78.3 3.5 %collective-permute-done.19.second = f32[128,768]{1,0:T(8,128)S(1)} collective-permute-done((f32[128,768]{1,0:T(8,128)S(1)}, f32[128,768]{1,0:T(8,128)S(1)}, u32[]{:S(2)}, u32[]{:S(2)}) %collective-permute-start.19) | collective-permute-done | bytes 393248 | tf_op jit(solution)/shard_map/ppermute | solution.py:428
  81.8 0.0 collective-permute-done.20.fourth
  81.8 0.1 relay.1
  81.9 1.0 %collective-permute-start.21 = (f32[128,768]{1,0:T(8,128)S(1)}, f32[128,768]{1,0:T(8,128)S(1)}, u32[]{:S(2)}, u32[]{:S(2)}) collective-permute-start(f32[128,768]{1,0:T(8,128)S(1)} %get-tuple-element.45), channel_id=1, source_target_pairs={{0,16},{16,32},{32,48},{48,0},{1,17},{17,33},{33,49},{49,1},{2,18}... | collective-permute-start | bytes 1179656 | tf_op jit(solution)/shard_map/ppermute | solution.py:428
  82.9 1.8 %collective-permute-start.24 = (f32[128,768]{1,0:T(8,128)S(1)}, f32[128,768]{1,0:T(8,128)S(1)}, u32[]{:S(2)}, u32[]{:S(2)}) collective-permute-start(f32[128,768]{1,0:T(8,128)S(1)} %get-tuple-element.48), channel_id=1, source_target_pairs={{0,48},{16,0},{32,16},{48,32},{1,49},{17,1},{33,17},{49,33},{2,50}... | collective-permute-start | bytes 1179656 | tf_op jit(solution)/shard_map/ppermute | solution.py:431
  84.7 1.4 %right.2 = (f32[128,768]{1,0:T(8,128)S(1)}, f32[128,768]{1,0:T(8,128)S(1)}) custom-call(bf16[256,1024]{1,0:T(8,128)(2,1)S(1)} %get-tuple-element.27.src_hi, bf16[256,1024]{1,0:T(8,128)(2,1)S(1)} %get-tuple-element.28.src_lo, bf16[1024,768]{1,0:T(8,128)(2,1)S(1)} %get-tuple-element.35.left_hi, bf16[1024,768]{1,0:T(8,128)(2,1)S(1)} %get-tuple-element.36.left_lo), custom_call_target="tpu_custom_call" | custom-call | flops 1000000000 | bytes 5000000 | tf_op jit(solution)/shard_map/right/pallas_call | solution.py:331
  86.1 4.2 %collective-permute-done.22.refs_3_ = f32[128,768]{1,0:T(8,128)S(1)} collective-permute-done((f32[128,768]{1,0:T(8,128)S(1)}, f32[128,768]{1,0:T(8,128)S(1)}, u32[]{:S(2)}, u32[]{:S(2)}) %collective-permute-start.22) | collective-permute-done | bytes 393248 | tf_op jit(solution)/shard_map/ppermute | solution.py:428
  90.3 0.0 collective-permute-done.23.refs_4_
  90.3 8.4 %collective-permute-done.21.refs_2_ = f32[128,768]{1,0:T(8,128)S(1)} collective-permute-done((f32[128,768]{1,0:T(8,128)S(1)}, f32[128,768]{1,0:T(8,128)S(1)}, u32[]{:S(2)}, u32[]{:S(2)}) %collective-permute-start.21) | collective-permute-done | bytes 393248 | tf_op jit(solution)/shard_map/ppermute | solution.py:428
  98.7 0.0 collective-permute-done.24.refs_5_
  98.7 1.4 %final.1 = f32[128,6,2,128]{3,2,1,0:T(2,128)} custom-call(f32[128,768]{1,0:T(8,128)S(1)} %get-tuple-element.37.refs_0_, f32[128,768]{1,0:T(8,128)S(1)} %get-tuple-element.38.refs_1_, f32[128,768]{1,0:T(8,128)S(1)} %collective-permute-done.21.refs_2_, f32[128,768]{1,0:T(8,128)S(1)} %collective-permute-done.22.refs_3_, ...), custom_call_target="tpu_custom_call" | custom-call | tf_op jit(solution)/shard_map/final/pallas_call | solution.py:368
  (19 shorter events, 0.1 us)
Async XLA Ops:
  0.0 29.9 %copy-start.4 = (s32[3]{0:T(128)S(1)}, s32[3]{0:T(128)}, u32[]{:S(2)}) copy-start(s32[3]{0:T(128)} %directions.3) | copy-start | bytes 40
  0.0 29.9 %copy-start = (f32[1,2,512,512]{3,2,1,0:T(8,128)S(1)}, f32[1,2,512,512]{3,2,1,0:T(8,128)}, u32[]{:S(2)}) copy-start(f32[1,2,512,512]{3,2,1,0:T(8,128)} %param.15) | copy-start | bytes 6291460
  0.0 29.9 %copy-start.3 = (s32[2,3]{1,0:T(2,128)S(1)}, s32[2,3]{1,0:T(2,128)}, u32[]{:S(2)}) copy-start(s32[2,3]{1,0:T(2,128)} %momenta.1) | copy-start | bytes 76
  2.1 8.2 %collective-permute-start = (f32[66,256]{1,0:T(8,128)S(1)}, f32[66,256]{1,0:T(8,128)S(1)}, u32[]{:S(2)}, u32[]{:S(2)}) collective-permute-start(f32[66,256]{1,0:T(8,128)S(1)} %pad_maximum_fusion.3), channel_id=1, source_target_pairs={{0,64},{64,128},{128,192},{192,0},{1,65},{65,129},{129,193},{193,1... | collective-permute-start | bytes 202760 | tf_op jit(solution)/shard_map/ppermute | solution.py:403
  5.2 5.1 %collective-permute-start.1 = (f32[2,3,8,256]{3,2,1,0:T(8,128)S(1)}, f32[2,3,8,256]{3,2,1,0:T(8,128)S(1)}, u32[]{:S(2)}, u32[]{:S(2)}) collective-permute-start(f32[2,3,8,256]{3,2,1,0:T(8,128)S(1)} %get-tuple-element.50), channel_id=1, source_target_pairs={{0,192},{64,0},{128,64},{192,128},{1,193},{65,1},{129,65},{193,129... | collective-permute-start | bytes 147464 | tf_op jit(solution)/shard_map/ppermute | solution.py:404
  5.5 10.4 %collective-permute-start.8 = (f32[2,4,3,8,256]{4,3,2,1,0:T(8,128)S(1)}, f32[2,4,3,8,256]{4,3,2,1,0:T(8,128)S(1)}, u32[]{:S(2)}, u32[]{:S(2)}) collective-permute-start(f32[2,4,3,8,256]{4,3,2,1,0:T(8,128)S(1)} %bitcast.48), channel_id=1, source_target_pairs={{0,12},{1,13},{2,14},{3,15},{4,0},{5,1},{6,2},{7,3},{8,4},{9,5},{1... | collective-permute-start | bytes 589832 | tf_op jit(solution)/shard_map/ppermute | solution.py:392
  10.4 10.1 %collective-permute-start.4 = (f32[2,6,3,8,256]{4,3,2,1,0:T(8,128)S(1)}, f32[2,6,3,8,256]{4,3,2,1,0:T(8,128)S(1)}, u32[]{:S(2)}, u32[]{:S(2)}) collective-permute-start(f32[2,6,3,8,256]{4,3,2,1,0:T(8,128)S(1)} %pad_maximum_fusion.1.refs_0_), channel_id=1, source_target_pairs={{0,3},{1,0},{2,1},{3,2},{4,7},{5,4},{6,5},{7,6},{8,11},{9,8},{10,9... | collective-permute-start | bytes 884744 | tf_op jit(solution)/shard_map/ppermute | solution.py:392
  12.9 12.1 %collective-permute-start.6 = (f32[2,4,3,8,256]{4,3,2,1,0:T(8,128)S(1)}, f32[2,4,3,8,256]{4,3,2,1,0:T(8,128)S(1)}, u32[]{:S(2)}, u32[]{:S(2)}) collective-permute-start(f32[2,4,3,8,256]{4,3,2,1,0:T(8,128)S(1)} %bitcast.50), channel_id=1, source_target_pairs={{0,4},{1,5},{2,6},{3,7},{4,8},{5,9},{6,10},{7,11},{8,12},{9,13},{1... | collective-permute-start | bytes 589832 | tf_op jit(solution)/shard_map/ppermute | solution.py:391
  14.9 10.0 %collective-permute-start.2 = (f32[2,6,3,8,256]{4,3,2,1,0:T(8,128)S(1)}, f32[2,6,3,8,256]{4,3,2,1,0:T(8,128)S(1)}, u32[]{:S(2)}, u32[]{:S(2)}) collective-permute-start(f32[2,6,3,8,256]{4,3,2,1,0:T(8,128)S(1)} %pad_maximum_fusion.1.refs_0_), channel_id=1, source_target_pairs={{0,1},{1,2},{2,3},{3,0},{4,5},{5,6},{6,7},{7,4},{8,9},{9,10},{10,1... | collective-permute-start | bytes 884744 | tf_op jit(solution)/shard_map/ppermute | solution.py:391
  15.9 17.0 %collective-permute-start.9 = (f32[4,3,8,256]{3,2,1,0:T(8,128)S(1)}, f32[4,3,8,256]{3,2,1,0:T(8,128)S(1)}, u32[]{:S(2)}, u32[]{:S(2)}) collective-permute-start(f32[4,3,8,256]{3,2,1,0:T(8,128)S(1)} %slice_bitcast_fusion.2), channel_id=1, source_target_pairs={{0,12},{1,13},{2,14},{3,15},{4,0},{5,1},{6,2},{7,3},{8,4},{9,5},{1... | collective-permute-start | bytes 294920 | tf_op jit(solution)/shard_map/ppermute | solution.py:394
  20.5 12.5 %copy-start.2 = (f32[1,3,2,3,3,4,256]{6,5,4,3,2,1,0:T(4,128)S(1)}, f32[1,3,2,3,3,4,256]{6,5,4,3,2,1,0:T(4,128)}, u32[]{:S(2)}) copy-start(f32[1,3,2,3,3,4,256]{6,5,4,3,2,1,0:T(4,128)} %param.9) | copy-start | bytes 663556
  20.5 12.5 %collective-permute-start.5 = (f32[6,3,8,256]{3,2,1,0:T(8,128)S(1)}, f32[6,3,8,256]{3,2,1,0:T(8,128)S(1)}, u32[]{:S(2)}, u32[]{:S(2)}) collective-permute-start(f32[6,3,8,256]{3,2,1,0:T(8,128)S(1)} %slice_bitcast_fusion), channel_id=1, source_target_pairs={{0,3},{1,0},{2,1},{3,2},{4,7},{5,4},{6,5},{7,6},{8,11},{9,8},{10,9... | collective-permute-start | bytes 442376 | tf_op jit(solution)/shard_map/ppermute | solution.py:394
  24.9 8.0 %collective-permute-start.3 = (f32[6,3,8,256]{3,2,1,0:T(8,128)S(1)}, f32[6,3,8,256]{3,2,1,0:T(8,128)S(1)}, u32[]{:S(2)}, u32[]{:S(2)}) collective-permute-start(f32[6,3,8,256]{3,2,1,0:T(8,128)S(1)} %slice_bitcast_fusion.1), channel_id=1, source_target_pairs={{0,1},{1,2},{2,3},{3,0},{4,5},{5,6},{6,7},{7,4},{8,9},{9,10},{10,1... | collective-permute-start | bytes 442376 | tf_op jit(solution)/shard_map/ppermute | solution.py:393
  25.1 7.9 %collective-permute-start.7 = (f32[4,3,8,256]{3,2,1,0:T(8,128)S(1)}, f32[4,3,8,256]{3,2,1,0:T(8,128)S(1)}, u32[]{:S(2)}, u32[]{:S(2)}) collective-permute-start(f32[4,3,8,256]{3,2,1,0:T(8,128)S(1)} %slice_bitcast_fusion.3), channel_id=1, source_target_pairs={{0,4},{1,5},{2,6},{3,7},{4,8},{5,9},{6,10},{7,11},{8,12},{9,13},{1... | collective-permute-start | bytes 294920 | tf_op jit(solution)/shard_map/ppermute | solution.py:393
  29.9 1.0 %copy-start.1 = (f32[1,1,2,128,512]{4,3,2,1,0:T(8,128)S(1)}, f32[1,1,2,128,512]{4,3,2,1,0:T(8,128)}, u32[]{:S(2)}) copy-start(f32[1,1,2,128,512]{4,3,2,1,0:T(8,128)} %param.14) | copy-start | bytes 1572868
  38.3 3.1 %collective-permute-start.10 = (f32[2,3,8,128]{3,2,1,0:T(8,128)S(1)}, f32[2,3,8,128]{3,2,1,0:T(8,128)S(1)}, u32[]{:S(2)}, u32[]{:S(2)}) collective-permute-start(f32[2,3,8,128]{3,2,1,0:T(8,128)S(1)} %slice_bitcast_fusion.5), channel_id=1, source_target_pairs={{0,64},{64,0},{128,192},{192,128},{1,65},{65,1},{129,193},{193,129... | collective-permute-start | bytes 73736 | tf_op jit(solution)/shard_map/ppermute | solution.py:417
  41.4 2.7 %collective-permute-start.11 = (f32[2,3,8,128]{3,2,1,0:T(8,128)S(1)}, f32[2,3,8,128]{3,2,1,0:T(8,128)S(1)}, u32[]{:S(2)}, u32[]{:S(2)}) collective-permute-start(f32[2,3,8,128]{3,2,1,0:T(8,128)S(1)} %fusion), channel_id=1, source_target_pairs={{0,128},{64,192},{128,0},{192,64},{1,129},{65,193},{129,1},{193,65... | collective-permute-start | bytes 73736 | tf_op jit(solution)/shard_map/ppermute | solution.py:418
  44.1 5.7 %collective-permute-start.14 = (f32[2,3,8,128]{3,2,1,0:T(8,128)S(1)}, f32[2,3,8,128]{3,2,1,0:T(8,128)S(1)}, u32[]{:S(2)}, u32[]{:S(2)}) collective-permute-start(f32[2,3,8,128]{3,2,1,0:T(8,128)S(1)} %add.7), channel_id=1, source_target_pairs={{0,12},{1,13},{2,14},{3,15},{4,0},{5,1},{6,2},{7,3},{8,4},{9,5},{1... | collective-permute-start | bytes 73736 | tf_op jit(solution)/shard_map/ppermute | solution.py:420
  44.8 6.6 %collective-permute-start.13 = (f32[2,3,8,128]{3,2,1,0:T(8,128)S(1)}, f32[2,3,8,128]{3,2,1,0:T(8,128)S(1)}, u32[]{:S(2)}, u32[]{:S(2)}) collective-permute-start(f32[2,3,8,128]{3,2,1,0:T(8,128)S(1)} %add.7), channel_id=1, source_target_pairs={{0,8},{1,9},{2,10},{3,11},{4,12},{5,13},{6,14},{7,15},{8,0},{9,1},... | collective-permute-start | bytes 73736 | tf_op jit(solution)/shard_map/ppermute | solution.py:420
  48.5 5.2 %collective-permute-start.12 = (f32[2,3,8,128]{3,2,1,0:T(8,128)S(1)}, f32[2,3,8,128]{3,2,1,0:T(8,128)S(1)}, u32[]{:S(2)}, u32[]{:S(2)}) collective-permute-start(f32[2,3,8,128]{3,2,1,0:T(8,128)S(1)} %add.7), channel_id=1, source_target_pairs={{0,4},{1,5},{2,6},{3,7},{4,8},{5,9},{6,10},{7,11},{8,12},{9,13},{1... | collective-permute-start | bytes 73736 | tf_op jit(solution)/shard_map/ppermute | solution.py:420
  53.7 5.1 %collective-permute-start.16 = (f32[4,2,3,8,128]{4,3,2,1,0:T(8,128)S(1)}, f32[4,2,3,8,128]{4,3,2,1,0:T(8,128)S(1)}, u32[]{:S(2)}, u32[]{:S(2)}) collective-permute-start(f32[4,2,3,8,128]{4,3,2,1,0:T(8,128)S(1)} %get-tuple-element.52), channel_id=1, source_target_pairs={{0,2},{1,3},{2,0},{3,1},{4,6},{5,7},{6,4},{7,5},{8,10},{9,11},{10,... | collective-permute-start | bytes 294920 | tf_op jit(solution)/shard_map/ppermute | solution.py:420
  54.8 5.1 %collective-permute-start.15 = (f32[4,2,3,8,128]{4,3,2,1,0:T(8,128)S(1)}, f32[4,2,3,8,128]{4,3,2,1,0:T(8,128)S(1)}, u32[]{:S(2)}, u32[]{:S(2)}) collective-permute-start(f32[4,2,3,8,128]{4,3,2,1,0:T(8,128)S(1)} %get-tuple-element.52), channel_id=1, source_target_pairs={{0,1},{1,2},{2,3},{3,0},{4,5},{5,6},{6,7},{7,4},{8,9},{9,10},{10,1... | collective-permute-start | bytes 294920 | tf_op jit(solution)/shard_map/ppermute | solution.py:420
  56.9 3.5 %collective-permute-start.17 = (f32[4,2,3,8,128]{4,3,2,1,0:T(8,128)S(1)}, f32[4,2,3,8,128]{4,3,2,1,0:T(8,128)S(1)}, u32[]{:S(2)}, u32[]{:S(2)}) collective-permute-start(f32[4,2,3,8,128]{4,3,2,1,0:T(8,128)S(1)} %get-tuple-element.52), channel_id=1, source_target_pairs={{0,3},{1,0},{2,1},{3,2},{4,7},{5,4},{6,5},{7,6},{8,11},{9,8},{10,9... | collective-permute-start | bytes 294920 | tf_op jit(solution)/shard_map/ppermute | solution.py:420
  60.4 6.3 %collective-permute-start.18 = (f32[4,4,2,3,8,128]{5,4,3,2,1,0:T(8,128)S(1)}, f32[4,4,2,3,8,128]{5,4,3,2,1,0:T(8,128)S(1)}, u32[]{:S(2)}, u32[]{:S(2)}) collective-permute-start(f32[4,4,2,3,8,128]{5,4,3,2,1,0:T(8,128)S(1)} %pad_maximum_fusion.mine), channel_id=1, source_target_pairs={{0,64},{64,0},{128,192},{192,128},{1,65},{65,1},{129,193},{193,129... | collective-permute-start | bytes 1179656 | tf_op jit(solution)/shard_map/ppermute | solution.py:421
  70.1 11.7 %collective-permute-start.19 = (f32[128,768]{1,0:T(8,128)S(1)}, f32[128,768]{1,0:T(8,128)S(1)}, u32[]{:S(2)}, u32[]{:S(2)}) collective-permute-start(f32[128,768]{1,0:T(8,128)S(1)} %get-tuple-element.42), channel_id=1, source_target_pairs={{0,16},{16,32},{32,48},{48,0},{1,17},{17,33},{33,49},{49,1},{2,18}... | collective-permute-start | bytes 1179656 | tf_op jit(solution)/shard_map/ppermute | solution.py:428
  71.5 10.4 %collective-permute-start.20 = (f32[128,768]{1,0:T(8,128)S(1)}, f32[128,768]{1,0:T(8,128)S(1)}, u32[]{:S(2)}, u32[]{:S(2)}) collective-permute-start(f32[128,768]{1,0:T(8,128)S(1)} %get-tuple-element.44), channel_id=1, source_target_pairs={{0,48},{16,0},{32,16},{48,32},{1,49},{17,1},{33,17},{49,33},{2,50}... | collective-permute-start | bytes 1179656 | tf_op jit(solution)/shard_map/ppermute | solution.py:431
  75.6 14.7 %collective-permute-start.22 = (f32[128,768]{1,0:T(8,128)S(1)}, f32[128,768]{1,0:T(8,128)S(1)}, u32[]{:S(2)}, u32[]{:S(2)}) collective-permute-start(f32[128,768]{1,0:T(8,128)S(1)} %get-tuple-element.46), channel_id=1, source_target_pairs={{0,16},{16,32},{32,48},{48,0},{1,17},{17,33},{33,49},{49,1},{2,18}... | collective-permute-start | bytes 1179656 | tf_op jit(solution)/shard_map/ppermute | solution.py:428
  75.7 14.6 %collective-permute-start.23 = (f32[128,768]{1,0:T(8,128)S(1)}, f32[128,768]{1,0:T(8,128)S(1)}, u32[]{:S(2)}, u32[]{:S(2)}) collective-permute-start(f32[128,768]{1,0:T(8,128)S(1)} %get-tuple-element.47), channel_id=1, source_target_pairs={{0,48},{16,0},{32,16},{48,32},{1,49},{17,1},{33,17},{49,33},{2,50}... | collective-permute-start | bytes 1179656 | tf_op jit(solution)/shard_map/ppermute | solution.py:431
  81.9 16.8 %collective-permute-start.21 = (f32[128,768]{1,0:T(8,128)S(1)}, f32[128,768]{1,0:T(8,128)S(1)}, u32[]{:S(2)}, u32[]{:S(2)}) collective-permute-start(f32[128,768]{1,0:T(8,128)S(1)} %get-tuple-element.45), channel_id=1, source_target_pairs={{0,16},{16,32},{32,48},{48,0},{1,17},{17,33},{33,49},{49,1},{2,18}... | collective-permute-start | bytes 1179656 | tf_op jit(solution)/shard_map/ppermute | solution.py:428
  82.9 15.8 %collective-permute-start.24 = (f32[128,768]{1,0:T(8,128)S(1)}, f32[128,768]{1,0:T(8,128)S(1)}, u32[]{:S(2)}, u32[]{:S(2)}) collective-permute-start(f32[128,768]{1,0:T(8,128)S(1)} %get-tuple-element.48), channel_id=1, source_target_pairs={{0,48},{16,0},{32,16},{48,32},{1,49},{17,1},{33,17},{49,33},{2,50}... | collective-permute-start | bytes 1179656 | tf_op jit(solution)/shard_map/ppermute | solution.py:431

commit v3 on v2

--- a/solution.py
+++ b/solution.py
@@ -83,35 +83,54 @@
     def pair(real, imag):
         return lambda z, comp, lanes: (real, imag)[comp // 3][z, comp % 3, :, lanes]
 
-    return [whole(refs[0]), whole(refs[1]), pair(refs[2], refs[3]), whole(refs[4])]
-
-
-def elemental_kernel(directions, *refs):
-    bras, kets = block_readers(refs[0:5]), block_readers(refs[5:10])
-    links, low_links, phase, turn, out, waves, phased, total, combined = refs[10:]
-    space, z_hi, x_pos = lax.axis_index("space"), z_place(), x_place()
+    readers, at = [], 0
+    while at < len(refs):
+        if len(refs[at].shape) == 5:
+            readers.append(whole(refs[at]))
+            at += 1
+        else:
+            readers.append(pair(refs[at], refs[at + 1]))
+            at += 2
+    return readers
+
+
+def pack_kernel(eig_far, own, eig, sem):
+    copy = pltpu.make_async_copy(eig_far, eig, sem)
+    copy.start()
+    copy.wait()
+    for part in range(2):
+        for colour in range(3):
+            for z in range(4):
+                own[part, z, colour] = eig[part, colour, :, z, :]
+
+
+def packed(eig):
+    return pl.pallas_call(
+        pack_kernel,
+        out_shape=jax.ShapeDtypeStruct((2, 4, 3, 8, 256), F32),
+        in_specs=[pl.BlockSpec(memory_space=pltpu.HBM)],
+        out_specs=VMEM,
+        scratch_shapes=[pltpu.VMEM((2, 3, 8, 4, 256), F32), pltpu.SemaphoreType.DMA],
+        compiler_params=params(8),
+        name="pack",
+    )(eig)
+
+
+def waves_kernel(count, *refs):
+    blocks = block_readers(refs[: len(refs) - 2 - 2 * count])
+    links, low_links = refs[len(refs) - 2 - 2 * count : len(refs) - 2 * count]
+    outs = refs[len(refs) - 2 * count :]
     lane = lax.broadcasted_iota(jnp.int32, (8, 128), 1)
     column = lane % L
-    total[...] = jnp.zeros_like(total)
-
     for z in range(4):
-        for block in range(4):
-            row = pl.multiple_of(((x_pos + 4 - block) % 4) * 8, 8)
-            bra = bras[block]
+        for block, read in enumerate(blocks):
+            high, low = outs[2 * block], outs[2 * block + 1]
 
             def vec(z_at, half):
                 lanes = slice(half * 128, half * 128 + 128)
-                return [bra(z_at, comp, lanes) for comp in range(6)]
+                return [read(z_at, comp, lanes) for comp in range(6)]
 
             here = [vec(z + 1, half) for half in range(2)]
-
-            def store(axis, sign, values):
-                base = (axis * 2 + sign) * 32
-                for half in range(2):
-                    for comp in range(6):
-                        start = comp * 256 + half * 128
-                        waves[pl.ds(base + row, 8), start : start + 128] = values[half][comp]
-
             for axis in range(3):
 
                 def link(half, shifted):
@@ -121,7 +140,7 @@
                         if not shifted:
                             return links[axis * 18 + index, z : z + 1, lanes]
                         if z == 0:
-                            return low_links[48 + index : 49 + index, lanes]
+                            return low_links[index : index + 1, lanes]
                         return links[axis * 18 + index, z - 1 : z, lanes]
 
                     return lambda a, b: (row(a * 3 + b), row(9 + a * 3 + b))
@@ -135,7 +154,7 @@
                     above = [[pair[h] for pair in pairs] for h in range(2)]
                 else:
                     above = [vec(z + 2, half) for half in range(2)]
-                store(axis, 0, [colour_product(use[h], above[h], False) for h in range(2)])
+                ahead = [colour_product(use[h], above[h], False) for h in range(2)]
                 source = here if axis < 2 else [vec(z, half) for half in range(2)]
                 back = [colour_product(below[h], source[h], True) for h in range(2)]
                 if axis == 0:
@@ -143,10 +162,38 @@
                 elif axis == 1:
                     pairs = [shift_y(a, b, -1, lane) for a, b in zip(back[0], back[1])]
                     back = [[pair[h] for pair in pairs] for h in range(2)]
-                store(axis, 1, back)
-
+                for half in range(2):
+                    for comp in range(6):
+                        cols = slice(comp * 256 + half * 128, comp * 256 + half * 128 + 128)
+                        both = jnp.concatenate([ahead[half][comp], back[half][comp]], axis=0)
+                        parts = halves(both)
+                        high[z, axis * 16 : axis * 16 + 16, cols] = parts[0]
+                        low[z, axis * 16 : axis * 16 + 16, cols] = parts[1]
+
+
+def wave_blocks(count, blocks, links, low_links):
+    shape = jax.ShapeDtypeStruct((4, 48, 1536), BF16)
+    return pl.pallas_call(
+        functools.partial(waves_kernel, count),
+        out_shape=(shape,) * (2 * count),
+        in_specs=[VMEM] * (len(blocks) + 2),
+        out_specs=(VMEM,) * (2 * count),
+        compiler_params=params(8),
+        cost_estimate=pl.CostEstimate(
+            flops=count * 10**7, bytes_accessed=count * 2 * 10**6, transcendentals=0
+        ),
+        name="waves",
+    )(*blocks, links, low_links)
+
+
+def elemental_kernel(directions, *refs):
+    kets = block_readers(refs[0:5])
+    waves = refs[5:13]
+    phase, turn, out, phased, total = refs[13:]
+    core, z_hi, x_at = lax.axis_index("space").astype(jnp.int32) & 1, z_place(), x_place()
+    for z in range(4):
         for block in range(4):
-            row = pl.multiple_of(((z_hi + 4 - block) % 4) * 8, 8)
+            row = pl.multiple_of(((z_hi - block) & 3) * 8, 8)
             ket = kets[block]
             for mom in range(2):
                 cos = phase[mom * 2, z : z + 1, :]
@@ -161,44 +208,47 @@
                     phased[pl.ds(mom * 64 + row, 8), second] = w_im
                     phased[pl.ds(mom * 64 + 32 + row, 8), first] = w_im
                     phased[pl.ds(mom * 64 + 32 + row, 8), second] = -w_re
-        total[...] += dot_three(halves(waves[...]), halves(phased[...]), ((1,), (1,)))
-
-    for block in range(6):
-        combined[block] = total[block * 32 : block * 32 + 32, :]
-    wide = lax.broadcasted_iota(jnp.int32, (32, 128), 1)
-    is_real = wide % 64 < 32
+        bras = jnp.concatenate(
+            [waves[2 * block + part][z] for part in range(2) for block in range(4)], axis=0
+        )
+        value = lax.dot_general(
+            bras,
+            jnp.concatenate(halves(phased[...]), axis=0),
+            (((1,), (1,)), ((), ())),
+            preferred_element_type=F32,
+        )
+        value = value[:192] + value[192:]
+        value = value[:, :128] + value[:, 128:]
+        total[...] = value if z == 0 else total[...] + value
+
+    is_real = lax.broadcasted_iota(jnp.int32, (8, 128), 1) % 64 < 32
     for pair in range(3):
         axis = directions[pair]
-        ahead, back = combined[axis * 2], combined[axis * 2 + 1]
-        added = ahead + back
-        swapped = jnp.where(is_real, pltpu.roll(added, 96, 1), pltpu.roll(added, 32, 1))
-        value = turn[0, pair, 0:1] * (back - ahead) + turn[1, pair, 0:1] * swapped
-        for group in range(4):
-            out[(space % 2) ^ (group % 2), group // 2, pair] = value[group * 8 : group * 8 + 8, :]
-
-
-def elemental_blocks(directions, bras, kets, links, low_links, phase, turn):
+        for block in range(4):
+            row = pl.multiple_of(block * 48 + axis * 16, 16)
+            ahead, back = total[pl.ds(row, 8), :], total[pl.ds(row + 8, 8), :]
+            added = ahead + back
+            swapped = jnp.where(is_real, pltpu.roll(added, 96, 1), pltpu.roll(added, 32, 1))
+            group = (x_at - block) & 3
+            out[core ^ (group & 1), lax.shift_right_logical(group, 1), pair] = (
+                turn[0, pair] * (back - ahead) + turn[1, pair] * swapped
+            )
+
+
+def elemental_blocks(directions, kets, waves, phase, turn):
     return pl.pallas_call(
         elemental_kernel,
         out_shape=jax.ShapeDtypeStruct((2, 2, 3, 8, 128), F32),
-        in_specs=[SMEM] + [VMEM] * 14,
+        in_specs=[SMEM] + [VMEM] * 15,
         out_specs=VMEM,
-        scratch_shapes=[
-            pltpu.VMEM((192, 1536), F32),
-            pltpu.VMEM((128, 1536), F32),
-            pltpu.VMEM((192, 128), F32),
-            pltpu.VMEM((6, 32, 128), F32),
-        ],
-        compiler_params=params(24),
+        scratch_shapes=[pltpu.VMEM((128, 1536), F32), pltpu.VMEM((192, 128), F32)],
+        compiler_params=params(16),
         cost_estimate=pl.CostEstimate(flops=10**9, bytes_accessed=3 * 10**6, transcendentals=0),
         name="elementals",
-    )(directions, *bras, *kets, links, low_links, phase, turn)
-
-
-def prepare_kernel(ins_time, sink_time, momenta, directions, source, sink, far_hi, far_lo, near_hi,
-                   near_lo, own_hi, own_lo, sink_hi, sink_lo, phase, turn, turned):
-    tins = lax.axis_index("tins").astype(jnp.int32)
-    weight = jnp.where(ins_time[0] < sink_time[0], 1.0, 0.0)
+    )(directions, *kets, *waves, phase, turn)
+
+
+def phases_kernel(momenta, directions, phase, turn):
     site = lax.broadcasted_iota(jnp.int32, (4, L * L), 1)
     z_at = lax.axis_index("space").astype(jnp.int32) * 4 + lax.broadcasted_iota(jnp.int32, (4, L * L), 0)
     for mom in range(2):
@@ -213,6 +263,26 @@
         angles = 2.0 * math.pi / L * (step & 15).astype(F32)
         turn[0, pair] = jnp.cos(angles)
         turn[1, pair] = jnp.where(lane % 64 < 32, -jnp.sin(angles), jnp.sin(angles))
+
+
+def phases(momenta, directions):
+    return pl.pallas_call(
+        phases_kernel,
+        out_shape=(
+            jax.ShapeDtypeStruct((4, 4, 256), F32),
+            jax.ShapeDtypeStruct((2, 3, 8, 128), F32),
+        ),
+        in_specs=[SMEM] * 2,
+        out_specs=(VMEM,) * 2,
+        compiler_params=params(4),
+        name="phases",
+    )(momenta, directions)
+
+
+def prepare_kernel(ins_time, sink_time, source, sink, far_hi, far_lo, near_hi, near_lo, own_hi, own_lo,
+                   sink_hi, sink_lo, turned):
+    tins = lax.axis_index("tins").astype(jnp.int32)
+    weight = jnp.where(ins_time[0] < sink_time[0], 1.0, 0.0)
     slots = (
         (2, far_hi, far_lo, 0),
         (1, near_hi, near_lo, 0),
@@ -246,24 +316,20 @@
             sink_lo[part * 128 : part * 128 + 128, spin * 128 : spin * 128 + 128] = low
 
 
-def prepare(ins_time, sink_time, momenta, directions, source, sink):
+def prepare(ins_time, sink_time, source, sink):
     one = jax.ShapeDtypeStruct((256, 1024), BF16)
     two = jax.ShapeDtypeStruct((512, 1024), BF16)
     snk = jax.ShapeDtypeStruct((256, 512), BF16)
-    phases = (
-        jax.ShapeDtypeStruct((4, 4, 256), F32),
-        jax.ShapeDtypeStruct((2, 3, 8, 128), F32),
-    )
     return pl.pallas_call(
         prepare_kernel,
-        out_shape=(one, one, two, two, one, one, snk, snk) + phases,
-        in_specs=[SMEM] * 4 + [VMEM] * 2,
-        out_specs=(VMEM,) * 10,
+        out_shape=(one, one, two, two, one, one, snk, snk),
+        in_specs=[SMEM] * 2 + [VMEM] * 2,
+        out_specs=(VMEM,) * 8,
         scratch_shapes=[pltpu.VMEM((512, 128), F32)],
         compiler_params=params(12),
         cost_estimate=pl.CostEstimate(flops=10**8, bytes_accessed=8 * 10**6, transcendentals=0),
         name="prepare",
-    )(ins_time, sink_time, momenta, directions, source, sink)
+    )(ins_time, sink_time, source, sink)
 
 
 def left_kernel(mine, others, sink_hi, sink_lo, src_hi, src_lo, left_hi, left_lo, out_re, out_im):
@@ -387,37 +453,50 @@
     return [(i * 4 + j, ((i + step) % 4) * 4 + j) for i in range(4) for j in range(4)]
 
 
-def gathered(block, along):
-    behind = lax.ppermute(block, "tsink", along(1))
-    ahead = lax.ppermute(block, "tsink", along(-1))
-    real = lax.ppermute(behind[0], "tsink", along(1))
-    imag = lax.ppermute(ahead[1], "tsink", along(-1))
-    return [block, behind, real, imag, ahead]
+def neighbours(block, along):
+    return lax.ppermute(block, "tsink", along(1)), lax.ppermute(block, "tsink", along(-1))
+
+
+def opposite(behind, ahead, along):
+    return lax.ppermute(behind[0], "tsink", along(1)), lax.ppermute(ahead[1], "tsink", along(-1))
 
 
 def on_device(eigvecs, links, momenta, directions, ins_time, sink_time, sink_peramb, source_peramb):
     depth = eigvecs.shape[4]
-    own = lax.optimization_barrier(jnp.transpose(eigvecs[0], (0, 3, 1, 2, 4)))
     links = links[0].reshape(54, depth, 256)
-    top = jnp.concatenate([own[:, depth - 1].reshape(48, 256), links[36:, depth - 1]], axis=0)
-    top = lax.ppermute(top, "space", ring(4, 1))
-    above = lax.ppermute(own[:, 0], "space", ring(4, -1))
-    kets = gathered(own, along_z)
-    below = top[:48].reshape(2, 1, 3, 8, 256)
-    bras = gathered(jnp.concatenate([below, own, above[:, None]], axis=1), along_x)
-
-    sources = prepare(
-        ins_time, sink_time, momenta, directions, source_peramb[0], sink_peramb[0, 0]
+    own = packed(eigvecs[0])
+    below = lax.ppermute(own[:, depth - 1 :], "space", ring(4, 1))
+    above = lax.ppermute(own[:, :1], "space", ring(4, -1))
+    ket_near = neighbours(own, along_z)
+    bra = jnp.concatenate([below, own, above], axis=1)
+    bra_near = neighbours(bra, along_x)
+    top = lax.ppermute(links[36:, depth - 1], "space", ring(4, 1))
+
+    phase, turn = phases(momenta, directions)
+    waves_own = wave_blocks(1, [bra], links, top)
+    ket_near, phase = lax.optimization_barrier((ket_near, phase))
+    bra_near, waves_own = lax.optimization_barrier((bra_near, waves_own))
+    ket_far = opposite(*ket_near, along_z)
+    bra_far = opposite(*bra_near, along_x)
+
+    waves_near = wave_blocks(2, bra_near, links, top)
+    waves_far = wave_blocks(1, bra_far, links, top)
+    waves = (*waves_own, *waves_near[:2], *waves_far, *waves_near[2:])
+    kets = (own, ket_near[0], *ket_far, ket_near[1])
+    blocks = elemental_blocks(directions, kets, waves, phase, turn)
+    core_pairs = [(i, i ^ 1) for i in range(4)]
+    summed = (
+        blocks[0]
+        + lax.ppermute(blocks[1], "space", core_pairs)
+        + lax.ppermute(blocks[0], "space", [(i, i ^ 2) for i in range(4)])
+        + lax.ppermute(blocks[1], "space", [(i, i ^ 3) for i in range(4)])
     )
-    far_hi, far_lo, near_hi, near_lo, own_hi, own_lo, sink_hi, sink_lo, phase, turn = sources
-
-    blocks = elemental_blocks(directions, bras, kets, links, top, phase, turn)
-    core_pairs = [(i, i ^ 1) for i in range(4)]
-    chip_pairs = [(i, i ^ 2) for i in range(4)]
-    summed = blocks[0] + lax.ppermute(blocks[1], "space", core_pairs)
-    summed = summed + lax.ppermute(summed, "space", chip_pairs)
-    for along in (along_z, along_x):
-        summed = jnp.stack([summed] + [lax.ppermute(summed, "tsink", along(d)) for d in (1, 2, 3)])
+    sources = prepare(ins_time, sink_time, source_peramb[0], sink_peramb[0, 0])
+    columns = [lax.ppermute(summed, "tsink", along_z(d)) for d in (1, 2, 3)]
+    columns, sources = lax.optimization_barrier((columns, sources))
+    far_hi, far_lo, near_hi, near_lo, own_hi, own_lo, sink_hi, sink_lo = sources
+    summed = jnp.stack([summed] + list(columns))
+    summed = jnp.stack([summed] + [lax.ppermute(summed, "tsink", along_x(d)) for d in (1, 2, 3)])
     others = lax.ppermute(summed, "space", core_pairs)
 
     left_hi, left_lo, far_re, far_im = left_product(
@@ -432,8 +511,9 @@
 
     from_below, from_above = up(far_re), down(far_im)
     next_re, next_im, prev_re, prev_im = right_product(near_hi, near_lo, left_hi, left_lo)
+    own_re, own_im = right_product(own_hi, own_lo, left_hi, left_lo)
+    next_im, prev_re, own_re, own_im = lax.optimization_barrier((next_im, prev_re, own_re, own_im))
     below_im, above_re = up(next_im), down(prev_re)
-    own_re, own_im = right_product(own_hi, own_lo, left_hi, left_lo)
     next_re, prev_im = relay_sums(next_re, from_below, prev_im, from_above)
     below_re, above_im = up(next_re), down(prev_im)
     return final_sum(own_re, own_im, below_re, below_im, above_re, above_im)[:, None]

time: 100 us -> 96.1 us (0.961)
  starting transfers between devices: 48.3 us -> 45.4 us
  waiting for transfers between devices: 30.9 us -> 28.2 us
  local copies, waits for them, and re-layouts: 3.14 us -> 4.21 us
    pallas_call x0 -> x5, Pallas kernels: none -> 3.84 us  [the longest x3 2.86 us: wave_blocks(): pl.pallas_call(functools.partial(waves_kernel, count), out_shape=(shape,)...]
    ppermute x18 -> x20, waiting for transfers between devices: 13.5 us -> 10.7 us  [the longest x2 3.33 us: opposite(): lax.ppermute(behind[0], 'tsink', along(1))]
    pallas_call x1, Pallas kernels: 5.33 us -> 2.63 us  [elemental_blocks(): pl.pallas_call(elemental_kernel, out_shape=jax.ShapeDtypeStruct((2, 2, 3,...]
    ppermute x18 -> x20, starting transfers between devices: 35 us -> 32.4 us  [the longest x2 7.38 us: neighbours(): lax.ppermute(block, 'tsink', along(-1))]
    unnamed x12 -> x17, local copies, waits for them, and re-layouts: 2.03 us -> 3.25 us
  transfers between devices with their start and end apart: 25 -> 27, of which waited for: 13 -> 12; matrix products, arithmetic and copies ran while one was open for 0% -> 1% of each run, Pallas kernels for 6% -> 9%
where the time goes in v3:
time: 96.1 us; the launch traced here: 95.9 us
  starting transfers between devices  45.4 us (47%)
  waiting for transfers between devices  28.2 us (29%)
  Pallas kernels  16.5 us (17%)
  local copies, waits for them, and re-layouts  4.21 us (4%)
  between operations  1.56 us (2%)
    ppermute x3, waiting for transfers between devices, up(): return lax.ppermute(value, 'tins', ring(4, 1))  16.1 us
    ppermute x2, starting transfers between devices, neighbours(): lax.ppermute(block, 'tsink', along(-1))  7.38 us
    ppermute x2, starting transfers between devices, opposite(): lax.ppermute(ahead[1], 'tsink', along(-1))  5.99 us
    ppermute x3, starting transfers between devices, down(): return lax.ppermute(value, 'tins', ring(4, -1))  5.94 us
    ppermute x1, starting transfers between devices, on_device(): lax.ppermute(blocks[1], 'space', [(i, i ^ 3) for i in range(4)])  4.67 us
    ppermute x1, starting transfers between devices, on_device(): others = lax.ppermute(summed, 'space', core_pairs)  4.57 us
    pallas_call x2, Pallas kernels, right_product(): pl.pallas_call(right_kernel, out_shape=(jax.ShapeDtypeStruct((128, 768),...  3.97 us
    ppermute x3, starting transfers between devices, on_device(): columns = [lax.ppermute(summed, 'tsink', along_z(d)) for d in (1, 2, 3)]  3.92 us
  transfers between devices with their start and end apart: 27, of which 12 were waited for; matrix products, arithmetic and copies ran while one was open for 1% of the time, Pallas kernels for 9%

profile of v3, /device:TPU:1, one launch (start us, length us, event | category | flops | bytes accessed | tf_op | source)
XLA Modules:
  0.0 95.9 jit_solution(8403616454908503721)
XLA Ops:
  0.0 1.0 %copy-done.4 = f32[1,2,3,8,4,256]{5,4,3,2,1,0:T(4,128)S(1)} copy-done((f32[1,2,3,8,4,256]{5,4,3,2,1,0:T(4,128)S(1)}, f32[1,2,3,8,4,256]{5,4,3,2,1,0:T(4,128)}, u32[]{:S(2)}) %copy-start.4) | copy-done | bytes 196632
  1.0 0.3 pack.1.refs_0_
  1.3 3.1 %collective-permute-start.4 = (f32[2,1,3,8,256]{4,3,2,1,0:T(8,128)S(1)}, f32[2,1,3,8,256]{4,3,2,1,0:T(8,128)S(1)}, u32[]{:S(2)}, u32[]{:S(2)}) collective-permute-start(f32[2,1,3,8,256]{4,3,2,1,0:T(8,128)S(1)} %get-tuple-element.109), channel_id=1, source_target_pairs={{0,64},{64,128},{128,192},{192,0},{1,65},{65,129},{129,193},{193,1... | collective-permute-start | bytes 147464 | tf_op jit(solution)/shard_map/ppermute | solution.py:468
  4.4 0.3 collective-permute-start.5
  4.7 4.8 %collective-permute-start.1 = (f32[2,4,3,8,256]{4,3,2,1,0:T(8,128)S(1)}, f32[2,4,3,8,256]{4,3,2,1,0:T(8,128)S(1)}, u32[]{:S(2)}, u32[]{:S(2)}) collective-permute-start(f32[2,4,3,8,256]{4,3,2,1,0:T(8,128)S(1)} %pack.1.refs_0_), channel_id=1, source_target_pairs={{0,12},{1,13},{2,14},{3,15},{4,0},{5,1},{6,2},{7,3},{8,4},{9,5},{1... | collective-permute-start | bytes 589832 | tf_op jit(solution)/shard_map/ppermute | solution.py:457
  9.5 0.0 collective-permute-start
  9.5 0.0 collective-permute-done.4
  9.6 0.0 copy-start.6
  9.6 2.6 %collective-permute-start.7 = (f32[2,6,3,8,256]{4,3,2,1,0:T(8,128)S(1)}, f32[2,6,3,8,256]{4,3,2,1,0:T(8,128)S(1)}, u32[]{:S(2)}, u32[]{:S(2)}) collective-permute-start(f32[2,6,3,8,256]{4,3,2,1,0:T(8,128)S(1)} %pad_maximum_fusion.1.refs_0_), channel_id=1, source_target_pairs={{0,3},{1,0},{2,1},{3,2},{4,7},{5,4},{6,5},{7,6},{8,11},{9,8},{10,9... | collective-permute-start | bytes 884744 | tf_op jit(solution)/shard_map/ppermute | solution.py:457
  12.1 0.0 collective-permute-start.6
  12.1 0.9 slice.40
  13.1 2.4 %collective-permute-start.8 = (f32[18,256]{1,0:T(8,128)S(1)}, f32[18,256]{1,0:T(8,128)S(1)}, u32[]{:S(2)}, u32[]{:S(2)}) collective-permute-start(f32[18,256]{1,0:T(8,128)S(1)} %bitcast.47), channel_id=1, source_target_pairs={{0,64},{64,128},{128,192},{192,0},{1,65},{65,129},{129,193},{193,1... | collective-permute-start | bytes 55304 | tf_op jit(solution)/shard_map/ppermute | solution.py:473
  15.4 0.7 copy-done.5
  16.1 0.7 copy-done.7
  16.8 0.7 phases.1
  17.5 0.0 copy-start
  17.5 0.9 copy-done
  18.4 0.7 waves.3
  19.1 0.0 collective-permute-done.1.refs_4_
  19.1 0.5 collective-permute-done.refs_1_
  19.7 0.5 collective-permute-done.6.refs_0_
  20.2 2.1 %collective-permute-start.10 = (f32[6,3,8,256]{3,2,1,0:T(8,128)S(1)}, f32[6,3,8,256]{3,2,1,0:T(8,128)S(1)}, u32[]{:S(2)}, u32[]{:S(2)}) collective-permute-start(f32[6,3,8,256]{3,2,1,0:T(8,128)S(1)} %slice_bitcast_fusion), channel_id=1, source_target_pairs={{0,3},{1,0},{2,1},{3,2},{4,7},{5,4},{6,5},{7,6},{8,11},{9,8},{10,9... | collective-permute-start | bytes 442376 | tf_op jit(solution)/shard_map/ppermute | solution.py:461
  22.3 0.0 collective-permute-start.9
  22.3 3.9 %collective-permute-start.3 = (f32[4,3,8,256]{3,2,1,0:T(8,128)S(1)}, f32[4,3,8,256]{3,2,1,0:T(8,128)S(1)}, u32[]{:S(2)}, u32[]{:S(2)}) collective-permute-start(f32[4,3,8,256]{3,2,1,0:T(8,128)S(1)} %slice_bitcast_fusion.2), channel_id=1, source_target_pairs={{0,12},{1,13},{2,14},{3,15},{4,0},{5,1},{6,2},{7,3},{8,4},{9,5},{1... | collective-permute-start | bytes 294920 | tf_op jit(solution)/shard_map/ppermute | solution.py:461
  26.2 0.0 collective-permute-start.2
  26.2 1.4 %waves.4 = (bf16[4,48,1536]{2,1,0:T(8,128)(2,1)S(1)}, bf16[4,48,1536]{2,1,0:T(8,128)(2,1)S(1)}, bf16[4,48,1536]{2,1,0:T(8,128)(2,1)S(1)}, bf16[4,48,1536]{2,1,0:T(8,128)(2,1)S(1)}) custom-call(f32[2,6,3,8,256]{4,3,2,1,0:T(8,128)S(1)} %collective-permute-done.6.refs_0_, f32[2,6,3,8,256]{4,3,2,1,0:T(8,128)S(1)} %collective-permute-done.7.refs_1_, ...), custom_call_target="tpu_custom_call" | custom-call | flops 20000000 | bytes 4000000 | tf_op jit(solution)/shard_map/waves/pallas_call | solution.py:176
  27.6 0.0 collective-permute-done.10.refs_1_
  27.6 0.0 collective-permute-done.9.refs_0_
  27.6 0.7 waves.5
  28.4 0.4 collective-permute-done.3.refs_3_
  28.8 3.3 %collective-permute-done.2.refs_2_ = f32[4,3,8,256]{3,2,1,0:T(8,128)S(1)} collective-permute-done((f32[4,3,8,256]{3,2,1,0:T(8,128)S(1)}, f32[4,3,8,256]{3,2,1,0:T(8,128)S(1)}, u32[]{:S(2)}, u32[]{:S(2)}) %collective-permute-start.2) | collective-permute-done | bytes 98336 | tf_op jit(solution)/shard_map/ppermute | solution.py:461
  32.2 2.6 %elementals.1 = f32[2,2,3,8,128]{4,3,2,1,0:T(8,128)S(1)} custom-call(s32[3]{0:T(128)S(1)} %copy-done.6, f32[2,4,3,8,256]{4,3,2,1,0:T(8,128)S(1)} %pack.1.refs_0_, f32[2,4,3,8,256]{4,3,2,1,0:T(8,128)S(1)} %collective-permute-done.refs_1_, f32[4,3,8,256]{3,2,1,0:T(8,128)S(1)} %collective-permute-done.2.refs_2_, ...), custom_call_target="tpu_custom_call" | custom-call | flops 1000000000 | bytes 3000000 | tf_op jit(solution)/shard_map/elementals/pallas_call | solution.py:239
  34.8 1.5 %collective-permute-start.12 = (f32[2,3,8,128]{3,2,1,0:T(8,128)S(1)}, f32[2,3,8,128]{3,2,1,0:T(8,128)S(1)}, u32[]{:S(2)}, u32[]{:S(2)}) collective-permute-start(f32[2,3,8,128]{3,2,1,0:T(8,128)S(1)} %get-tuple-element.113), channel_id=1, source_target_pairs={{0,128},{64,192},{128,0},{192,64},{1,129},{65,193},{129,1},{193,65... | collective-permute-start | bytes 73736 | tf_op jit(solution)/shard_map/ppermute | solution.py:491
  36.3 4.7 %collective-permute-start.13 = (f32[2,3,8,128]{3,2,1,0:T(8,128)S(1)}, f32[2,3,8,128]{3,2,1,0:T(8,128)S(1)}, u32[]{:S(2)}, u32[]{:S(2)}) collective-permute-start(f32[2,3,8,128]{3,2,1,0:T(8,128)S(1)} %get-tuple-element.114), channel_id=1, source_target_pairs={{0,192},{64,128},{128,64},{192,0},{1,193},{65,129},{129,65},{193,1... | collective-permute-start | bytes 73736 | tf_op jit(solution)/shard_map/ppermute | solution.py:492
  41.0 0.0 collective-permute-done.12
  41.0 1.8 %collective-permute-done.13 = f32[2,3,8,128]{3,2,1,0:T(8,128)S(1)} collective-permute-done((f32[2,3,8,128]{3,2,1,0:T(8,128)S(1)}, f32[2,3,8,128]{3,2,1,0:T(8,128)S(1)}, u32[]{:S(2)}, u32[]{:S(2)}) %collective-permute-start.13) | collective-permute-done | bytes 24608 | tf_op jit(solution)/shard_map/ppermute | solution.py:492
  42.8 1.0 %collective-permute-start.16 = (f32[2,3,8,128]{3,2,1,0:T(8,128)S(1)}, f32[2,3,8,128]{3,2,1,0:T(8,128)S(1)}, u32[]{:S(2)}, u32[]{:S(2)}) collective-permute-start(f32[2,3,8,128]{3,2,1,0:T(8,128)S(1)} %add_add_fusion), channel_id=1, source_target_pairs={{0,12},{1,13},{2,14},{3,15},{4,0},{5,1},{6,2},{7,3},{8,4},{9,5},{1... | collective-permute-start | bytes 73736 | tf_op jit(solution)/shard_map/ppermute | solution.py:495
  43.8 1.1 %collective-permute-start.15 = (f32[2,3,8,128]{3,2,1,0:T(8,128)S(1)}, f32[2,3,8,128]{3,2,1,0:T(8,128)S(1)}, u32[]{:S(2)}, u32[]{:S(2)}) collective-permute-start(f32[2,3,8,128]{3,2,1,0:T(8,128)S(1)} %add_add_fusion), channel_id=1, source_target_pairs={{0,8},{1,9},{2,10},{3,11},{4,12},{5,13},{6,14},{7,15},{8,0},{9,1},... | collective-permute-start | bytes 73736 | tf_op jit(solution)/shard_map/ppermute | solution.py:495
  44.9 1.9 %collective-permute-start.14 = (f32[2,3,8,128]{3,2,1,0:T(8,128)S(1)}, f32[2,3,8,128]{3,2,1,0:T(8,128)S(1)}, u32[]{:S(2)}, u32[]{:S(2)}) collective-permute-start(f32[2,3,8,128]{3,2,1,0:T(8,128)S(1)} %add_add_fusion), channel_id=1, source_target_pairs={{0,4},{1,5},{2,6},{3,7},{4,8},{5,9},{6,10},{7,11},{8,12},{9,13},{1... | collective-permute-start | bytes 73736 | tf_op jit(solution)/shard_map/ppermute | solution.py:495
  48.0 1.3 %prepare.1 = (bf16[256,1024]{1,0:T(8,128)(2,1)S(1)}, bf16[256,1024]{1,0:T(8,128)(2,1)S(1)}, bf16[512,1024]{1,0:T(8,128)(2,1)S(1)}, bf16[512,1024]{1,0:T(8,128)(2...) custom-call(s32[1]{0:T(128)S(6)} %copy.19.ins_time, ...), custom_call_target="tpu_custom_call" | custom-call | flops 100000000 | bytes 8000000 | tf_op jit(solution)/shard_map/prepare/pallas_call | solution.py:323
  49.3 0.0 collective-permute-done.16
  49.3 1.2 %collective-permute-done.15 = f32[2,3,8,128]{3,2,1,0:T(8,128)S(1)} collective-permute-done((f32[2,3,8,128]{3,2,1,0:T(8,128)S(1)}, f32[2,3,8,128]{3,2,1,0:T(8,128)S(1)}, u32[]{:S(2)}, u32[]{:S(2)}) %collective-permute-start.15) | collective-permute-done | bytes 24608 | tf_op jit(solution)/shard_map/ppermute | solution.py:495
  50.5 0.0 collective-permute-done.14
  50.5 0.5 collective-permute-start.18
  51.0 1.5 %collective-permute-start.17 = (f32[4,2,3,8,128]{4,3,2,1,0:T(8,128)S(1)}, f32[4,2,3,8,128]{4,3,2,1,0:T(8,128)S(1)}, u32[]{:S(2)}, u32[]{:S(2)}) collective-permute-start(f32[4,2,3,8,128]{4,3,2,1,0:T(8,128)S(1)} %get-tuple-element.112), channel_id=1, source_target_pairs={{0,1},{1,2},{2,3},{3,0},{4,5},{5,6},{6,7},{7,4},{8,9},{9,10},{10,1... | collective-permute-start | bytes 294920 | tf_op jit(solution)/shard_map/ppermute | solution.py:499
  52.4 1.2 %collective-permute-start.19 = (f32[4,2,3,8,128]{4,3,2,1,0:T(8,128)S(1)}, f32[4,2,3,8,128]{4,3,2,1,0:T(8,128)S(1)}, u32[]{:S(2)}, u32[]{:S(2)}) collective-permute-start(f32[4,2,3,8,128]{4,3,2,1,0:T(8,128)S(1)} %get-tuple-element.112), channel_id=1, source_target_pairs={{0,3},{1,0},{2,1},{3,2},{4,7},{5,4},{6,5},{7,6},{8,11},{9,8},{10,9... | collective-permute-start | bytes 294920 | tf_op jit(solution)/shard_map/ppermute | solution.py:499
  53.7 2.0 %collective-permute-done.18 = f32[4,2,3,8,128]{4,3,2,1,0:T(8,128)S(1)} collective-permute-done((f32[4,2,3,8,128]{4,3,2,1,0:T(8,128)S(1)}, f32[4,2,3,8,128]{4,3,2,1,0:T(8,128)S(1)}, u32[]{:S(2)}, u32[]{:S(2)}) %collective-permute-start.18) | collective-permute-done | bytes 98336 | tf_op jit(solution)/shard_map/ppermute | solution.py:499
  55.7 0.9 collective-permute-done.17
  56.6 4.6 %collective-permute-start.20 = (f32[4,4,2,3,8,128]{5,4,3,2,1,0:T(8,128)S(1)}, f32[4,4,2,3,8,128]{5,4,3,2,1,0:T(8,128)S(1)}, u32[]{:S(2)}, u32[]{:S(2)}) collective-permute-start(f32[4,4,2,3,8,128]{5,4,3,2,1,0:T(8,128)S(1)} %pad_maximum_fusion.mine), channel_id=1, source_target_pairs={{0,64},{64,0},{128,192},{192,128},{1,65},{65,1},{129,193},{193,129... | collective-permute-start | bytes 1179656 | tf_op jit(solution)/shard_map/ppermute | solution.py:500
  61.2 1.3 %collective-permute-done.20.others = f32[4,4,2,3,8,128]{5,4,3,2,1,0:T(8,128)S(1)} collective-permute-done((f32[4,4,2,3,8,128]{5,4,3,2,1,0:T(8,128)S(1)}, f32[4,4,2,3,8,128]{5,4,3,2,1,0:T(8,128)S(1)}, u32[]{:S(2)}, u32[]{:S(2)}) %collective-permute-start.20) | collective-permute-done | bytes 393248 | tf_op jit(solution)/shard_map/ppermute | solution.py:500
  62.6 3.3 %left.1 = (bf16[1024,768]{1,0:T(8,128)(2,1)S(1)}, bf16[1024,768]{1,0:T(8,128)(2,1)S(1)}, f32[128,768]{1,0:T(8,128)S(1)}, f32[128,768]{1,0:T(8,128)S(1)}) custom-call(f32[4,4,2,3,8,128]{5,4,3,2,1,0:T(8,128)S(1)} %pad_maximum_fusion.mine, f32[4,4,2,3,8,128]{5,4,3,2,1,0:T(8,128)S(1)} %collective-permute-done.20.others, ...), custom_call_target="tpu_custom_call" | custom-call | flops 1000000000 | bytes 4000000 | tf_op jit(solution)/shard_map/left/pallas_call | solution.py:374
  65.9 1.4 %collective-permute-start.21 = (f32[128,768]{1,0:T(8,128)S(1)}, f32[128,768]{1,0:T(8,128)S(1)}, u32[]{:S(2)}, u32[]{:S(2)}) collective-permute-start(f32[128,768]{1,0:T(8,128)S(1)} %get-tuple-element.102), channel_id=1, source_target_pairs={{0,16},{16,32},{32,48},{48,0},{1,17},{17,33},{33,49},{49,1},{2,18}... | collective-permute-start | bytes 1179656 | tf_op jit(solution)/shard_map/ppermute | solution.py:507
  67.3 1.5 %collective-permute-start.22 = (f32[128,768]{1,0:T(8,128)S(1)}, f32[128,768]{1,0:T(8,128)S(1)}, u32[]{:S(2)}, u32[]{:S(2)}) collective-permute-start(f32[128,768]{1,0:T(8,128)S(1)} %get-tuple-element.104), channel_id=1, source_target_pairs={{0,48},{16,0},{32,16},{48,32},{1,49},{17,1},{33,17},{49,33},{2,50}... | collective-permute-start | bytes 1179656 | tf_op jit(solution)/shard_map/ppermute | solution.py:510
  68.8 2.6 %right.2 = (f32[128,768]{1,0:T(8,128)S(1)}, f32[128,768]{1,0:T(8,128)S(1)}, f32[128,768]{1,0:T(8,128)S(1)}, f32[128,768]{1,0:T(8,128)S(1)}) custom-call(bf16[512,1024]{1,0:T(8,128)(2,1)S(1)} %get-tuple-element.82.src_hi, bf16[512,1024]{1,0:T(8,128)(2,1)S(1)} %get-tuple-element.83.src_lo, bf16[1024,768]{1,0:T(8,128)(2,1)S(1)} %get-tuple-element.91.left_hi, ...), custom_call_target="tpu_custom_call" | custom-call | flops 1000000000 | bytes 5000000 | tf_op jit(solution)/shard_map/right/pallas_call | solution.py:397
  71.4 1.4 %right.3 = (f32[128,768]{1,0:T(8,128)S(1)}, f32[128,768]{1,0:T(8,128)S(1)}) custom-call(bf16[256,1024]{1,0:T(8,128)(2,1)S(1)} %get-tuple-element.95.src_hi, bf16[256,1024]{1,0:T(8,128)(2,1)S(1)} %get-tuple-element.96.src_lo, bf16[1024,768]{1,0:T(8,128)(2,1)S(1)} %get-tuple-element.91.left_hi, bf16[1024,768]{1,0:T(8,128)(2,1)S(1)} %get-tuple-element.92.left_lo), custom_call_target="tpu_custom_call" | custom-call | flops 1000000000 | bytes 5000000 | tf_op jit(solution)/shard_map/right/pallas_call | solution.py:397
  72.8 0.1 collective-permute-start.24
  72.9 2.7 %collective-permute-start.25 = (f32[128,768]{1,0:T(8,128)S(1)}, f32[128,768]{1,0:T(8,128)S(1)}, u32[]{:S(2)}, u32[]{:S(2)}) collective-permute-start(f32[128,768]{1,0:T(8,128)S(1)} %get-tuple-element.107), channel_id=1, source_target_pairs={{0,48},{16,0},{32,16},{48,32},{1,49},{17,1},{33,17},{49,33},{2,50}... | collective-permute-start | bytes 1179656 | tf_op jit(solution)/shard_map/ppermute | solution.py:510
  75.5 2.1 %collective-permute-done.21.second = f32[128,768]{1,0:T(8,128)S(1)} collective-permute-done((f32[128,768]{1,0:T(8,128)S(1)}, f32[128,768]{1,0:T(8,128)S(1)}, u32[]{:S(2)}, u32[]{:S(2)}) %collective-permute-start.21) | collective-permute-done | bytes 393248 | tf_op jit(solution)/shard_map/ppermute | solution.py:507
  77.7 0.1 relay.1
  77.7 1.0 %collective-permute-start.23 = (f32[128,768]{1,0:T(8,128)S(1)}, f32[128,768]{1,0:T(8,128)S(1)}, u32[]{:S(2)}, u32[]{:S(2)}) collective-permute-start(f32[128,768]{1,0:T(8,128)S(1)} %get-tuple-element.105), channel_id=1, source_target_pairs={{0,16},{16,32},{32,48},{48,0},{1,17},{17,33},{33,49},{49,1},{2,18}... | collective-permute-start | bytes 1179656 | tf_op jit(solution)/shard_map/ppermute | solution.py:507
  78.7 1.7 %collective-permute-start.26 = (f32[128,768]{1,0:T(8,128)S(1)}, f32[128,768]{1,0:T(8,128)S(1)}, u32[]{:S(2)}, u32[]{:S(2)}) collective-permute-start(f32[128,768]{1,0:T(8,128)S(1)} %get-tuple-element.108), channel_id=1, source_target_pairs={{0,48},{16,0},{32,16},{48,32},{1,49},{17,1},{33,17},{49,33},{2,50}... | collective-permute-start | bytes 1179656 | tf_op jit(solution)/shard_map/ppermute | solution.py:510
  80.5 5.6 %collective-permute-done.24.refs_3_ = f32[128,768]{1,0:T(8,128)S(1)} collective-permute-done((f32[128,768]{1,0:T(8,128)S(1)}, f32[128,768]{1,0:T(8,128)S(1)}, u32[]{:S(2)}, u32[]{:S(2)}) %collective-permute-start.24) | collective-permute-done | bytes 393248 | tf_op jit(solution)/shard_map/ppermute | solution.py:507
  86.1 8.4 %collective-permute-done.23.refs_2_ = f32[128,768]{1,0:T(8,128)S(1)} collective-permute-done((f32[128,768]{1,0:T(8,128)S(1)}, f32[128,768]{1,0:T(8,128)S(1)}, u32[]{:S(2)}, u32[]{:S(2)}) %collective-permute-start.23) | collective-permute-done | bytes 393248 | tf_op jit(solution)/shard_map/ppermute | solution.py:507
  94.5 1.4 %final.1 = f32[128,6,2,128]{3,2,1,0:T(2,128)} custom-call(f32[128,768]{1,0:T(8,128)S(1)} %get-tuple-element.99.refs_0_, f32[128,768]{1,0:T(8,128)S(1)} %get-tuple-element.100.refs_1_, f32[128,768]{1,0:T(8,128)S(1)} %collective-permute-done.23.refs_2_, f32[128,768]{1,0:T(8,128)S(1)} %collective-permute-done.24.refs_3_, ...), custom_call_target="tpu_custom_call" | custom-call | tf_op jit(solution)/shard_map/final/pallas_call | solution.py:434
  (30 shorter events, 0.2 us)
Async XLA Ops:
  0.0 26.2 %copy-start.1 = (f32[1,3,2,3,3,4,256]{6,5,4,3,2,1,0:T(4,128)S(1)}, f32[1,3,2,3,3,4,256]{6,5,4,3,2,1,0:T(4,128)}, u32[]{:S(2)}) copy-start(f32[1,3,2,3,3,4,256]{6,5,4,3,2,1,0:T(4,128)} %param.9) | copy-start | bytes 663556
  0.0 1.0 %copy-start.4 = (f32[1,2,3,8,4,256]{5,4,3,2,1,0:T(4,128)S(1)}, f32[1,2,3,8,4,256]{5,4,3,2,1,0:T(4,128)}, u32[]{:S(2)}) copy-start(f32[1,2,3,8,4,256]{5,4,3,2,1,0:T(4,128)} %param.8) | copy-start | bytes 589828
  1.3 8.2 %collective-permute-start.4 = (f32[2,1,3,8,256]{4,3,2,1,0:T(8,128)S(1)}, f32[2,1,3,8,256]{4,3,2,1,0:T(8,128)S(1)}, u32[]{:S(2)}, u32[]{:S(2)}) collective-permute-start(f32[2,1,3,8,256]{4,3,2,1,0:T(8,128)S(1)} %get-tuple-element.109), channel_id=1, source_target_pairs={{0,64},{64,128},{128,192},{192,0},{1,65},{65,129},{129,193},{193,1... | collective-permute-start | bytes 147464 | tf_op jit(solution)/shard_map/ppermute | solution.py:468
  4.4 5.1 %collective-permute-start.5 = (f32[2,1,3,8,256]{4,3,2,1,0:T(8,128)S(1)}, f32[2,1,3,8,256]{4,3,2,1,0:T(8,128)S(1)}, u32[]{:S(2)}, u32[]{:S(2)}) collective-permute-start(f32[2,1,3,8,256]{4,3,2,1,0:T(8,128)S(1)} %get-tuple-element.110), channel_id=1, source_target_pairs={{0,192},{64,0},{128,64},{192,128},{1,193},{65,1},{129,65},{193,129... | collective-permute-start | bytes 147464 | tf_op jit(solution)/shard_map/ppermute | solution.py:469
  4.7 14.4 %collective-permute-start.1 = (f32[2,4,3,8,256]{4,3,2,1,0:T(8,128)S(1)}, f32[2,4,3,8,256]{4,3,2,1,0:T(8,128)S(1)}, u32[]{:S(2)}, u32[]{:S(2)}) collective-permute-start(f32[2,4,3,8,256]{4,3,2,1,0:T(8,128)S(1)} %pack.1.refs_0_), channel_id=1, source_target_pairs={{0,12},{1,13},{2,14},{3,15},{4,0},{5,1},{6,2},{7,3},{8,4},{9,5},{1... | collective-permute-start | bytes 589832 | tf_op jit(solution)/shard_map/ppermute | solution.py:457
  9.5 10.2 %collective-permute-start = (f32[2,4,3,8,256]{4,3,2,1,0:T(8,128)S(1)}, f32[2,4,3,8,256]{4,3,2,1,0:T(8,128)S(1)}, u32[]{:S(2)}, u32[]{:S(2)}) collective-permute-start(f32[2,4,3,8,256]{4,3,2,1,0:T(8,128)S(1)} %pack.1.refs_0_), channel_id=1, source_target_pairs={{0,4},{1,5},{2,6},{3,7},{4,8},{5,9},{6,10},{7,11},{8,12},{9,13},{1... | collective-permute-start | bytes 589832 | tf_op jit(solution)/shard_map/ppermute | solution.py:457
  9.6 22.6 %copy-start.6 = (s32[3]{0:T(128)S(1)}, s32[3]{0:T(128)}, u32[]{:S(2)}) copy-start(s32[3]{0:T(128)} %directions.3) | copy-start | bytes 40
  9.6 10.1 %collective-permute-start.7 = (f32[2,6,3,8,256]{4,3,2,1,0:T(8,128)S(1)}, f32[2,6,3,8,256]{4,3,2,1,0:T(8,128)S(1)}, u32[]{:S(2)}, u32[]{:S(2)}) collective-permute-start(f32[2,6,3,8,256]{4,3,2,1,0:T(8,128)S(1)} %pad_maximum_fusion.1.refs_0_), channel_id=1, source_target_pairs={{0,3},{1,0},{2,1},{3,2},{4,7},{5,4},{6,5},{7,6},{8,11},{9,8},{10,9... | collective-permute-start | bytes 884744 | tf_op jit(solution)/shard_map/ppermute | solution.py:457
  12.1 8.0 %collective-permute-start.6 = (f32[2,6,3,8,256]{4,3,2,1,0:T(8,128)S(1)}, f32[2,6,3,8,256]{4,3,2,1,0:T(8,128)S(1)}, u32[]{:S(2)}, u32[]{:S(2)}) collective-permute-start(f32[2,6,3,8,256]{4,3,2,1,0:T(8,128)S(1)} %pad_maximum_fusion.1.refs_0_), channel_id=1, source_target_pairs={{0,1},{1,2},{2,3},{3,0},{4,5},{5,6},{6,7},{7,4},{8,9},{9,10},{10,1... | collective-permute-start | bytes 884744 | tf_op jit(solution)/shard_map/ppermute | solution.py:457
  13.1 4.4 %collective-permute-start.8 = (f32[18,256]{1,0:T(8,128)S(1)}, f32[18,256]{1,0:T(8,128)S(1)}, u32[]{:S(2)}, u32[]{:S(2)}) collective-permute-start(f32[18,256]{1,0:T(8,128)S(1)} %bitcast.47), channel_id=1, source_target_pairs={{0,64},{64,128},{128,192},{192,0},{1,65},{65,129},{129,193},{193,1... | collective-permute-start | bytes 55304 | tf_op jit(solution)/shard_map/ppermute | solution.py:473
  15.4 0.7 copy-start.5
  16.1 0.7 copy-start.7
  17.5 0.9 copy-start
  20.2 7.4 %collective-permute-start.10 = (f32[6,3,8,256]{3,2,1,0:T(8,128)S(1)}, f32[6,3,8,256]{3,2,1,0:T(8,128)S(1)}, u32[]{:S(2)}, u32[]{:S(2)}) collective-permute-start(f32[6,3,8,256]{3,2,1,0:T(8,128)S(1)} %slice_bitcast_fusion), channel_id=1, source_target_pairs={{0,3},{1,0},{2,1},{3,2},{4,7},{5,4},{6,5},{7,6},{8,11},{9,8},{10,9... | collective-permute-start | bytes 442376 | tf_op jit(solution)/shard_map/ppermute | solution.py:461
  22.3 5.3 %collective-permute-start.9 = (f32[6,3,8,256]{3,2,1,0:T(8,128)S(1)}, f32[6,3,8,256]{3,2,1,0:T(8,128)S(1)}, u32[]{:S(2)}, u32[]{:S(2)}) collective-permute-start(f32[6,3,8,256]{3,2,1,0:T(8,128)S(1)} %slice_bitcast_fusion.1), channel_id=1, source_target_pairs={{0,1},{1,2},{2,3},{3,0},{4,5},{5,6},{6,7},{7,4},{8,9},{9,10},{10,1... | collective-permute-start | bytes 442376 | tf_op jit(solution)/shard_map/ppermute | solution.py:461
  22.3 6.5 %collective-permute-start.3 = (f32[4,3,8,256]{3,2,1,0:T(8,128)S(1)}, f32[4,3,8,256]{3,2,1,0:T(8,128)S(1)}, u32[]{:S(2)}, u32[]{:S(2)}) collective-permute-start(f32[4,3,8,256]{3,2,1,0:T(8,128)S(1)} %slice_bitcast_fusion.2), channel_id=1, source_target_pairs={{0,12},{1,13},{2,14},{3,15},{4,0},{5,1},{6,2},{7,3},{8,4},{9,5},{1... | collective-permute-start | bytes 294920 | tf_op jit(solution)/shard_map/ppermute | solution.py:461
  26.2 5.9 %collective-permute-start.2 = (f32[4,3,8,256]{3,2,1,0:T(8,128)S(1)}, f32[4,3,8,256]{3,2,1,0:T(8,128)S(1)}, u32[]{:S(2)}, u32[]{:S(2)}) collective-permute-start(f32[4,3,8,256]{3,2,1,0:T(8,128)S(1)} %slice_bitcast_fusion.3), channel_id=1, source_target_pairs={{0,4},{1,5},{2,6},{3,7},{4,8},{5,9},{6,10},{7,11},{8,12},{9,13},{1... | collective-permute-start | bytes 294920 | tf_op jit(solution)/shard_map/ppermute | solution.py:461
  32.1 15.9 %copy-start.2 = (f32[1,2,512,512]{3,2,1,0:T(8,128)S(1)}, f32[1,2,512,512]{3,2,1,0:T(8,128)}, u32[]{:S(2)}) copy-start(f32[1,2,512,512]{3,2,1,0:T(8,128)} %param.15) | copy-start | bytes 6291460
  32.2 15.9 %copy-start.3 = (f32[1,1,2,128,512]{4,3,2,1,0:T(8,128)S(1)}, f32[1,1,2,128,512]{4,3,2,1,0:T(8,128)}, u32[]{:S(2)}) copy-start(f32[1,1,2,128,512]{4,3,2,1,0:T(8,128)} %param.14) | copy-start | bytes 1572868
  34.8 6.2 %collective-permute-start.12 = (f32[2,3,8,128]{3,2,1,0:T(8,128)S(1)}, f32[2,3,8,128]{3,2,1,0:T(8,128)S(1)}, u32[]{:S(2)}, u32[]{:S(2)}) collective-permute-start(f32[2,3,8,128]{3,2,1,0:T(8,128)S(1)} %get-tuple-element.113), channel_id=1, source_target_pairs={{0,128},{64,192},{128,0},{192,64},{1,129},{65,193},{129,1},{193,65... | collective-permute-start | bytes 73736 | tf_op jit(solution)/shard_map/ppermute | solution.py:491
  36.3 6.5 %collective-permute-start.13 = (f32[2,3,8,128]{3,2,1,0:T(8,128)S(1)}, f32[2,3,8,128]{3,2,1,0:T(8,128)S(1)}, u32[]{:S(2)}, u32[]{:S(2)}) collective-permute-start(f32[2,3,8,128]{3,2,1,0:T(8,128)S(1)} %get-tuple-element.114), channel_id=1, source_target_pairs={{0,192},{64,128},{128,64},{192,0},{1,193},{65,129},{129,65},{193,1... | collective-permute-start | bytes 73736 | tf_op jit(solution)/shard_map/ppermute | solution.py:492
  41.0 1.8 %collective-permute-start.11 = (f32[2,3,8,128]{3,2,1,0:T(8,128)S(1)}, f32[2,3,8,128]{3,2,1,0:T(8,128)S(1)}, u32[]{:S(2)}, u32[]{:S(2)}) collective-permute-start(f32[2,3,8,128]{3,2,1,0:T(8,128)S(1)} %get-tuple-element.114), channel_id=1, source_target_pairs={{0,64},{64,0},{128,192},{192,128},{1,65},{65,1},{129,193},{193,129... | collective-permute-start | bytes 73736 | tf_op jit(solution)/shard_map/ppermute | solution.py:490
  42.8 6.5 %collective-permute-start.16 = (f32[2,3,8,128]{3,2,1,0:T(8,128)S(1)}, f32[2,3,8,128]{3,2,1,0:T(8,128)S(1)}, u32[]{:S(2)}, u32[]{:S(2)}) collective-permute-start(f32[2,3,8,128]{3,2,1,0:T(8,128)S(1)} %add_add_fusion), channel_id=1, source_target_pairs={{0,12},{1,13},{2,14},{3,15},{4,0},{5,1},{6,2},{7,3},{8,4},{9,5},{1... | collective-permute-start | bytes 73736 | tf_op jit(solution)/shard_map/ppermute | solution.py:495
  43.8 6.7 %collective-permute-start.15 = (f32[2,3,8,128]{3,2,1,0:T(8,128)S(1)}, f32[2,3,8,128]{3,2,1,0:T(8,128)S(1)}, u32[]{:S(2)}, u32[]{:S(2)}) collective-permute-start(f32[2,3,8,128]{3,2,1,0:T(8,128)S(1)} %add_add_fusion), channel_id=1, source_target_pairs={{0,8},{1,9},{2,10},{3,11},{4,12},{5,13},{6,14},{7,15},{8,0},{9,1},... | collective-permute-start | bytes 73736 | tf_op jit(solution)/shard_map/ppermute | solution.py:495
  44.9 5.6 %collective-permute-start.14 = (f32[2,3,8,128]{3,2,1,0:T(8,128)S(1)}, f32[2,3,8,128]{3,2,1,0:T(8,128)S(1)}, u32[]{:S(2)}, u32[]{:S(2)}) collective-permute-start(f32[2,3,8,128]{3,2,1,0:T(8,128)S(1)} %add_add_fusion), channel_id=1, source_target_pairs={{0,4},{1,5},{2,6},{3,7},{4,8},{5,9},{6,10},{7,11},{8,12},{9,13},{1... | collective-permute-start | bytes 73736 | tf_op jit(solution)/shard_map/ppermute | solution.py:495
  50.5 5.2 %collective-permute-start.18 = (f32[4,2,3,8,128]{4,3,2,1,0:T(8,128)S(1)}, f32[4,2,3,8,128]{4,3,2,1,0:T(8,128)S(1)}, u32[]{:S(2)}, u32[]{:S(2)}) collective-permute-start(f32[4,2,3,8,128]{4,3,2,1,0:T(8,128)S(1)} %get-tuple-element.112), channel_id=1, source_target_pairs={{0,2},{1,3},{2,0},{3,1},{4,6},{5,7},{6,4},{7,5},{8,10},{9,11},{10,... | collective-permute-start | bytes 294920 | tf_op jit(solution)/shard_map/ppermute | solution.py:499
  51.0 5.6 %collective-permute-start.17 = (f32[4,2,3,8,128]{4,3,2,1,0:T(8,128)S(1)}, f32[4,2,3,8,128]{4,3,2,1,0:T(8,128)S(1)}, u32[]{:S(2)}, u32[]{:S(2)}) collective-permute-start(f32[4,2,3,8,128]{4,3,2,1,0:T(8,128)S(1)} %get-tuple-element.112), channel_id=1, source_target_pairs={{0,1},{1,2},{2,3},{3,0},{4,5},{5,6},{6,7},{7,4},{8,9},{9,10},{10,1... | collective-permute-start | bytes 294920 | tf_op jit(solution)/shard_map/ppermute | solution.py:499
  52.4 4.2 %collective-permute-start.19 = (f32[4,2,3,8,128]{4,3,2,1,0:T(8,128)S(1)}, f32[4,2,3,8,128]{4,3,2,1,0:T(8,128)S(1)}, u32[]{:S(2)}, u32[]{:S(2)}) collective-permute-start(f32[4,2,3,8,128]{4,3,2,1,0:T(8,128)S(1)} %get-tuple-element.112), channel_id=1, source_target_pairs={{0,3},{1,0},{2,1},{3,2},{4,7},{5,4},{6,5},{7,6},{8,11},{9,8},{10,9... | collective-permute-start | bytes 294920 | tf_op jit(solution)/shard_map/ppermute | solution.py:499
  56.6 5.9 %collective-permute-start.20 = (f32[4,4,2,3,8,128]{5,4,3,2,1,0:T(8,128)S(1)}, f32[4,4,2,3,8,128]{5,4,3,2,1,0:T(8,128)S(1)}, u32[]{:S(2)}, u32[]{:S(2)}) collective-permute-start(f32[4,4,2,3,8,128]{5,4,3,2,1,0:T(8,128)S(1)} %pad_maximum_fusion.mine), channel_id=1, source_target_pairs={{0,64},{64,0},{128,192},{192,128},{1,65},{65,1},{129,193},{193,129... | collective-permute-start | bytes 1179656 | tf_op jit(solution)/shard_map/ppermute | solution.py:500
  65.9 11.7 %collective-permute-start.21 = (f32[128,768]{1,0:T(8,128)S(1)}, f32[128,768]{1,0:T(8,128)S(1)}, u32[]{:S(2)}, u32[]{:S(2)}) collective-permute-start(f32[128,768]{1,0:T(8,128)S(1)} %get-tuple-element.102), channel_id=1, source_target_pairs={{0,16},{16,32},{32,48},{48,0},{1,17},{17,33},{33,49},{49,1},{2,18}... | collective-permute-start | bytes 1179656 | tf_op jit(solution)/shard_map/ppermute | solution.py:507
  67.3 10.4 %collective-permute-start.22 = (f32[128,768]{1,0:T(8,128)S(1)}, f32[128,768]{1,0:T(8,128)S(1)}, u32[]{:S(2)}, u32[]{:S(2)}) collective-permute-start(f32[128,768]{1,0:T(8,128)S(1)} %get-tuple-element.104), channel_id=1, source_target_pairs={{0,48},{16,0},{32,16},{48,32},{1,49},{17,1},{33,17},{49,33},{2,50}... | collective-permute-start | bytes 1179656 | tf_op jit(solution)/shard_map/ppermute | solution.py:510
  72.8 13.3 %collective-permute-start.24 = (f32[128,768]{1,0:T(8,128)S(1)}, f32[128,768]{1,0:T(8,128)S(1)}, u32[]{:S(2)}, u32[]{:S(2)}) collective-permute-start(f32[128,768]{1,0:T(8,128)S(1)} %get-tuple-element.106), channel_id=1, source_target_pairs={{0,16},{16,32},{32,48},{48,0},{1,17},{17,33},{33,49},{49,1},{2,18}... | collective-permute-start | bytes 1179656 | tf_op jit(solution)/shard_map/ppermute | solution.py:507
  72.9 13.2 %collective-permute-start.25 = (f32[128,768]{1,0:T(8,128)S(1)}, f32[128,768]{1,0:T(8,128)S(1)}, u32[]{:S(2)}, u32[]{:S(2)}) collective-permute-start(f32[128,768]{1,0:T(8,128)S(1)} %get-tuple-element.107), channel_id=1, source_target_pairs={{0,48},{16,0},{32,16},{48,32},{1,49},{17,1},{33,17},{49,33},{2,50}... | collective-permute-start | bytes 1179656 | tf_op jit(solution)/shard_map/ppermute | solution.py:510
  77.7 16.8 %collective-permute-start.23 = (f32[128,768]{1,0:T(8,128)S(1)}, f32[128,768]{1,0:T(8,128)S(1)}, u32[]{:S(2)}, u32[]{:S(2)}) collective-permute-start(f32[128,768]{1,0:T(8,128)S(1)} %get-tuple-element.105), channel_id=1, source_target_pairs={{0,16},{16,32},{32,48},{48,0},{1,17},{17,33},{33,49},{49,1},{2,18}... | collective-permute-start | bytes 1179656 | tf_op jit(solution)/shard_map/ppermute | solution.py:507
  78.7 15.8 %collective-permute-start.26 = (f32[128,768]{1,0:T(8,128)S(1)}, f32[128,768]{1,0:T(8,128)S(1)}, u32[]{:S(2)}, u32[]{:S(2)}) collective-permute-start(f32[128,768]{1,0:T(8,128)S(1)} %get-tuple-element.108), channel_id=1, source_target_pairs={{0,48},{16,0},{32,16},{48,32},{1,49},{17,1},{33,17},{49,33},{2,50}... | collective-permute-start | bytes 1179656 | tf_op jit(solution)/shard_map/ppermute | solution.py:510

commit v4 on v3

--- a/solution.py
+++ b/solution.py
@@ -474,12 +474,12 @@
 
     phase, turn = phases(momenta, directions)
     waves_own = wave_blocks(1, [bra], links, top)
-    ket_near, phase = lax.optimization_barrier((ket_near, phase))
-    bra_near, waves_own = lax.optimization_barrier((bra_near, waves_own))
     ket_far = opposite(*ket_near, along_z)
+    ket_near, waves_own, phase = lax.optimization_barrier((ket_near, waves_own, phase))
+    waves_near = wave_blocks(2, bra_near, links, top)
+    bra_near, waves_near = lax.optimization_barrier((bra_near, waves_near))
     bra_far = opposite(*bra_near, along_x)
 
-    waves_near = wave_blocks(2, bra_near, links, top)
     waves_far = wave_blocks(1, bra_far, links, top)
     waves = (*waves_own, *waves_near[:2], *waves_far, *waves_near[2:])
     kets = (own, ket_near[0], *ket_far, ket_near[1])

time: 96.1 us -> 97.8 us (1.018)
  starting transfers between devices: 45.4 us -> 47.9 us
  local copies, waits for them, and re-layouts: 4.21 us -> 1.95 us
  waiting for transfers between devices: 28.2 us -> 29.6 us
    ppermute x1, waiting for transfers between devices: 0.01 us -> 2.72 us  [on_device(): top = lax.ppermute(links[36:, depth - 1], 'space', ring(4, 1))]
    unnamed x17 -> x13, local copies, waits for them, and re-layouts: 3.25 us -> 0.99 us
    ppermute x2, starting transfers between devices: 0.01 us -> 2.07 us  [opposite(): lax.ppermute(behind[0], 'tsink', along(1))]
    ppermute x2, starting transfers between devices: 0.01 us -> 1.84 us  [neighbours(): lax.ppermute(block, 'tsink', along(1))]
    ppermute x1, starting transfers between devices: 2.38 us -> 0.54 us  [on_device(): top = lax.ppermute(links[36:, depth - 1], 'space', ring(4, 1))]
    ppermute x1, starting transfers between devices: 4.67 us -> 2.96 us  [on_device(): lax.ppermute(blocks[1], 'space', [(i, i ^ 3) for i in range(4)])]
    ppermute x2, starting transfers between devices: 5.99 us -> 7.49 us  [opposite(): lax.ppermute(ahead[1], 'tsink', along(-1))]
    ppermute x3, starting transfers between devices: 3.92 us -> 5.38 us  [on_device(): columns = [lax.ppermute(summed, 'tsink', along_z(d)) for d in (1, 2, 3)]]
  transfers between devices with their start and end apart: 27 -> 27, of which waited for: 12 -> 11; matrix products, arithmetic and copies ran while one was open for 1% -> 1% of each run, Pallas kernels for 9% -> 9%
where the time goes in v4:
time: 97.8 us; the launch traced here: 97.6 us
  starting transfers between devices  47.9 us (49%)
  waiting for transfers between devices  29.6 us (30%)
  Pallas kernels  16.5 us (17%)
  local copies, waits for them, and re-layouts  1.95 us (2%)
  between operations  1.56 us (2%)
    ppermute x3, waiting for transfers between devices, up(): return lax.ppermute(value, 'tins', ring(4, 1))  16.1 us
    ppermute x2, starting transfers between devices, opposite(): lax.ppermute(ahead[1], 'tsink', along(-1))  7.49 us
    ppermute x2, starting transfers between devices, neighbours(): lax.ppermute(block, 'tsink', along(-1))  7.38 us
    ppermute x3, starting transfers between devices, down(): return lax.ppermute(value, 'tins', ring(4, -1))  5.94 us
    ppermute x3, starting transfers between devices, on_device(): columns = [lax.ppermute(summed, 'tsink', along_z(d)) for d in (1, 2, 3)]  5.38 us
    ppermute x1, starting transfers between devices, on_device(): others = lax.ppermute(summed, 'space', core_pairs)  5.2 us
    pallas_call x2, Pallas kernels, right_product(): pl.pallas_call(right_kernel, out_shape=(jax.ShapeDtypeStruct((128, 768),...  3.97 us
    ppermute x2, waiting for transfers between devices, opposite(): lax.ppermute(behind[0], 'tsink', along(1))  3.46 us
  transfers between devices with their start and end apart: 27, of which 11 were waited for; matrix products, arithmetic and copies ran while one was open for 1% of the time, Pallas kernels for 9%

profile of v4, /device:TPU:1, one launch (start us, length us, event | category | flops | bytes accessed | tf_op | source)
XLA Modules:
  0.0 97.6 jit_solution(15342094655049363311)
XLA Ops:
  0.0 1.0 copy-done.3
  1.0 0.3 pack.1.refs_0_
  1.3 3.1 %collective-permute-start.2 = (f32[2,1,3,8,256]{4,3,2,1,0:T(8,128)S(1)}, f32[2,1,3,8,256]{4,3,2,1,0:T(8,128)S(1)}, u32[]{:S(2)}, u32[]{:S(2)}) collective-permute-start(f32[2,1,3,8,256]{4,3,2,1,0:T(8,128)S(1)} %get-tuple-element.117), channel_id=1, source_target_pairs={{0,64},{64,128},{128,192},{192,0},{1,65},{65,129},{129,193},{193,1... | collective-permute-start | bytes 147464 | tf_op jit(solution)/shard_map/ppermute | solution.py:468
  4.4 0.3 collective-permute-start.3
  4.7 4.8 %collective-permute-start.1 = (f32[2,4,3,8,256]{4,3,2,1,0:T(8,128)S(1)}, f32[2,4,3,8,256]{4,3,2,1,0:T(8,128)S(1)}, u32[]{:S(2)}, u32[]{:S(2)}) collective-permute-start(f32[2,4,3,8,256]{4,3,2,1,0:T(8,128)S(1)} %pack.1.refs_0_), channel_id=1, source_target_pairs={{0,12},{1,13},{2,14},{3,15},{4,0},{5,1},{6,2},{7,3},{8,4},{9,5},{1... | collective-permute-start | bytes 589832 | tf_op jit(solution)/shard_map/ppermute | solution.py:457
  9.6 2.6 %collective-permute-start.8 = (f32[2,6,3,8,256]{4,3,2,1,0:T(8,128)S(1)}, f32[2,6,3,8,256]{4,3,2,1,0:T(8,128)S(1)}, u32[]{:S(2)}, u32[]{:S(2)}) collective-permute-start(f32[2,6,3,8,256]{4,3,2,1,0:T(8,128)S(1)} %pad_maximum_fusion.1.refs_0_), channel_id=1, source_target_pairs={{0,3},{1,0},{2,1},{3,2},{4,7},{5,4},{6,5},{7,6},{8,11},{9,8},{10,9... | collective-permute-start | bytes 884744 | tf_op jit(solution)/shard_map/ppermute | solution.py:457
  12.1 0.0 collective-permute-start.7
  12.1 1.8 %collective-permute-start = (f32[2,4,3,8,256]{4,3,2,1,0:T(8,128)S(1)}, f32[2,4,3,8,256]{4,3,2,1,0:T(8,128)S(1)}, u32[]{:S(2)}, u32[]{:S(2)}) collective-permute-start(f32[2,4,3,8,256]{4,3,2,1,0:T(8,128)S(1)} %pack.1.refs_0_), channel_id=1, source_target_pairs={{0,4},{1,5},{2,6},{3,7},{4,8},{5,9},{6,10},{7,11},{8,12},{9,13},{1... | collective-permute-start | bytes 589832 | tf_op jit(solution)/shard_map/ppermute | solution.py:457
  14.0 0.9 slice.40
  14.9 0.5 collective-permute-start.4
  15.4 0.0 collective-permute-done.1.refs_4_
  15.5 4.5 %collective-permute-start.6 = (f32[4,3,8,256]{3,2,1,0:T(8,128)S(1)}, f32[4,3,8,256]{3,2,1,0:T(8,128)S(1)}, u32[]{:S(2)}, u32[]{:S(2)}) collective-permute-start(f32[4,3,8,256]{3,2,1,0:T(8,128)S(1)} %slice_bitcast_fusion.2), channel_id=1, source_target_pairs={{0,12},{1,13},{2,14},{3,15},{4,0},{5,1},{6,2},{7,3},{8,4},{9,5},{1... | collective-permute-start | bytes 294920 | tf_op jit(solution)/shard_map/ppermute | solution.py:461
  19.9 2.7 %collective-permute-done.4.refs_2_.refs_3_ = f32[18,256]{1,0:T(8,128)S(1)} collective-permute-done((f32[18,256]{1,0:T(8,128)S(1)}, f32[18,256]{1,0:T(8,128)S(1)}, u32[]{:S(2)}, u32[]{:S(2)}) %collective-permute-start.4) | collective-permute-done | bytes 18464 | tf_op jit(solution)/shard_map/ppermute | solution.py:473
  22.6 0.0 collective-permute-done.8.refs_1_
  22.6 0.0 collective-permute-done.7.refs_0_
  22.7 1.4 %waves.4 = (bf16[4,48,1536]{2,1,0:T(8,128)(2,1)S(1)}, bf16[4,48,1536]{2,1,0:T(8,128)(2,1)S(1)}, bf16[4,48,1536]{2,1,0:T(8,128)(2,1)S(1)}, bf16[4,48,1536]{2,1,0:T(8,128)(2,1)S(1)}) custom-call(f32[2,6,3,8,256]{4,3,2,1,0:T(8,128)S(1)} %collective-permute-done.7.refs_0_, f32[2,6,3,8,256]{4,3,2,1,0:T(8,128)S(1)} %collective-permute-done.8.refs_1_, ...), custom_call_target="tpu_custom_call" | custom-call | flops 20000000 | bytes 4000000 | tf_op jit(solution)/shard_map/waves/pallas_call | solution.py:176
  24.1 3.0 %collective-permute-start.10 = (f32[6,3,8,256]{3,2,1,0:T(8,128)S(1)}, f32[6,3,8,256]{3,2,1,0:T(8,128)S(1)}, u32[]{:S(2)}, u32[]{:S(2)}) collective-permute-start(f32[6,3,8,256]{3,2,1,0:T(8,128)S(1)} %slice_bitcast_fusion), channel_id=1, source_target_pairs={{0,3},{1,0},{2,1},{3,2},{4,7},{5,4},{6,5},{7,6},{8,11},{9,8},{10,9... | collective-permute-start | bytes 442376 | tf_op jit(solution)/shard_map/ppermute | solution.py:461
  27.1 0.1 collective-permute-start.9
  27.2 0.0 collective-permute-done.refs_1_
  27.3 2.0 %collective-permute-start.5 = (f32[4,3,8,256]{3,2,1,0:T(8,128)S(1)}, f32[4,3,8,256]{3,2,1,0:T(8,128)S(1)}, u32[]{:S(2)}, u32[]{:S(2)}) collective-permute-start(f32[4,3,8,256]{3,2,1,0:T(8,128)S(1)} %slice_bitcast_fusion.3), channel_id=1, source_target_pairs={{0,4},{1,5},{2,6},{3,7},{4,8},{5,9},{6,10},{7,11},{8,12},{9,13},{1... | collective-permute-start | bytes 294920 | tf_op jit(solution)/shard_map/ppermute | solution.py:461
  29.2 0.7 phases.1
  29.9 0.7 waves.3
  30.7 0.0 collective-permute-done.10.refs_1_
  30.7 3.2 %collective-permute-done.9.refs_0_ = f32[6,3,8,256]{3,2,1,0:T(8,128)S(1)} collective-permute-done((f32[6,3,8,256]{3,2,1,0:T(8,128)S(1)}, f32[6,3,8,256]{3,2,1,0:T(8,128)S(1)}, u32[]{:S(2)}, u32[]{:S(2)}) %collective-permute-start.9) | collective-permute-done | bytes 147488 | tf_op jit(solution)/shard_map/ppermute | solution.py:461
  33.8 0.7 waves.5
  34.6 0.3 collective-permute-done.5.refs_2_
  34.9 2.6 %elementals.1 = f32[2,2,3,8,128]{4,3,2,1,0:T(8,128)S(1)} custom-call(s32[3]{0:T(128)S(1)} %copy-done.4, f32[2,4,3,8,256]{4,3,2,1,0:T(8,128)S(1)} %pack.1.refs_0_, f32[2,4,3,8,256]{4,3,2,1,0:T(8,128)S(1)} %collective-permute-done.refs_1_, f32[4,3,8,256]{3,2,1,0:T(8,128)S(1)} %collective-permute-done.5.refs_2_, ...), custom_call_target="tpu_custom_call" | custom-call | flops 1000000000 | bytes 3000000 | tf_op jit(solution)/shard_map/elementals/pallas_call | solution.py:239
  37.6 0.1 collective-permute-start.12
  37.7 3.0 %collective-permute-start.13 = (f32[2,3,8,128]{3,2,1,0:T(8,128)S(1)}, f32[2,3,8,128]{3,2,1,0:T(8,128)S(1)}, u32[]{:S(2)}, u32[]{:S(2)}) collective-permute-start(f32[2,3,8,128]{3,2,1,0:T(8,128)S(1)} %get-tuple-element.122), channel_id=1, source_target_pairs={{0,192},{64,128},{128,64},{192,0},{1,193},{65,129},{129,65},{193,1... | collective-permute-start | bytes 73736 | tf_op jit(solution)/shard_map/ppermute | solution.py:492
  40.6 0.3 collective-permute-start.11
  40.9 0.0 collective-permute-done.12
  40.9 1.4 %collective-permute-done.13 = f32[2,3,8,128]{3,2,1,0:T(8,128)S(1)} collective-permute-done((f32[2,3,8,128]{3,2,1,0:T(8,128)S(1)}, f32[2,3,8,128]{3,2,1,0:T(8,128)S(1)}, u32[]{:S(2)}, u32[]{:S(2)}) %collective-permute-start.13) | collective-permute-done | bytes 24608 | tf_op jit(solution)/shard_map/ppermute | solution.py:492
  42.3 0.0 collective-permute-done.11
  42.3 0.4 collective-permute-start.16
  42.7 4.0 %collective-permute-start.15 = (f32[2,3,8,128]{3,2,1,0:T(8,128)S(1)}, f32[2,3,8,128]{3,2,1,0:T(8,128)S(1)}, u32[]{:S(2)}, u32[]{:S(2)}) collective-permute-start(f32[2,3,8,128]{3,2,1,0:T(8,128)S(1)} %add_add_fusion), channel_id=1, source_target_pairs={{0,8},{1,9},{2,10},{3,11},{4,12},{5,13},{6,14},{7,15},{8,0},{9,1},... | collective-permute-start | bytes 73736 | tf_op jit(solution)/shard_map/ppermute | solution.py:495
  46.7 1.0 collective-permute-start.14
  49.0 1.3 %prepare.1 = (bf16[256,1024]{1,0:T(8,128)(2,1)S(1)}, bf16[256,1024]{1,0:T(8,128)(2,1)S(1)}, bf16[512,1024]{1,0:T(8,128)(2,1)S(1)}, bf16[512,1024]{1,0:T(8,128)(2...) custom-call(s32[1]{0:T(128)S(6)} %copy.19.ins_time, ...), custom_call_target="tpu_custom_call" | custom-call | flops 100000000 | bytes 8000000 | tf_op jit(solution)/shard_map/prepare/pallas_call | solution.py:323
  50.3 0.0 collective-permute-done.15
  50.3 1.5 %collective-permute-done.14 = f32[2,3,8,128]{3,2,1,0:T(8,128)S(1)} collective-permute-done((f32[2,3,8,128]{3,2,1,0:T(8,128)S(1)}, f32[2,3,8,128]{3,2,1,0:T(8,128)S(1)}, u32[]{:S(2)}, u32[]{:S(2)}) %collective-permute-start.14) | collective-permute-done | bytes 24608 | tf_op jit(solution)/shard_map/ppermute | solution.py:495
  51.8 0.1 collective-permute-start.18
  51.9 1.9 %collective-permute-start.17 = (f32[4,2,3,8,128]{4,3,2,1,0:T(8,128)S(1)}, f32[4,2,3,8,128]{4,3,2,1,0:T(8,128)S(1)}, u32[]{:S(2)}, u32[]{:S(2)}) collective-permute-start(f32[4,2,3,8,128]{4,3,2,1,0:T(8,128)S(1)} %get-tuple-element.120), channel_id=1, source_target_pairs={{0,1},{1,2},{2,3},{3,0},{4,5},{5,6},{6,7},{7,4},{8,9},{9,10},{10,1... | collective-permute-start | bytes 294920 | tf_op jit(solution)/shard_map/ppermute | solution.py:499
  53.8 0.9 collective-permute-start.19
  54.7 2.3 %collective-permute-done.18 = f32[4,2,3,8,128]{4,3,2,1,0:T(8,128)S(1)} collective-permute-done((f32[4,2,3,8,128]{4,3,2,1,0:T(8,128)S(1)}, f32[4,2,3,8,128]{4,3,2,1,0:T(8,128)S(1)}, u32[]{:S(2)}, u32[]{:S(2)}) %collective-permute-start.18) | collective-permute-done | bytes 98336 | tf_op jit(solution)/shard_map/ppermute | solution.py:499
  57.0 0.7 collective-permute-done.17
  57.8 0.0 collective-permute-done.19
  57.8 5.2 %collective-permute-start.20 = (f32[4,4,2,3,8,128]{5,4,3,2,1,0:T(8,128)S(1)}, f32[4,4,2,3,8,128]{5,4,3,2,1,0:T(8,128)S(1)}, u32[]{:S(2)}, u32[]{:S(2)}) collective-permute-start(f32[4,4,2,3,8,128]{5,4,3,2,1,0:T(8,128)S(1)} %pad_maximum_fusion.mine), channel_id=1, source_target_pairs={{0,64},{64,0},{128,192},{192,128},{1,65},{65,1},{129,193},{193,129... | collective-permute-start | bytes 1179656 | tf_op jit(solution)/shard_map/ppermute | solution.py:500
  63.0 1.3 %collective-permute-done.20.others = f32[4,4,2,3,8,128]{5,4,3,2,1,0:T(8,128)S(1)} collective-permute-done((f32[4,4,2,3,8,128]{5,4,3,2,1,0:T(8,128)S(1)}, f32[4,4,2,3,8,128]{5,4,3,2,1,0:T(8,128)S(1)}, u32[]{:S(2)}, u32[]{:S(2)}) %collective-permute-start.20) | collective-permute-done | bytes 393248 | tf_op jit(solution)/shard_map/ppermute | solution.py:500
  64.3 3.3 %left.1 = (bf16[1024,768]{1,0:T(8,128)(2,1)S(1)}, bf16[1024,768]{1,0:T(8,128)(2,1)S(1)}, f32[128,768]{1,0:T(8,128)S(1)}, f32[128,768]{1,0:T(8,128)S(1)}) custom-call(f32[4,4,2,3,8,128]{5,4,3,2,1,0:T(8,128)S(1)} %pad_maximum_fusion.mine, f32[4,4,2,3,8,128]{5,4,3,2,1,0:T(8,128)S(1)} %collective-permute-done.20.others, ...), custom_call_target="tpu_custom_call" | custom-call | flops 1000000000 | bytes 4000000 | tf_op jit(solution)/shard_map/left/pallas_call | solution.py:374
  67.7 1.4 %collective-permute-start.21 = (f32[128,768]{1,0:T(8,128)S(1)}, f32[128,768]{1,0:T(8,128)S(1)}, u32[]{:S(2)}, u32[]{:S(2)}) collective-permute-start(f32[128,768]{1,0:T(8,128)S(1)} %get-tuple-element.110), channel_id=1, source_target_pairs={{0,16},{16,32},{32,48},{48,0},{1,17},{17,33},{33,49},{49,1},{2,18}... | collective-permute-start | bytes 1179656 | tf_op jit(solution)/shard_map/ppermute | solution.py:507
  69.0 1.5 %collective-permute-start.22 = (f32[128,768]{1,0:T(8,128)S(1)}, f32[128,768]{1,0:T(8,128)S(1)}, u32[]{:S(2)}, u32[]{:S(2)}) collective-permute-start(f32[128,768]{1,0:T(8,128)S(1)} %get-tuple-element.112), channel_id=1, source_target_pairs={{0,48},{16,0},{32,16},{48,32},{1,49},{17,1},{33,17},{49,33},{2,50}... | collective-permute-start | bytes 1179656 | tf_op jit(solution)/shard_map/ppermute | solution.py:510
  70.6 2.6 %right.2 = (f32[128,768]{1,0:T(8,128)S(1)}, f32[128,768]{1,0:T(8,128)S(1)}, f32[128,768]{1,0:T(8,128)S(1)}, f32[128,768]{1,0:T(8,128)S(1)}) custom-call(bf16[512,1024]{1,0:T(8,128)(2,1)S(1)} %get-tuple-element.90.src_hi, bf16[512,1024]{1,0:T(8,128)(2,1)S(1)} %get-tuple-element.91.src_lo, bf16[1024,768]{1,0:T(8,128)(2,1)S(1)} %get-tuple-element.99.left_hi, ...), custom_call_target="tpu_custom_call" | custom-call | flops 1000000000 | bytes 5000000 | tf_op jit(solution)/shard_map/right/pallas_call | solution.py:397
  73.2 1.4 %right.3 = (f32[128,768]{1,0:T(8,128)S(1)}, f32[128,768]{1,0:T(8,128)S(1)}) custom-call(bf16[256,1024]{1,0:T(8,128)(2,1)S(1)} %get-tuple-element.103.src_hi, bf16[256,1024]{1,0:T(8,128)(2,1)S(1)} %get-tuple-element.104.src_lo, bf16[1024,768]{1,0:T(8,128)(2,1)S(1)} %get-tuple-element.99.left_hi, bf16[1024,768]{1,0:T(8,128)(2,1)S(1)} %get-tuple-element.100.left_lo), custom_call_target="tpu_custom_call" | custom-call | flops 1000000000 | bytes 5000000 | tf_op jit(solution)/shard_map/right/pallas_call | solution.py:397
  74.6 0.1 collective-permute-start.24
  74.7 2.7 %collective-permute-start.25 = (f32[128,768]{1,0:T(8,128)S(1)}, f32[128,768]{1,0:T(8,128)S(1)}, u32[]{:S(2)}, u32[]{:S(2)}) collective-permute-start(f32[128,768]{1,0:T(8,128)S(1)} %get-tuple-element.115), channel_id=1, source_target_pairs={{0,48},{16,0},{32,16},{48,32},{1,49},{17,1},{33,17},{49,33},{2,50}... | collective-permute-start | bytes 1179656 | tf_op jit(solution)/shard_map/ppermute | solution.py:510
  77.3 2.1 %collective-permute-done.21.second = f32[128,768]{1,0:T(8,128)S(1)} collective-permute-done((f32[128,768]{1,0:T(8,128)S(1)}, f32[128,768]{1,0:T(8,128)S(1)}, u32[]{:S(2)}, u32[]{:S(2)}) %collective-permute-start.21) | collective-permute-done | bytes 393248 | tf_op jit(solution)/shard_map/ppermute | solution.py:507
  79.4 0.0 collective-permute-done.22.fourth
  79.4 0.1 relay.1
  79.5 1.0 %collective-permute-start.23 = (f32[128,768]{1,0:T(8,128)S(1)}, f32[128,768]{1,0:T(8,128)S(1)}, u32[]{:S(2)}, u32[]{:S(2)}) collective-permute-start(f32[128,768]{1,0:T(8,128)S(1)} %get-tuple-element.113), channel_id=1, source_target_pairs={{0,16},{16,32},{32,48},{48,0},{1,17},{17,33},{33,49},{49,1},{2,18}... | collective-permute-start | bytes 1179656 | tf_op jit(solution)/shard_map/ppermute | solution.py:507
  80.5 1.8 %collective-permute-start.26 = (f32[128,768]{1,0:T(8,128)S(1)}, f32[128,768]{1,0:T(8,128)S(1)}, u32[]{:S(2)}, u32[]{:S(2)}) collective-permute-start(f32[128,768]{1,0:T(8,128)S(1)} %get-tuple-element.116), channel_id=1, source_target_pairs={{0,48},{16,0},{32,16},{48,32},{1,49},{17,1},{33,17},{49,33},{2,50}... | collective-permute-start | bytes 1179656 | tf_op jit(solution)/shard_map/ppermute | solution.py:510
  82.3 5.6 %collective-permute-done.24.refs_3_ = f32[128,768]{1,0:T(8,128)S(1)} collective-permute-done((f32[128,768]{1,0:T(8,128)S(1)}, f32[128,768]{1,0:T(8,128)S(1)}, u32[]{:S(2)}, u32[]{:S(2)}) %collective-permute-start.24) | collective-permute-done | bytes 393248 | tf_op jit(solution)/shard_map/ppermute | solution.py:507
  87.8 0.0 collective-permute-done.25.refs_4_
  87.8 8.4 %collective-permute-done.23.refs_2_ = f32[128,768]{1,0:T(8,128)S(1)} collective-permute-done((f32[128,768]{1,0:T(8,128)S(1)}, f32[128,768]{1,0:T(8,128)S(1)}, u32[]{:S(2)}, u32[]{:S(2)}) %collective-permute-start.23) | collective-permute-done | bytes 393248 | tf_op jit(solution)/shard_map/ppermute | solution.py:507
  96.3 0.0 collective-permute-done.26.refs_5_
  96.3 1.4 %final.1 = f32[128,6,2,128]{3,2,1,0:T(2,128)} custom-call(f32[128,768]{1,0:T(8,128)S(1)} %get-tuple-element.107.refs_0_, f32[128,768]{1,0:T(8,128)S(1)} %get-tuple-element.108.refs_1_, f32[128,768]{1,0:T(8,128)S(1)} %collective-permute-done.23.refs_2_, f32[128,768]{1,0:T(8,128)S(1)} %collective-permute-done.24.refs_3_, ...), custom_call_target="tpu_custom_call" | custom-call | tf_op jit(solution)/shard_map/final/pallas_call | solution.py:434
  (26 shorter events, 0.2 us)
Async XLA Ops:
  0.0 22.7 %copy-start = (f32[1,3,2,3,3,4,256]{6,5,4,3,2,1,0:T(4,128)S(1)}, f32[1,3,2,3,3,4,256]{6,5,4,3,2,1,0:T(4,128)}, u32[]{:S(2)}) copy-start(f32[1,3,2,3,3,4,256]{6,5,4,3,2,1,0:T(4,128)} %param.9) | copy-start | bytes 663556
  0.0 1.0 copy-start.3
  1.0 28.3 %copy-start.4 = (s32[3]{0:T(128)S(1)}, s32[3]{0:T(128)}, u32[]{:S(2)}) copy-start(s32[3]{0:T(128)} %directions.3) | copy-start | bytes 40
  1.0 28.3 %copy-start.5 = (s32[2,3]{1,0:T(2,128)S(1)}, s32[2,3]{1,0:T(2,128)}, u32[]{:S(2)}) copy-start(s32[2,3]{1,0:T(2,128)} %momenta.1) | copy-start | bytes 76
  1.3 8.2 %collective-permute-start.2 = (f32[2,1,3,8,256]{4,3,2,1,0:T(8,128)S(1)}, f32[2,1,3,8,256]{4,3,2,1,0:T(8,128)S(1)}, u32[]{:S(2)}, u32[]{:S(2)}) collective-permute-start(f32[2,1,3,8,256]{4,3,2,1,0:T(8,128)S(1)} %get-tuple-element.117), channel_id=1, source_target_pairs={{0,64},{64,128},{128,192},{192,0},{1,65},{65,129},{129,193},{193,1... | collective-permute-start | bytes 147464 | tf_op jit(solution)/shard_map/ppermute | solution.py:468
  4.4 5.1 %collective-permute-start.3 = (f32[2,1,3,8,256]{4,3,2,1,0:T(8,128)S(1)}, f32[2,1,3,8,256]{4,3,2,1,0:T(8,128)S(1)}, u32[]{:S(2)}, u32[]{:S(2)}) collective-permute-start(f32[2,1,3,8,256]{4,3,2,1,0:T(8,128)S(1)} %get-tuple-element.118), channel_id=1, source_target_pairs={{0,192},{64,0},{128,64},{192,128},{1,193},{65,1},{129,65},{193,129... | collective-permute-start | bytes 147464 | tf_op jit(solution)/shard_map/ppermute | solution.py:469
  4.7 10.7 %collective-permute-start.1 = (f32[2,4,3,8,256]{4,3,2,1,0:T(8,128)S(1)}, f32[2,4,3,8,256]{4,3,2,1,0:T(8,128)S(1)}, u32[]{:S(2)}, u32[]{:S(2)}) collective-permute-start(f32[2,4,3,8,256]{4,3,2,1,0:T(8,128)S(1)} %pack.1.refs_0_), channel_id=1, source_target_pairs={{0,12},{1,13},{2,14},{3,15},{4,0},{5,1},{6,2},{7,3},{8,4},{9,5},{1... | collective-permute-start | bytes 589832 | tf_op jit(solution)/shard_map/ppermute | solution.py:457
  9.6 13.1 %collective-permute-start.8 = (f32[2,6,3,8,256]{4,3,2,1,0:T(8,128)S(1)}, f32[2,6,3,8,256]{4,3,2,1,0:T(8,128)S(1)}, u32[]{:S(2)}, u32[]{:S(2)}) collective-permute-start(f32[2,6,3,8,256]{4,3,2,1,0:T(8,128)S(1)} %pad_maximum_fusion.1.refs_0_), channel_id=1, source_target_pairs={{0,3},{1,0},{2,1},{3,2},{4,7},{5,4},{6,5},{7,6},{8,11},{9,8},{10,9... | collective-permute-start | bytes 884744 | tf_op jit(solution)/shard_map/ppermute | solution.py:457
  12.1 10.5 %collective-permute-start.7 = (f32[2,6,3,8,256]{4,3,2,1,0:T(8,128)S(1)}, f32[2,6,3,8,256]{4,3,2,1,0:T(8,128)S(1)}, u32[]{:S(2)}, u32[]{:S(2)}) collective-permute-start(f32[2,6,3,8,256]{4,3,2,1,0:T(8,128)S(1)} %pad_maximum_fusion.1.refs_0_), channel_id=1, source_target_pairs={{0,1},{1,2},{2,3},{3,0},{4,5},{5,6},{6,7},{7,4},{8,9},{9,10},{10,1... | collective-permute-start | bytes 884744 | tf_op jit(solution)/shard_map/ppermute | solution.py:457
  12.1 15.1 %collective-permute-start = (f32[2,4,3,8,256]{4,3,2,1,0:T(8,128)S(1)}, f32[2,4,3,8,256]{4,3,2,1,0:T(8,128)S(1)}, u32[]{:S(2)}, u32[]{:S(2)}) collective-permute-start(f32[2,4,3,8,256]{4,3,2,1,0:T(8,128)S(1)} %pack.1.refs_0_), channel_id=1, source_target_pairs={{0,4},{1,5},{2,6},{3,7},{4,8},{5,9},{6,10},{7,11},{8,12},{9,13},{1... | collective-permute-start | bytes 589832 | tf_op jit(solution)/shard_map/ppermute | solution.py:457
  14.9 7.8 %collective-permute-start.4 = (f32[18,256]{1,0:T(8,128)S(1)}, f32[18,256]{1,0:T(8,128)S(1)}, u32[]{:S(2)}, u32[]{:S(2)}) collective-permute-start(f32[18,256]{1,0:T(8,128)S(1)} %bitcast.47), channel_id=1, source_target_pairs={{0,64},{64,128},{128,192},{192,0},{1,65},{65,129},{129,193},{193,1... | collective-permute-start | bytes 55304 | tf_op jit(solution)/shard_map/ppermute | solution.py:473
  15.5 19.1 %collective-permute-start.6 = (f32[4,3,8,256]{3,2,1,0:T(8,128)S(1)}, f32[4,3,8,256]{3,2,1,0:T(8,128)S(1)}, u32[]{:S(2)}, u32[]{:S(2)}) collective-permute-start(f32[4,3,8,256]{3,2,1,0:T(8,128)S(1)} %slice_bitcast_fusion.2), channel_id=1, source_target_pairs={{0,12},{1,13},{2,14},{3,15},{4,0},{5,1},{6,2},{7,3},{8,4},{9,5},{1... | collective-permute-start | bytes 294920 | tf_op jit(solution)/shard_map/ppermute | solution.py:461
  24.1 6.6 %collective-permute-start.10 = (f32[6,3,8,256]{3,2,1,0:T(8,128)S(1)}, f32[6,3,8,256]{3,2,1,0:T(8,128)S(1)}, u32[]{:S(2)}, u32[]{:S(2)}) collective-permute-start(f32[6,3,8,256]{3,2,1,0:T(8,128)S(1)} %slice_bitcast_fusion), channel_id=1, source_target_pairs={{0,3},{1,0},{2,1},{3,2},{4,7},{5,4},{6,5},{7,6},{8,11},{9,8},{10,9... | collective-permute-start | bytes 442376 | tf_op jit(solution)/shard_map/ppermute | solution.py:461
  27.1 6.7 %collective-permute-start.9 = (f32[6,3,8,256]{3,2,1,0:T(8,128)S(1)}, f32[6,3,8,256]{3,2,1,0:T(8,128)S(1)}, u32[]{:S(2)}, u32[]{:S(2)}) collective-permute-start(f32[6,3,8,256]{3,2,1,0:T(8,128)S(1)} %slice_bitcast_fusion.1), channel_id=1, source_target_pairs={{0,1},{1,2},{2,3},{3,0},{4,5},{5,6},{6,7},{7,4},{8,9},{9,10},{10,1... | collective-permute-start | bytes 442376 | tf_op jit(solution)/shard_map/ppermute | solution.py:461
  27.3 7.6 %collective-permute-start.5 = (f32[4,3,8,256]{3,2,1,0:T(8,128)S(1)}, f32[4,3,8,256]{3,2,1,0:T(8,128)S(1)}, u32[]{:S(2)}, u32[]{:S(2)}) collective-permute-start(f32[4,3,8,256]{3,2,1,0:T(8,128)S(1)} %slice_bitcast_fusion.3), channel_id=1, source_target_pairs={{0,4},{1,5},{2,6},{3,7},{4,8},{5,9},{6,10},{7,11},{8,12},{9,13},{1... | collective-permute-start | bytes 294920 | tf_op jit(solution)/shard_map/ppermute | solution.py:461
  34.9 14.1 %copy-start.1 = (f32[1,2,512,512]{3,2,1,0:T(8,128)S(1)}, f32[1,2,512,512]{3,2,1,0:T(8,128)}, u32[]{:S(2)}) copy-start(f32[1,2,512,512]{3,2,1,0:T(8,128)} %param.15) | copy-start | bytes 6291460
  34.9 14.1 %copy-start.2 = (f32[1,1,2,128,512]{4,3,2,1,0:T(8,128)S(1)}, f32[1,1,2,128,512]{4,3,2,1,0:T(8,128)}, u32[]{:S(2)}) copy-start(f32[1,1,2,128,512]{4,3,2,1,0:T(8,128)} %param.14) | copy-start | bytes 1572868
  37.6 3.4 %collective-permute-start.12 = (f32[2,3,8,128]{3,2,1,0:T(8,128)S(1)}, f32[2,3,8,128]{3,2,1,0:T(8,128)S(1)}, u32[]{:S(2)}, u32[]{:S(2)}) collective-permute-start(f32[2,3,8,128]{3,2,1,0:T(8,128)S(1)} %get-tuple-element.121), channel_id=1, source_target_pairs={{0,128},{64,192},{128,0},{192,64},{1,129},{65,193},{129,1},{193,65... | collective-permute-start | bytes 73736 | tf_op jit(solution)/shard_map/ppermute | solution.py:491
  37.7 4.7 %collective-permute-start.13 = (f32[2,3,8,128]{3,2,1,0:T(8,128)S(1)}, f32[2,3,8,128]{3,2,1,0:T(8,128)S(1)}, u32[]{:S(2)}, u32[]{:S(2)}) collective-permute-start(f32[2,3,8,128]{3,2,1,0:T(8,128)S(1)} %get-tuple-element.122), channel_id=1, source_target_pairs={{0,192},{64,128},{128,64},{192,0},{1,193},{65,129},{129,65},{193,1... | collective-permute-start | bytes 73736 | tf_op jit(solution)/shard_map/ppermute | solution.py:492
  40.6 1.7 %collective-permute-start.11 = (f32[2,3,8,128]{3,2,1,0:T(8,128)S(1)}, f32[2,3,8,128]{3,2,1,0:T(8,128)S(1)}, u32[]{:S(2)}, u32[]{:S(2)}) collective-permute-start(f32[2,3,8,128]{3,2,1,0:T(8,128)S(1)} %get-tuple-element.122), channel_id=1, source_target_pairs={{0,64},{64,0},{128,192},{192,128},{1,65},{65,1},{129,193},{193,129... | collective-permute-start | bytes 73736 | tf_op jit(solution)/shard_map/ppermute | solution.py:490
  42.3 8.0 %collective-permute-start.16 = (f32[2,3,8,128]{3,2,1,0:T(8,128)S(1)}, f32[2,3,8,128]{3,2,1,0:T(8,128)S(1)}, u32[]{:S(2)}, u32[]{:S(2)}) collective-permute-start(f32[2,3,8,128]{3,2,1,0:T(8,128)S(1)} %add_add_fusion), channel_id=1, source_target_pairs={{0,12},{1,13},{2,14},{3,15},{4,0},{5,1},{6,2},{7,3},{8,4},{9,5},{1... | collective-permute-start | bytes 73736 | tf_op jit(solution)/shard_map/ppermute | solution.py:495
  42.7 7.6 %collective-permute-start.15 = (f32[2,3,8,128]{3,2,1,0:T(8,128)S(1)}, f32[2,3,8,128]{3,2,1,0:T(8,128)S(1)}, u32[]{:S(2)}, u32[]{:S(2)}) collective-permute-start(f32[2,3,8,128]{3,2,1,0:T(8,128)S(1)} %add_add_fusion), channel_id=1, source_target_pairs={{0,8},{1,9},{2,10},{3,11},{4,12},{5,13},{6,14},{7,15},{8,0},{9,1},... | collective-permute-start | bytes 73736 | tf_op jit(solution)/shard_map/ppermute | solution.py:495
  46.7 5.1 %collective-permute-start.14 = (f32[2,3,8,128]{3,2,1,0:T(8,128)S(1)}, f32[2,3,8,128]{3,2,1,0:T(8,128)S(1)}, u32[]{:S(2)}, u32[]{:S(2)}) collective-permute-start(f32[2,3,8,128]{3,2,1,0:T(8,128)S(1)} %add_add_fusion), channel_id=1, source_target_pairs={{0,4},{1,5},{2,6},{3,7},{4,8},{5,9},{6,10},{7,11},{8,12},{9,13},{1... | collective-permute-start | bytes 73736 | tf_op jit(solution)/shard_map/ppermute | solution.py:495
  51.8 5.2 %collective-permute-start.18 = (f32[4,2,3,8,128]{4,3,2,1,0:T(8,128)S(1)}, f32[4,2,3,8,128]{4,3,2,1,0:T(8,128)S(1)}, u32[]{:S(2)}, u32[]{:S(2)}) collective-permute-start(f32[4,2,3,8,128]{4,3,2,1,0:T(8,128)S(1)} %get-tuple-element.120), channel_id=1, source_target_pairs={{0,2},{1,3},{2,0},{3,1},{4,6},{5,7},{6,4},{7,5},{8,10},{9,11},{10,... | collective-permute-start | bytes 294920 | tf_op jit(solution)/shard_map/ppermute | solution.py:499
  51.9 5.8 %collective-permute-start.17 = (f32[4,2,3,8,128]{4,3,2,1,0:T(8,128)S(1)}, f32[4,2,3,8,128]{4,3,2,1,0:T(8,128)S(1)}, u32[]{:S(2)}, u32[]{:S(2)}) collective-permute-start(f32[4,2,3,8,128]{4,3,2,1,0:T(8,128)S(1)} %get-tuple-element.120), channel_id=1, source_target_pairs={{0,1},{1,2},{2,3},{3,0},{4,5},{5,6},{6,7},{7,4},{8,9},{9,10},{10,1... | collective-permute-start | bytes 294920 | tf_op jit(solution)/shard_map/ppermute | solution.py:499
  53.8 3.9 %collective-permute-start.19 = (f32[4,2,3,8,128]{4,3,2,1,0:T(8,128)S(1)}, f32[4,2,3,8,128]{4,3,2,1,0:T(8,128)S(1)}, u32[]{:S(2)}, u32[]{:S(2)}) collective-permute-start(f32[4,2,3,8,128]{4,3,2,1,0:T(8,128)S(1)} %get-tuple-element.120), channel_id=1, source_target_pairs={{0,3},{1,0},{2,1},{3,2},{4,7},{5,4},{6,5},{7,6},{8,11},{9,8},{10,9... | collective-permute-start | bytes 294920 | tf_op jit(solution)/shard_map/ppermute | solution.py:499
  57.8 6.5 %collective-permute-start.20 = (f32[4,4,2,3,8,128]{5,4,3,2,1,0:T(8,128)S(1)}, f32[4,4,2,3,8,128]{5,4,3,2,1,0:T(8,128)S(1)}, u32[]{:S(2)}, u32[]{:S(2)}) collective-permute-start(f32[4,4,2,3,8,128]{5,4,3,2,1,0:T(8,128)S(1)} %pad_maximum_fusion.mine), channel_id=1, source_target_pairs={{0,64},{64,0},{128,192},{192,128},{1,65},{65,1},{129,193},{193,129... | collective-permute-start | bytes 1179656 | tf_op jit(solution)/shard_map/ppermute | solution.py:500
  67.7 11.7 %collective-permute-start.21 = (f32[128,768]{1,0:T(8,128)S(1)}, f32[128,768]{1,0:T(8,128)S(1)}, u32[]{:S(2)}, u32[]{:S(2)}) collective-permute-start(f32[128,768]{1,0:T(8,128)S(1)} %get-tuple-element.110), channel_id=1, source_target_pairs={{0,16},{16,32},{32,48},{48,0},{1,17},{17,33},{33,49},{49,1},{2,18}... | collective-permute-start | bytes 1179656 | tf_op jit(solution)/shard_map/ppermute | solution.py:507
  69.0 10.4 %collective-permute-start.22 = (f32[128,768]{1,0:T(8,128)S(1)}, f32[128,768]{1,0:T(8,128)S(1)}, u32[]{:S(2)}, u32[]{:S(2)}) collective-permute-start(f32[128,768]{1,0:T(8,128)S(1)} %get-tuple-element.112), channel_id=1, source_target_pairs={{0,48},{16,0},{32,16},{48,32},{1,49},{17,1},{33,17},{49,33},{2,50}... | collective-permute-start | bytes 1179656 | tf_op jit(solution)/shard_map/ppermute | solution.py:510
  74.6 13.3 %collective-permute-start.24 = (f32[128,768]{1,0:T(8,128)S(1)}, f32[128,768]{1,0:T(8,128)S(1)}, u32[]{:S(2)}, u32[]{:S(2)}) collective-permute-start(f32[128,768]{1,0:T(8,128)S(1)} %get-tuple-element.114), channel_id=1, source_target_pairs={{0,16},{16,32},{32,48},{48,0},{1,17},{17,33},{33,49},{49,1},{2,18}... | collective-permute-start | bytes 1179656 | tf_op jit(solution)/shard_map/ppermute | solution.py:507
  74.7 13.2 %collective-permute-start.25 = (f32[128,768]{1,0:T(8,128)S(1)}, f32[128,768]{1,0:T(8,128)S(1)}, u32[]{:S(2)}, u32[]{:S(2)}) collective-permute-start(f32[128,768]{1,0:T(8,128)S(1)} %get-tuple-element.115), channel_id=1, source_target_pairs={{0,48},{16,0},{32,16},{48,32},{1,49},{17,1},{33,17},{49,33},{2,50}... | collective-permute-start | bytes 1179656 | tf_op jit(solution)/shard_map/ppermute | solution.py:510
  79.5 16.8 %collective-permute-start.23 = (f32[128,768]{1,0:T(8,128)S(1)}, f32[128,768]{1,0:T(8,128)S(1)}, u32[]{:S(2)}, u32[]{:S(2)}) collective-permute-start(f32[128,768]{1,0:T(8,128)S(1)} %get-tuple-element.113), channel_id=1, source_target_pairs={{0,16},{16,32},{32,48},{48,0},{1,17},{17,33},{33,49},{49,1},{2,18}... | collective-permute-start | bytes 1179656 | tf_op jit(solution)/shard_map/ppermute | solution.py:507
  80.5 15.8 %collective-permute-start.26 = (f32[128,768]{1,0:T(8,128)S(1)}, f32[128,768]{1,0:T(8,128)S(1)}, u32[]{:S(2)}, u32[]{:S(2)}) collective-permute-start(f32[128,768]{1,0:T(8,128)S(1)} %get-tuple-element.116), channel_id=1, source_target_pairs={{0,48},{16,0},{32,16},{48,32},{1,49},{17,1},{33,17},{49,33},{2,50}... | collective-permute-start | bytes 1179656 | tf_op jit(solution)/shard_map/ppermute | solution.py:510

commit v5 on v3

--- a/solution.py
+++ b/solution.py
@@ -474,12 +474,12 @@
 
     phase, turn = phases(momenta, directions)
     waves_own = wave_blocks(1, [bra], links, top)
-    ket_near, phase = lax.optimization_barrier((ket_near, phase))
+    ket_near, waves_own = lax.optimization_barrier((ket_near, waves_own))
     bra_near, waves_own = lax.optimization_barrier((bra_near, waves_own))
     ket_far = opposite(*ket_near, along_z)
     bra_far = opposite(*bra_near, along_x)
-
     waves_near = wave_blocks(2, bra_near, links, top)
+    waves_near, phase, turn = lax.optimization_barrier((waves_near, phase, turn))
     waves_far = wave_blocks(1, bra_far, links, top)
     waves = (*waves_own, *waves_near[:2], *waves_far, *waves_near[2:])
     kets = (own, ket_near[0], *ket_far, ket_near[1])

time: 96.1 us -> 96.1 us (level)
  local copies, waits for them, and re-layouts: 4.21 us -> 2.88 us
  waiting for transfers between devices: 28.2 us -> 29.5 us
    ppermute x1, starting transfers between devices: 4.67 us -> 6.17 us  [on_device(): lax.ppermute(blocks[1], 'space', [(i, i ^ 3) for i in range(4)])]
    ppermute x1, starting transfers between devices: 1.5 us -> 0.09 us  [on_device(): lax.ppermute(blocks[0], 'space', [(i, i ^ 2) for i in range(4)])]
    unnamed x17 -> x15, local copies, waits for them, and re-layouts: 3.25 us -> 1.92 us
    ppermute x2, waiting for transfers between devices: 0.99 us -> 2.08 us  [neighbours(): lax.ppermute(block, 'tsink', along(1))]
where the time goes in v5:
time: 96.1 us; the launch traced here: 95.9 us
  starting transfers between devices  45.4 us (47%)
  waiting for transfers between devices  29.5 us (31%)
  Pallas kernels  16.5 us (17%)
  local copies, waits for them, and re-layouts  2.88 us (3%)
  between operations  1.56 us (2%)
    ppermute x3, waiting for transfers between devices, up(): return lax.ppermute(value, 'tins', ring(4, 1))  16.1 us
    ppermute x2, starting transfers between devices, neighbours(): lax.ppermute(block, 'tsink', along(-1))  7.38 us
    ppermute x1, starting transfers between devices, on_device(): lax.ppermute(blocks[1], 'space', [(i, i ^ 3) for i in range(4)])  6.17 us
    ppermute x3, starting transfers between devices, down(): return lax.ppermute(value, 'tins', ring(4, -1))  5.94 us
    ppermute x2, starting transfers between devices, opposite(): lax.ppermute(ahead[1], 'tsink', along(-1))  5.81 us
    ppermute x1, starting transfers between devices, on_device(): others = lax.ppermute(summed, 'space', core_pairs)  4.87 us
    pallas_call x2, Pallas kernels, right_product(): pl.pallas_call(right_kernel, out_shape=(jax.ShapeDtypeStruct((128, 768),...  3.97 us
    ppermute x3, starting transfers between devices, on_device(): columns = [lax.ppermute(summed, 'tsink', along_z(d)) for d in (1, 2, 3)]  3.92 us
  transfers between devices with their start and end apart: 27, of which 12 were waited for; matrix products, arithmetic and copies ran while one was open for 1% of the time, Pallas kernels for 9%

profile of v5, /device:TPU:1, one launch (start us, length us, event | category | flops | bytes accessed | tf_op | source)
XLA Modules:
  0.0 95.9 jit_solution(12534765636313867312)
XLA Ops:
  0.0 1.0 %copy-done.4 = f32[1,2,3,8,4,256]{5,4,3,2,1,0:T(4,128)S(1)} copy-done((f32[1,2,3,8,4,256]{5,4,3,2,1,0:T(4,128)S(1)}, f32[1,2,3,8,4,256]{5,4,3,2,1,0:T(4,128)}, u32[]{:S(2)}) %copy-start.4) | copy-done | bytes 196632
  1.0 0.3 pack.1.refs_0_
  1.3 3.1 %collective-permute-start.2 = (f32[2,1,3,8,256]{4,3,2,1,0:T(8,128)S(1)}, f32[2,1,3,8,256]{4,3,2,1,0:T(8,128)S(1)}, u32[]{:S(2)}, u32[]{:S(2)}) collective-permute-start(f32[2,1,3,8,256]{4,3,2,1,0:T(8,128)S(1)} %get-tuple-element.123), channel_id=1, source_target_pairs={{0,64},{64,128},{128,192},{192,0},{1,65},{65,129},{129,193},{193,1... | collective-permute-start | bytes 147464 | tf_op jit(solution)/shard_map/ppermute | solution.py:468
  4.4 0.3 collective-permute-start.3
  4.7 4.8 %collective-permute-start.1 = (f32[2,4,3,8,256]{4,3,2,1,0:T(8,128)S(1)}, f32[2,4,3,8,256]{4,3,2,1,0:T(8,128)S(1)}, u32[]{:S(2)}, u32[]{:S(2)}) collective-permute-start(f32[2,4,3,8,256]{4,3,2,1,0:T(8,128)S(1)} %pack.1.refs_0_), channel_id=1, source_target_pairs={{0,12},{1,13},{2,14},{3,15},{4,0},{5,1},{6,2},{7,3},{8,4},{9,5},{1... | collective-permute-start | bytes 589832 | tf_op jit(solution)/shard_map/ppermute | solution.py:457
  9.5 0.0 collective-permute-start
  9.5 0.0 collective-permute-done.2
  9.5 0.0 collective-permute-done.3
  9.6 2.6 %collective-permute-start.8 = (f32[2,6,3,8,256]{4,3,2,1,0:T(8,128)S(1)}, f32[2,6,3,8,256]{4,3,2,1,0:T(8,128)S(1)}, u32[]{:S(2)}, u32[]{:S(2)}) collective-permute-start(f32[2,6,3,8,256]{4,3,2,1,0:T(8,128)S(1)} %pad_maximum_fusion.1.refs_0_), channel_id=1, source_target_pairs={{0,3},{1,0},{2,1},{3,2},{4,7},{5,4},{6,5},{7,6},{8,11},{9,8},{10,9... | collective-permute-start | bytes 884744 | tf_op jit(solution)/shard_map/ppermute | solution.py:457
  12.1 0.0 collective-permute-start.7
  12.1 0.9 slice.40
  13.1 2.4 %collective-permute-start.4 = (f32[18,256]{1,0:T(8,128)S(1)}, f32[18,256]{1,0:T(8,128)S(1)}, u32[]{:S(2)}, u32[]{:S(2)}) collective-permute-start(f32[18,256]{1,0:T(8,128)S(1)} %bitcast.47), channel_id=1, source_target_pairs={{0,64},{64,128},{128,192},{192,0},{1,65},{65,129},{129,193},{193,1... | collective-permute-start | bytes 55304 | tf_op jit(solution)/shard_map/ppermute | solution.py:473
  15.4 0.9 collective-permute-done.4.refs_2_.refs_3_
  16.4 0.9 copy-done
  17.3 0.7 waves.3
  18.1 0.0 collective-permute-done.1.refs_4_
  18.1 1.6 %collective-permute-done.refs_1_ = f32[2,4,3,8,256]{4,3,2,1,0:T(8,128)S(1)} collective-permute-done((f32[2,4,3,8,256]{4,3,2,1,0:T(8,128)S(1)}, f32[2,4,3,8,256]{4,3,2,1,0:T(8,128)S(1)}, u32[]{:S(2)}, u32[]{:S(2)}) %collective-permute-start) | collective-permute-done | bytes 196640 | tf_op jit(solution)/shard_map/ppermute | solution.py:457
  19.7 0.0 collective-permute-done.8.refs_1_
  19.7 0.4 collective-permute-done.7.refs_0_
  20.2 2.1 %collective-permute-start.10 = (f32[6,3,8,256]{3,2,1,0:T(8,128)S(1)}, f32[6,3,8,256]{3,2,1,0:T(8,128)S(1)}, u32[]{:S(2)}, u32[]{:S(2)}) collective-permute-start(f32[6,3,8,256]{3,2,1,0:T(8,128)S(1)} %slice_bitcast_fusion), channel_id=1, source_target_pairs={{0,3},{1,0},{2,1},{3,2},{4,7},{5,4},{6,5},{7,6},{8,11},{9,8},{10,9... | collective-permute-start | bytes 442376 | tf_op jit(solution)/shard_map/ppermute | solution.py:461
  22.3 0.0 collective-permute-start.9
  22.3 3.7 %collective-permute-start.6 = (f32[4,3,8,256]{3,2,1,0:T(8,128)S(1)}, f32[4,3,8,256]{3,2,1,0:T(8,128)S(1)}, u32[]{:S(2)}, u32[]{:S(2)}) collective-permute-start(f32[4,3,8,256]{3,2,1,0:T(8,128)S(1)} %slice_bitcast_fusion.2), channel_id=1, source_target_pairs={{0,12},{1,13},{2,14},{3,15},{4,0},{5,1},{6,2},{7,3},{8,4},{9,5},{1... | collective-permute-start | bytes 294920 | tf_op jit(solution)/shard_map/ppermute | solution.py:461
  26.0 0.0 collective-permute-start.5
  26.0 0.7 phases.1
  26.7 1.4 %waves.4 = (bf16[4,48,1536]{2,1,0:T(8,128)(2,1)S(1)}, bf16[4,48,1536]{2,1,0:T(8,128)(2,1)S(1)}, bf16[4,48,1536]{2,1,0:T(8,128)(2,1)S(1)}, bf16[4,48,1536]{2,1,0:T(8,128)(2,1)S(1)}) custom-call(f32[2,6,3,8,256]{4,3,2,1,0:T(8,128)S(1)} %collective-permute-done.7.refs_0_, f32[2,6,3,8,256]{4,3,2,1,0:T(8,128)S(1)} %collective-permute-done.8.refs_1_, ...), custom_call_target="tpu_custom_call" | custom-call | flops 20000000 | bytes 4000000 | tf_op jit(solution)/shard_map/waves/pallas_call | solution.py:176
  28.2 0.0 collective-permute-done.10.refs_1_
  28.2 0.0 collective-permute-done.9.refs_0_
  28.2 0.7 waves.5
  28.9 0.0 collective-permute-done.6.refs_3_
  28.9 3.1 %collective-permute-done.5.refs_2_ = f32[4,3,8,256]{3,2,1,0:T(8,128)S(1)} collective-permute-done((f32[4,3,8,256]{3,2,1,0:T(8,128)S(1)}, f32[4,3,8,256]{3,2,1,0:T(8,128)S(1)}, u32[]{:S(2)}, u32[]{:S(2)}) %collective-permute-start.5) | collective-permute-done | bytes 98336 | tf_op jit(solution)/shard_map/ppermute | solution.py:461
  32.1 2.6 %elementals.1 = f32[2,2,3,8,128]{4,3,2,1,0:T(8,128)S(1)} custom-call(s32[3]{0:T(128)S(1)} %copy-done.5, f32[2,4,3,8,256]{4,3,2,1,0:T(8,128)S(1)} %pack.1.refs_0_, f32[2,4,3,8,256]{4,3,2,1,0:T(8,128)S(1)} %collective-permute-done.refs_1_, f32[4,3,8,256]{3,2,1,0:T(8,128)S(1)} %collective-permute-done.5.refs_2_, ...), custom_call_target="tpu_custom_call" | custom-call | flops 1000000000 | bytes 3000000 | tf_op jit(solution)/shard_map/elementals/pallas_call | solution.py:239
  34.7 0.1 collective-permute-start.12
  34.8 6.2 %collective-permute-start.13 = (f32[2,3,8,128]{3,2,1,0:T(8,128)S(1)}, f32[2,3,8,128]{3,2,1,0:T(8,128)S(1)}, u32[]{:S(2)}, u32[]{:S(2)}) collective-permute-start(f32[2,3,8,128]{3,2,1,0:T(8,128)S(1)} %get-tuple-element.128), channel_id=1, source_target_pairs={{0,192},{64,128},{128,64},{192,0},{1,193},{65,129},{129,65},{193,1... | collective-permute-start | bytes 73736 | tf_op jit(solution)/shard_map/ppermute | solution.py:492
  41.0 1.8 %collective-permute-done.13 = f32[2,3,8,128]{3,2,1,0:T(8,128)S(1)} collective-permute-done((f32[2,3,8,128]{3,2,1,0:T(8,128)S(1)}, f32[2,3,8,128]{3,2,1,0:T(8,128)S(1)}, u32[]{:S(2)}, u32[]{:S(2)}) %collective-permute-start.13) | collective-permute-done | bytes 24608 | tf_op jit(solution)/shard_map/ppermute | solution.py:492
  42.8 0.0 collective-permute-done.11
  42.8 0.9 collective-permute-start.16
  43.7 0.7 collective-permute-start.15
  44.5 2.3 %collective-permute-start.14 = (f32[2,3,8,128]{3,2,1,0:T(8,128)S(1)}, f32[2,3,8,128]{3,2,1,0:T(8,128)S(1)}, u32[]{:S(2)}, u32[]{:S(2)}) collective-permute-start(f32[2,3,8,128]{3,2,1,0:T(8,128)S(1)} %add_add_fusion), channel_id=1, source_target_pairs={{0,4},{1,5},{2,6},{3,7},{4,8},{5,9},{6,10},{7,11},{8,12},{9,13},{1... | collective-permute-start | bytes 73736 | tf_op jit(solution)/shard_map/ppermute | solution.py:495
  48.0 1.3 %prepare.1 = (bf16[256,1024]{1,0:T(8,128)(2,1)S(1)}, bf16[256,1024]{1,0:T(8,128)(2,1)S(1)}, bf16[512,1024]{1,0:T(8,128)(2,1)S(1)}, bf16[512,1024]{1,0:T(8,128)(2...) custom-call(s32[1]{0:T(128)S(6)} %copy.19.ins_time, ...), custom_call_target="tpu_custom_call" | custom-call | flops 100000000 | bytes 8000000 | tf_op jit(solution)/shard_map/prepare/pallas_call | solution.py:323
  49.3 1.0 %collective-permute-done.15 = f32[2,3,8,128]{3,2,1,0:T(8,128)S(1)} collective-permute-done((f32[2,3,8,128]{3,2,1,0:T(8,128)S(1)}, f32[2,3,8,128]{3,2,1,0:T(8,128)S(1)}, u32[]{:S(2)}, u32[]{:S(2)}) %collective-permute-start.15) | collective-permute-done | bytes 24608 | tf_op jit(solution)/shard_map/ppermute | solution.py:495
  50.3 0.3 collective-permute-start.18
  50.6 1.6 %collective-permute-start.17 = (f32[4,2,3,8,128]{4,3,2,1,0:T(8,128)S(1)}, f32[4,2,3,8,128]{4,3,2,1,0:T(8,128)S(1)}, u32[]{:S(2)}, u32[]{:S(2)}) collective-permute-start(f32[4,2,3,8,128]{4,3,2,1,0:T(8,128)S(1)} %get-tuple-element.126), channel_id=1, source_target_pairs={{0,1},{1,2},{2,3},{3,0},{4,5},{5,6},{6,7},{7,4},{8,9},{9,10},{10,1... | collective-permute-start | bytes 294920 | tf_op jit(solution)/shard_map/ppermute | solution.py:499
  52.2 1.1 %collective-permute-start.19 = (f32[4,2,3,8,128]{4,3,2,1,0:T(8,128)S(1)}, f32[4,2,3,8,128]{4,3,2,1,0:T(8,128)S(1)}, u32[]{:S(2)}, u32[]{:S(2)}) collective-permute-start(f32[4,2,3,8,128]{4,3,2,1,0:T(8,128)S(1)} %get-tuple-element.126), channel_id=1, source_target_pairs={{0,3},{1,0},{2,1},{3,2},{4,7},{5,4},{6,5},{7,6},{8,11},{9,8},{10,9... | collective-permute-start | bytes 294920 | tf_op jit(solution)/shard_map/ppermute | solution.py:499
  53.3 2.2 %collective-permute-done.18 = f32[4,2,3,8,128]{4,3,2,1,0:T(8,128)S(1)} collective-permute-done((f32[4,2,3,8,128]{4,3,2,1,0:T(8,128)S(1)}, f32[4,2,3,8,128]{4,3,2,1,0:T(8,128)S(1)}, u32[]{:S(2)}, u32[]{:S(2)}) %collective-permute-start.18) | collective-permute-done | bytes 98336 | tf_op jit(solution)/shard_map/ppermute | solution.py:499
  55.5 0.8 collective-permute-done.17
  56.3 0.0 collective-permute-done.19
  56.4 4.9 %collective-permute-start.20 = (f32[4,4,2,3,8,128]{5,4,3,2,1,0:T(8,128)S(1)}, f32[4,4,2,3,8,128]{5,4,3,2,1,0:T(8,128)S(1)}, u32[]{:S(2)}, u32[]{:S(2)}) collective-permute-start(f32[4,4,2,3,8,128]{5,4,3,2,1,0:T(8,128)S(1)} %pad_maximum_fusion.mine), channel_id=1, source_target_pairs={{0,64},{64,0},{128,192},{192,128},{1,65},{65,1},{129,193},{193,129... | collective-permute-start | bytes 1179656 | tf_op jit(solution)/shard_map/ppermute | solution.py:500
  61.2 1.3 %collective-permute-done.20.others = f32[4,4,2,3,8,128]{5,4,3,2,1,0:T(8,128)S(1)} collective-permute-done((f32[4,4,2,3,8,128]{5,4,3,2,1,0:T(8,128)S(1)}, f32[4,4,2,3,8,128]{5,4,3,2,1,0:T(8,128)S(1)}, u32[]{:S(2)}, u32[]{:S(2)}) %collective-permute-start.20) | collective-permute-done | bytes 393248 | tf_op jit(solution)/shard_map/ppermute | solution.py:500
  62.6 3.3 %left.1 = (bf16[1024,768]{1,0:T(8,128)(2,1)S(1)}, bf16[1024,768]{1,0:T(8,128)(2,1)S(1)}, f32[128,768]{1,0:T(8,128)S(1)}, f32[128,768]{1,0:T(8,128)S(1)}) custom-call(f32[4,4,2,3,8,128]{5,4,3,2,1,0:T(8,128)S(1)} %pad_maximum_fusion.mine, f32[4,4,2,3,8,128]{5,4,3,2,1,0:T(8,128)S(1)} %collective-permute-done.20.others, ...), custom_call_target="tpu_custom_call" | custom-call | flops 1000000000 | bytes 4000000 | tf_op jit(solution)/shard_map/left/pallas_call | solution.py:374
  65.9 1.4 %collective-permute-start.21 = (f32[128,768]{1,0:T(8,128)S(1)}, f32[128,768]{1,0:T(8,128)S(1)}, u32[]{:S(2)}, u32[]{:S(2)}) collective-permute-start(f32[128,768]{1,0:T(8,128)S(1)} %get-tuple-element.116), channel_id=1, source_target_pairs={{0,16},{16,32},{32,48},{48,0},{1,17},{17,33},{33,49},{49,1},{2,18}... | collective-permute-start | bytes 1179656 | tf_op jit(solution)/shard_map/ppermute | solution.py:507
  67.3 1.5 %collective-permute-start.22 = (f32[128,768]{1,0:T(8,128)S(1)}, f32[128,768]{1,0:T(8,128)S(1)}, u32[]{:S(2)}, u32[]{:S(2)}) collective-permute-start(f32[128,768]{1,0:T(8,128)S(1)} %get-tuple-element.118), channel_id=1, source_target_pairs={{0,48},{16,0},{32,16},{48,32},{1,49},{17,1},{33,17},{49,33},{2,50}... | collective-permute-start | bytes 1179656 | tf_op jit(solution)/shard_map/ppermute | solution.py:510
  68.8 2.6 %right.2 = (f32[128,768]{1,0:T(8,128)S(1)}, f32[128,768]{1,0:T(8,128)S(1)}, f32[128,768]{1,0:T(8,128)S(1)}, f32[128,768]{1,0:T(8,128)S(1)}) custom-call(bf16[512,1024]{1,0:T(8,128)(2,1)S(1)} %get-tuple-element.96.src_hi, bf16[512,1024]{1,0:T(8,128)(2,1)S(1)} %get-tuple-element.97.src_lo, bf16[1024,768]{1,0:T(8,128)(2,1)S(1)} %get-tuple-element.105.left_hi, ...), custom_call_target="tpu_custom_call" | custom-call | flops 1000000000 | bytes 5000000 | tf_op jit(solution)/shard_map/right/pallas_call | solution.py:397
  71.4 1.4 %right.3 = (f32[128,768]{1,0:T(8,128)S(1)}, f32[128,768]{1,0:T(8,128)S(1)}) custom-call(bf16[256,1024]{1,0:T(8,128)(2,1)S(1)} %get-tuple-element.109.src_hi, bf16[256,1024]{1,0:T(8,128)(2,1)S(1)} %get-tuple-element.110.src_lo, bf16[1024,768]{1,0:T(8,128)(2,1)S(1)} %get-tuple-element.105.left_hi, bf16[1024,768]{1,0:T(8,128)(2,1)S(1)} %get-tuple-element.106.left_lo), custom_call_target="tpu_custom_call" | custom-call | flops 1000000000 | bytes 5000000 | tf_op jit(solution)/shard_map/right/pallas_call | solution.py:397
  72.8 0.1 collective-permute-start.24
  72.9 2.7 %collective-permute-start.25 = (f32[128,768]{1,0:T(8,128)S(1)}, f32[128,768]{1,0:T(8,128)S(1)}, u32[]{:S(2)}, u32[]{:S(2)}) collective-permute-start(f32[128,768]{1,0:T(8,128)S(1)} %get-tuple-element.121), channel_id=1, source_target_pairs={{0,48},{16,0},{32,16},{48,32},{1,49},{17,1},{33,17},{49,33},{2,50}... | collective-permute-start | bytes 1179656 | tf_op jit(solution)/shard_map/ppermute | solution.py:510
  75.6 2.1 %collective-permute-done.21.second = f32[128,768]{1,0:T(8,128)S(1)} collective-permute-done((f32[128,768]{1,0:T(8,128)S(1)}, f32[128,768]{1,0:T(8,128)S(1)}, u32[]{:S(2)}, u32[]{:S(2)}) %collective-permute-start.21) | collective-permute-done | bytes 393248 | tf_op jit(solution)/shard_map/ppermute | solution.py:507
  77.7 0.0 collective-permute-done.22.fourth
  77.7 0.1 relay.1
  77.8 1.0 %collective-permute-start.23 = (f32[128,768]{1,0:T(8,128)S(1)}, f32[128,768]{1,0:T(8,128)S(1)}, u32[]{:S(2)}, u32[]{:S(2)}) collective-permute-start(f32[128,768]{1,0:T(8,128)S(1)} %get-tuple-element.119), channel_id=1, source_target_pairs={{0,16},{16,32},{32,48},{48,0},{1,17},{17,33},{33,49},{49,1},{2,18}... | collective-permute-start | bytes 1179656 | tf_op jit(solution)/shard_map/ppermute | solution.py:507
  78.8 1.8 %collective-permute-start.26 = (f32[128,768]{1,0:T(8,128)S(1)}, f32[128,768]{1,0:T(8,128)S(1)}, u32[]{:S(2)}, u32[]{:S(2)}) collective-permute-start(f32[128,768]{1,0:T(8,128)S(1)} %get-tuple-element.122), channel_id=1, source_target_pairs={{0,48},{16,0},{32,16},{48,32},{1,49},{17,1},{33,17},{49,33},{2,50}... | collective-permute-start | bytes 1179656 | tf_op jit(solution)/shard_map/ppermute | solution.py:510
  80.5 5.6 %collective-permute-done.24.refs_3_ = f32[128,768]{1,0:T(8,128)S(1)} collective-permute-done((f32[128,768]{1,0:T(8,128)S(1)}, f32[128,768]{1,0:T(8,128)S(1)}, u32[]{:S(2)}, u32[]{:S(2)}) %collective-permute-start.24) | collective-permute-done | bytes 393248 | tf_op jit(solution)/shard_map/ppermute | solution.py:507
  86.1 8.4 %collective-permute-done.23.refs_2_ = f32[128,768]{1,0:T(8,128)S(1)} collective-permute-done((f32[128,768]{1,0:T(8,128)S(1)}, f32[128,768]{1,0:T(8,128)S(1)}, u32[]{:S(2)}, u32[]{:S(2)}) %collective-permute-start.23) | collective-permute-done | bytes 393248 | tf_op jit(solution)/shard_map/ppermute | solution.py:507
  94.5 0.0 collective-permute-done.26.refs_5_
  94.5 1.4 %final.1 = f32[128,6,2,128]{3,2,1,0:T(2,128)} custom-call(f32[128,768]{1,0:T(8,128)S(1)} %get-tuple-element.113.refs_0_, f32[128,768]{1,0:T(8,128)S(1)} %get-tuple-element.114.refs_1_, f32[128,768]{1,0:T(8,128)S(1)} %collective-permute-done.23.refs_2_, f32[128,768]{1,0:T(8,128)S(1)} %collective-permute-done.24.refs_3_, ...), custom_call_target="tpu_custom_call" | custom-call | tf_op jit(solution)/shard_map/final/pallas_call | solution.py:434
  (28 shorter events, 0.2 us)
Async XLA Ops:
  0.0 26.7 %copy-start.1 = (f32[1,3,2,3,3,4,256]{6,5,4,3,2,1,0:T(4,128)S(1)}, f32[1,3,2,3,3,4,256]{6,5,4,3,2,1,0:T(4,128)}, u32[]{:S(2)}) copy-start(f32[1,3,2,3,3,4,256]{6,5,4,3,2,1,0:T(4,128)} %param.9) | copy-start | bytes 663556
  0.0 1.0 %copy-start.4 = (f32[1,2,3,8,4,256]{5,4,3,2,1,0:T(4,128)S(1)}, f32[1,2,3,8,4,256]{5,4,3,2,1,0:T(4,128)}, u32[]{:S(2)}) copy-start(f32[1,2,3,8,4,256]{5,4,3,2,1,0:T(4,128)} %param.8) | copy-start | bytes 589828
  1.0 25.1 %copy-start.5 = (s32[3]{0:T(128)S(1)}, s32[3]{0:T(128)}, u32[]{:S(2)}) copy-start(s32[3]{0:T(128)} %directions.3) | copy-start | bytes 40
  1.0 25.1 %copy-start.6 = (s32[2,3]{1,0:T(2,128)S(1)}, s32[2,3]{1,0:T(2,128)}, u32[]{:S(2)}) copy-start(s32[2,3]{1,0:T(2,128)} %momenta.1) | copy-start | bytes 76
  1.3 8.2 %collective-permute-start.2 = (f32[2,1,3,8,256]{4,3,2,1,0:T(8,128)S(1)}, f32[2,1,3,8,256]{4,3,2,1,0:T(8,128)S(1)}, u32[]{:S(2)}, u32[]{:S(2)}) collective-permute-start(f32[2,1,3,8,256]{4,3,2,1,0:T(8,128)S(1)} %get-tuple-element.123), channel_id=1, source_target_pairs={{0,64},{64,128},{128,192},{192,0},{1,65},{65,129},{129,193},{193,1... | collective-permute-start | bytes 147464 | tf_op jit(solution)/shard_map/ppermute | solution.py:468
  4.4 5.1 %collective-permute-start.3 = (f32[2,1,3,8,256]{4,3,2,1,0:T(8,128)S(1)}, f32[2,1,3,8,256]{4,3,2,1,0:T(8,128)S(1)}, u32[]{:S(2)}, u32[]{:S(2)}) collective-permute-start(f32[2,1,3,8,256]{4,3,2,1,0:T(8,128)S(1)} %get-tuple-element.124), channel_id=1, source_target_pairs={{0,192},{64,0},{128,64},{192,128},{1,193},{65,1},{129,65},{193,129... | collective-permute-start | bytes 147464 | tf_op jit(solution)/shard_map/ppermute | solution.py:469
  4.7 13.3 %collective-permute-start.1 = (f32[2,4,3,8,256]{4,3,2,1,0:T(8,128)S(1)}, f32[2,4,3,8,256]{4,3,2,1,0:T(8,128)S(1)}, u32[]{:S(2)}, u32[]{:S(2)}) collective-permute-start(f32[2,4,3,8,256]{4,3,2,1,0:T(8,128)S(1)} %pack.1.refs_0_), channel_id=1, source_target_pairs={{0,12},{1,13},{2,14},{3,15},{4,0},{5,1},{6,2},{7,3},{8,4},{9,5},{1... | collective-permute-start | bytes 589832 | tf_op jit(solution)/shard_map/ppermute | solution.py:457
  9.5 10.2 %collective-permute-start = (f32[2,4,3,8,256]{4,3,2,1,0:T(8,128)S(1)}, f32[2,4,3,8,256]{4,3,2,1,0:T(8,128)S(1)}, u32[]{:S(2)}, u32[]{:S(2)}) collective-permute-start(f32[2,4,3,8,256]{4,3,2,1,0:T(8,128)S(1)} %pack.1.refs_0_), channel_id=1, source_target_pairs={{0,4},{1,5},{2,6},{3,7},{4,8},{5,9},{6,10},{7,11},{8,12},{9,13},{1... | collective-permute-start | bytes 589832 | tf_op jit(solution)/shard_map/ppermute | solution.py:457
  9.6 10.1 %collective-permute-start.8 = (f32[2,6,3,8,256]{4,3,2,1,0:T(8,128)S(1)}, f32[2,6,3,8,256]{4,3,2,1,0:T(8,128)S(1)}, u32[]{:S(2)}, u32[]{:S(2)}) collective-permute-start(f32[2,6,3,8,256]{4,3,2,1,0:T(8,128)S(1)} %pad_maximum_fusion.1.refs_0_), channel_id=1, source_target_pairs={{0,3},{1,0},{2,1},{3,2},{4,7},{5,4},{6,5},{7,6},{8,11},{9,8},{10,9... | collective-permute-start | bytes 884744 | tf_op jit(solution)/shard_map/ppermute | solution.py:457
  12.1 8.0 %collective-permute-start.7 = (f32[2,6,3,8,256]{4,3,2,1,0:T(8,128)S(1)}, f32[2,6,3,8,256]{4,3,2,1,0:T(8,128)S(1)}, u32[]{:S(2)}, u32[]{:S(2)}) collective-permute-start(f32[2,6,3,8,256]{4,3,2,1,0:T(8,128)S(1)} %pad_maximum_fusion.1.refs_0_), channel_id=1, source_target_pairs={{0,1},{1,2},{2,3},{3,0},{4,5},{5,6},{6,7},{7,4},{8,9},{9,10},{10,1... | collective-permute-start | bytes 884744 | tf_op jit(solution)/shard_map/ppermute | solution.py:457
  13.1 3.3 %collective-permute-start.4 = (f32[18,256]{1,0:T(8,128)S(1)}, f32[18,256]{1,0:T(8,128)S(1)}, u32[]{:S(2)}, u32[]{:S(2)}) collective-permute-start(f32[18,256]{1,0:T(8,128)S(1)} %bitcast.47), channel_id=1, source_target_pairs={{0,64},{64,128},{128,192},{192,0},{1,65},{65,129},{129,193},{193,1... | collective-permute-start | bytes 55304 | tf_op jit(solution)/shard_map/ppermute | solution.py:473
  16.4 0.9 copy-start
  20.2 8.0 %collective-permute-start.10 = (f32[6,3,8,256]{3,2,1,0:T(8,128)S(1)}, f32[6,3,8,256]{3,2,1,0:T(8,128)S(1)}, u32[]{:S(2)}, u32[]{:S(2)}) collective-permute-start(f32[6,3,8,256]{3,2,1,0:T(8,128)S(1)} %slice_bitcast_fusion), channel_id=1, source_target_pairs={{0,3},{1,0},{2,1},{3,2},{4,7},{5,4},{6,5},{7,6},{8,11},{9,8},{10,9... | collective-permute-start | bytes 442376 | tf_op jit(solution)/shard_map/ppermute | solution.py:461
  22.3 5.8 %collective-permute-start.9 = (f32[6,3,8,256]{3,2,1,0:T(8,128)S(1)}, f32[6,3,8,256]{3,2,1,0:T(8,128)S(1)}, u32[]{:S(2)}, u32[]{:S(2)}) collective-permute-start(f32[6,3,8,256]{3,2,1,0:T(8,128)S(1)} %slice_bitcast_fusion.1), channel_id=1, source_target_pairs={{0,1},{1,2},{2,3},{3,0},{4,5},{5,6},{6,7},{7,4},{8,9},{9,10},{10,1... | collective-permute-start | bytes 442376 | tf_op jit(solution)/shard_map/ppermute | solution.py:461
  22.3 6.6 %collective-permute-start.6 = (f32[4,3,8,256]{3,2,1,0:T(8,128)S(1)}, f32[4,3,8,256]{3,2,1,0:T(8,128)S(1)}, u32[]{:S(2)}, u32[]{:S(2)}) collective-permute-start(f32[4,3,8,256]{3,2,1,0:T(8,128)S(1)} %slice_bitcast_fusion.2), channel_id=1, source_target_pairs={{0,12},{1,13},{2,14},{3,15},{4,0},{5,1},{6,2},{7,3},{8,4},{9,5},{1... | collective-permute-start | bytes 294920 | tf_op jit(solution)/shard_map/ppermute | solution.py:461
  26.0 6.0 %collective-permute-start.5 = (f32[4,3,8,256]{3,2,1,0:T(8,128)S(1)}, f32[4,3,8,256]{3,2,1,0:T(8,128)S(1)}, u32[]{:S(2)}, u32[]{:S(2)}) collective-permute-start(f32[4,3,8,256]{3,2,1,0:T(8,128)S(1)} %slice_bitcast_fusion.3), channel_id=1, source_target_pairs={{0,4},{1,5},{2,6},{3,7},{4,8},{5,9},{6,10},{7,11},{8,12},{9,13},{1... | collective-permute-start | bytes 294920 | tf_op jit(solution)/shard_map/ppermute | solution.py:461
  32.1 16.0 %copy-start.2 = (f32[1,2,512,512]{3,2,1,0:T(8,128)S(1)}, f32[1,2,512,512]{3,2,1,0:T(8,128)}, u32[]{:S(2)}) copy-start(f32[1,2,512,512]{3,2,1,0:T(8,128)} %param.15) | copy-start | bytes 6291460
  32.1 16.0 %copy-start.3 = (f32[1,1,2,128,512]{4,3,2,1,0:T(8,128)S(1)}, f32[1,1,2,128,512]{4,3,2,1,0:T(8,128)}, u32[]{:S(2)}) copy-start(f32[1,1,2,128,512]{4,3,2,1,0:T(8,128)} %param.14) | copy-start | bytes 1572868
  34.7 6.3 %collective-permute-start.12 = (f32[2,3,8,128]{3,2,1,0:T(8,128)S(1)}, f32[2,3,8,128]{3,2,1,0:T(8,128)S(1)}, u32[]{:S(2)}, u32[]{:S(2)}) collective-permute-start(f32[2,3,8,128]{3,2,1,0:T(8,128)S(1)} %get-tuple-element.127), channel_id=1, source_target_pairs={{0,128},{64,192},{128,0},{192,64},{1,129},{65,193},{129,1},{193,65... | collective-permute-start | bytes 73736 | tf_op jit(solution)/shard_map/ppermute | solution.py:491
  34.8 8.0 %collective-permute-start.13 = (f32[2,3,8,128]{3,2,1,0:T(8,128)S(1)}, f32[2,3,8,128]{3,2,1,0:T(8,128)S(1)}, u32[]{:S(2)}, u32[]{:S(2)}) collective-permute-start(f32[2,3,8,128]{3,2,1,0:T(8,128)S(1)} %get-tuple-element.128), channel_id=1, source_target_pairs={{0,192},{64,128},{128,64},{192,0},{1,193},{65,129},{129,65},{193,1... | collective-permute-start | bytes 73736 | tf_op jit(solution)/shard_map/ppermute | solution.py:492
  41.0 1.8 %collective-permute-start.11 = (f32[2,3,8,128]{3,2,1,0:T(8,128)S(1)}, f32[2,3,8,128]{3,2,1,0:T(8,128)S(1)}, u32[]{:S(2)}, u32[]{:S(2)}) collective-permute-start(f32[2,3,8,128]{3,2,1,0:T(8,128)S(1)} %get-tuple-element.128), channel_id=1, source_target_pairs={{0,64},{64,0},{128,192},{192,128},{1,65},{65,1},{129,193},{193,129... | collective-permute-start | bytes 73736 | tf_op jit(solution)/shard_map/ppermute | solution.py:490
  42.8 6.5 %collective-permute-start.16 = (f32[2,3,8,128]{3,2,1,0:T(8,128)S(1)}, f32[2,3,8,128]{3,2,1,0:T(8,128)S(1)}, u32[]{:S(2)}, u32[]{:S(2)}) collective-permute-start(f32[2,3,8,128]{3,2,1,0:T(8,128)S(1)} %add_add_fusion), channel_id=1, source_target_pairs={{0,12},{1,13},{2,14},{3,15},{4,0},{5,1},{6,2},{7,3},{8,4},{9,5},{1... | collective-permute-start | bytes 73736 | tf_op jit(solution)/shard_map/ppermute | solution.py:495
  43.7 6.6 %collective-permute-start.15 = (f32[2,3,8,128]{3,2,1,0:T(8,128)S(1)}, f32[2,3,8,128]{3,2,1,0:T(8,128)S(1)}, u32[]{:S(2)}, u32[]{:S(2)}) collective-permute-start(f32[2,3,8,128]{3,2,1,0:T(8,128)S(1)} %add_add_fusion), channel_id=1, source_target_pairs={{0,8},{1,9},{2,10},{3,11},{4,12},{5,13},{6,14},{7,15},{8,0},{9,1},... | collective-permute-start | bytes 73736 | tf_op jit(solution)/shard_map/ppermute | solution.py:495
  44.5 5.9 %collective-permute-start.14 = (f32[2,3,8,128]{3,2,1,0:T(8,128)S(1)}, f32[2,3,8,128]{3,2,1,0:T(8,128)S(1)}, u32[]{:S(2)}, u32[]{:S(2)}) collective-permute-start(f32[2,3,8,128]{3,2,1,0:T(8,128)S(1)} %add_add_fusion), channel_id=1, source_target_pairs={{0,4},{1,5},{2,6},{3,7},{4,8},{5,9},{6,10},{7,11},{8,12},{9,13},{1... | collective-permute-start | bytes 73736 | tf_op jit(solution)/shard_map/ppermute | solution.py:495
  50.3 5.2 %collective-permute-start.18 = (f32[4,2,3,8,128]{4,3,2,1,0:T(8,128)S(1)}, f32[4,2,3,8,128]{4,3,2,1,0:T(8,128)S(1)}, u32[]{:S(2)}, u32[]{:S(2)}) collective-permute-start(f32[4,2,3,8,128]{4,3,2,1,0:T(8,128)S(1)} %get-tuple-element.126), channel_id=1, source_target_pairs={{0,2},{1,3},{2,0},{3,1},{4,6},{5,7},{6,4},{7,5},{8,10},{9,11},{10,... | collective-permute-start | bytes 294920 | tf_op jit(solution)/shard_map/ppermute | solution.py:499
  50.6 5.7 %collective-permute-start.17 = (f32[4,2,3,8,128]{4,3,2,1,0:T(8,128)S(1)}, f32[4,2,3,8,128]{4,3,2,1,0:T(8,128)S(1)}, u32[]{:S(2)}, u32[]{:S(2)}) collective-permute-start(f32[4,2,3,8,128]{4,3,2,1,0:T(8,128)S(1)} %get-tuple-element.126), channel_id=1, source_target_pairs={{0,1},{1,2},{2,3},{3,0},{4,5},{5,6},{6,7},{7,4},{8,9},{9,10},{10,1... | collective-permute-start | bytes 294920 | tf_op jit(solution)/shard_map/ppermute | solution.py:499
  52.2 4.2 %collective-permute-start.19 = (f32[4,2,3,8,128]{4,3,2,1,0:T(8,128)S(1)}, f32[4,2,3,8,128]{4,3,2,1,0:T(8,128)S(1)}, u32[]{:S(2)}, u32[]{:S(2)}) collective-permute-start(f32[4,2,3,8,128]{4,3,2,1,0:T(8,128)S(1)} %get-tuple-element.126), channel_id=1, source_target_pairs={{0,3},{1,0},{2,1},{3,2},{4,7},{5,4},{6,5},{7,6},{8,11},{9,8},{10,9... | collective-permute-start | bytes 294920 | tf_op jit(solution)/shard_map/ppermute | solution.py:499
  56.4 6.2 %collective-permute-start.20 = (f32[4,4,2,3,8,128]{5,4,3,2,1,0:T(8,128)S(1)}, f32[4,4,2,3,8,128]{5,4,3,2,1,0:T(8,128)S(1)}, u32[]{:S(2)}, u32[]{:S(2)}) collective-permute-start(f32[4,4,2,3,8,128]{5,4,3,2,1,0:T(8,128)S(1)} %pad_maximum_fusion.mine), channel_id=1, source_target_pairs={{0,64},{64,0},{128,192},{192,128},{1,65},{65,1},{129,193},{193,129... | collective-permute-start | bytes 1179656 | tf_op jit(solution)/shard_map/ppermute | solution.py:500
  65.9 11.7 %collective-permute-start.21 = (f32[128,768]{1,0:T(8,128)S(1)}, f32[128,768]{1,0:T(8,128)S(1)}, u32[]{:S(2)}, u32[]{:S(2)}) collective-permute-start(f32[128,768]{1,0:T(8,128)S(1)} %get-tuple-element.116), channel_id=1, source_target_pairs={{0,16},{16,32},{32,48},{48,0},{1,17},{17,33},{33,49},{49,1},{2,18}... | collective-permute-start | bytes 1179656 | tf_op jit(solution)/shard_map/ppermute | solution.py:507
  67.3 10.4 %collective-permute-start.22 = (f32[128,768]{1,0:T(8,128)S(1)}, f32[128,768]{1,0:T(8,128)S(1)}, u32[]{:S(2)}, u32[]{:S(2)}) collective-permute-start(f32[128,768]{1,0:T(8,128)S(1)} %get-tuple-element.118), channel_id=1, source_target_pairs={{0,48},{16,0},{32,16},{48,32},{1,49},{17,1},{33,17},{49,33},{2,50}... | collective-permute-start | bytes 1179656 | tf_op jit(solution)/shard_map/ppermute | solution.py:510
  72.8 13.3 %collective-permute-start.24 = (f32[128,768]{1,0:T(8,128)S(1)}, f32[128,768]{1,0:T(8,128)S(1)}, u32[]{:S(2)}, u32[]{:S(2)}) collective-permute-start(f32[128,768]{1,0:T(8,128)S(1)} %get-tuple-element.120), channel_id=1, source_target_pairs={{0,16},{16,32},{32,48},{48,0},{1,17},{17,33},{33,49},{49,1},{2,18}... | collective-permute-start | bytes 1179656 | tf_op jit(solution)/shard_map/ppermute | solution.py:507
  72.9 13.2 %collective-permute-start.25 = (f32[128,768]{1,0:T(8,128)S(1)}, f32[128,768]{1,0:T(8,128)S(1)}, u32[]{:S(2)}, u32[]{:S(2)}) collective-permute-start(f32[128,768]{1,0:T(8,128)S(1)} %get-tuple-element.121), channel_id=1, source_target_pairs={{0,48},{16,0},{32,16},{48,32},{1,49},{17,1},{33,17},{49,33},{2,50}... | collective-permute-start | bytes 1179656 | tf_op jit(solution)/shard_map/ppermute | solution.py:510
  77.8 16.8 %collective-permute-start.23 = (f32[128,768]{1,0:T(8,128)S(1)}, f32[128,768]{1,0:T(8,128)S(1)}, u32[]{:S(2)}, u32[]{:S(2)}) collective-permute-start(f32[128,768]{1,0:T(8,128)S(1)} %get-tuple-element.119), channel_id=1, source_target_pairs={{0,16},{16,32},{32,48},{48,0},{1,17},{17,33},{33,49},{49,1},{2,18}... | collective-permute-start | bytes 1179656 | tf_op jit(solution)/shard_map/ppermute | solution.py:507
  78.8 15.8 %collective-permute-start.26 = (f32[128,768]{1,0:T(8,128)S(1)}, f32[128,768]{1,0:T(8,128)S(1)}, u32[]{:S(2)}, u32[]{:S(2)}) collective-permute-start(f32[128,768]{1,0:T(8,128)S(1)} %get-tuple-element.122), channel_id=1, source_target_pairs={{0,48},{16,0},{32,16},{48,32},{1,49},{17,1},{33,17},{49,33},{2,50}... | collective-permute-start | bytes 1179656 | tf_op jit(solution)/shard_map/ppermute | solution.py:510

commit v6 on v5

--- a/solution.py
+++ b/solution.py
@@ -405,18 +405,17 @@
     )(src_hi, src_lo, left_hi, left_lo)
 
 
-def relay_kernel(first, second, third, fourth, out_one, out_two):
-    out_one[...] = first[...] + second[...]
-    out_two[...] = third[...] + fourth[...]
-
-
-def relay_sums(*terms):
+def relay_kernel(first, second, out):
+    out[...] = first[...] + second[...]
+
+
+def relay_sum(*terms):
     shape = jax.ShapeDtypeStruct((128, 768), F32)
     return pl.pallas_call(
         relay_kernel,
-        out_shape=(shape, shape),
-        in_specs=[VMEM] * 4,
-        out_specs=(VMEM,) * 2,
+        out_shape=shape,
+        in_specs=[VMEM] * 2,
+        out_specs=VMEM,
         compiler_params=params(8),
         name="relay",
     )(*terms)
@@ -514,8 +513,8 @@
     own_re, own_im = right_product(own_hi, own_lo, left_hi, left_lo)
     next_im, prev_re, own_re, own_im = lax.optimization_barrier((next_im, prev_re, own_re, own_im))
     below_im, above_re = up(next_im), down(prev_re)
-    next_re, prev_im = relay_sums(next_re, from_below, prev_im, from_above)
-    below_re, above_im = up(next_re), down(prev_im)
+    below_re = up(relay_sum(next_re, from_below))
+    above_im = down(relay_sum(prev_im, from_above))
     return final_sum(own_re, own_im, below_re, below_im, above_re, above_im)[:, None]
 
 

time: 96.1 us -> 96.1 us (level)
    ppermute x3, starting transfers between devices: 5.94 us -> 6.92 us  [down(): return lax.ppermute(value, 'tins', ring(4, -1))]
where the time goes in v6:
time: 96.1 us; the launch traced here: 95.9 us
  starting transfers between devices  45.4 us (47%)
  waiting for transfers between devices  29.4 us (31%)
  Pallas kernels  16.5 us (17%)
  local copies, waits for them, and re-layouts  2.88 us (3%)
  between operations  1.58 us (2%)
    ppermute x3, waiting for transfers between devices, up(): return lax.ppermute(value, 'tins', ring(4, 1))  16 us
    ppermute x2, starting transfers between devices, neighbours(): lax.ppermute(block, 'tsink', along(-1))  7.38 us
    ppermute x3, starting transfers between devices, down(): return lax.ppermute(value, 'tins', ring(4, -1))  6.92 us
    ppermute x1, starting transfers between devices, on_device(): lax.ppermute(blocks[1], 'space', [(i, i ^ 3) for i in range(4)])  6.17 us
    ppermute x2, starting transfers between devices, opposite(): lax.ppermute(ahead[1], 'tsink', along(-1))  5.81 us
    ppermute x1, starting transfers between devices, on_device(): others = lax.ppermute(summed, 'space', core_pairs)  4.87 us
    pallas_call x2, Pallas kernels, right_product(): pl.pallas_call(right_kernel, out_shape=(jax.ShapeDtypeStruct((128, 768),...  3.97 us
    ppermute x3, starting transfers between devices, on_device(): columns = [lax.ppermute(summed, 'tsink', along_z(d)) for d in (1, 2, 3)]  3.92 us
  transfers between devices with their start and end apart: 27, of which 12 were waited for; matrix products, arithmetic and copies ran while one was open for 1% of the time, Pallas kernels for 9%

profile of v6, /device:TPU:1, one launch (start us, length us, event | category | flops | bytes accessed | tf_op | source)
XLA Modules:
  0.0 95.9 jit_solution(435275543838307468)
XLA Ops:
  0.0 1.0 %copy-done.4 = f32[1,2,3,8,4,256]{5,4,3,2,1,0:T(4,128)S(1)} copy-done((f32[1,2,3,8,4,256]{5,4,3,2,1,0:T(4,128)S(1)}, f32[1,2,3,8,4,256]{5,4,3,2,1,0:T(4,128)}, u32[]{:S(2)}) %copy-start.4) | copy-done | bytes 196632
  1.0 0.3 pack.1.refs_0_
  1.3 3.1 %collective-permute-start.2 = (f32[2,1,3,8,256]{4,3,2,1,0:T(8,128)S(1)}, f32[2,1,3,8,256]{4,3,2,1,0:T(8,128)S(1)}, u32[]{:S(2)}, u32[]{:S(2)}) collective-permute-start(f32[2,1,3,8,256]{4,3,2,1,0:T(8,128)S(1)} %get-tuple-element.119), channel_id=1, source_target_pairs={{0,64},{64,128},{128,192},{192,0},{1,65},{65,129},{129,193},{193,1... | collective-permute-start | bytes 147464 | tf_op jit(solution)/shard_map/ppermute | solution.py:467
  4.4 0.3 collective-permute-start.3
  4.7 4.8 %collective-permute-start.1 = (f32[2,4,3,8,256]{4,3,2,1,0:T(8,128)S(1)}, f32[2,4,3,8,256]{4,3,2,1,0:T(8,128)S(1)}, u32[]{:S(2)}, u32[]{:S(2)}) collective-permute-start(f32[2,4,3,8,256]{4,3,2,1,0:T(8,128)S(1)} %pack.1.refs_0_), channel_id=1, source_target_pairs={{0,12},{1,13},{2,14},{3,15},{4,0},{5,1},{6,2},{7,3},{8,4},{9,5},{1... | collective-permute-start | bytes 589832 | tf_op jit(solution)/shard_map/ppermute | solution.py:456
  9.5 0.0 collective-permute-start
  9.5 0.0 collective-permute-done.2
  9.5 0.0 collective-permute-done.3
  9.6 2.6 %collective-permute-start.8 = (f32[2,6,3,8,256]{4,3,2,1,0:T(8,128)S(1)}, f32[2,6,3,8,256]{4,3,2,1,0:T(8,128)S(1)}, u32[]{:S(2)}, u32[]{:S(2)}) collective-permute-start(f32[2,6,3,8,256]{4,3,2,1,0:T(8,128)S(1)} %pad_maximum_fusion.1.refs_0_), channel_id=1, source_target_pairs={{0,3},{1,0},{2,1},{3,2},{4,7},{5,4},{6,5},{7,6},{8,11},{9,8},{10,9... | collective-permute-start | bytes 884744 | tf_op jit(solution)/shard_map/ppermute | solution.py:456
  12.1 0.0 collective-permute-start.7
  12.1 0.9 slice.40
  13.1 2.4 %collective-permute-start.4 = (f32[18,256]{1,0:T(8,128)S(1)}, f32[18,256]{1,0:T(8,128)S(1)}, u32[]{:S(2)}, u32[]{:S(2)}) collective-permute-start(f32[18,256]{1,0:T(8,128)S(1)} %bitcast.47), channel_id=1, source_target_pairs={{0,64},{64,128},{128,192},{192,0},{1,65},{65,129},{129,193},{193,1... | collective-permute-start | bytes 55304 | tf_op jit(solution)/shard_map/ppermute | solution.py:472
  15.4 0.9 collective-permute-done.4.refs_2_.refs_3_
  16.4 0.9 copy-done
  17.3 0.7 waves.3
  18.1 0.0 collective-permute-done.1.refs_4_
  18.1 1.6 %collective-permute-done.refs_1_ = f32[2,4,3,8,256]{4,3,2,1,0:T(8,128)S(1)} collective-permute-done((f32[2,4,3,8,256]{4,3,2,1,0:T(8,128)S(1)}, f32[2,4,3,8,256]{4,3,2,1,0:T(8,128)S(1)}, u32[]{:S(2)}, u32[]{:S(2)}) %collective-permute-start) | collective-permute-done | bytes 196640 | tf_op jit(solution)/shard_map/ppermute | solution.py:456
  19.7 0.0 collective-permute-done.8.refs_1_
  19.7 0.4 collective-permute-done.7.refs_0_
  20.2 2.1 %collective-permute-start.10 = (f32[6,3,8,256]{3,2,1,0:T(8,128)S(1)}, f32[6,3,8,256]{3,2,1,0:T(8,128)S(1)}, u32[]{:S(2)}, u32[]{:S(2)}) collective-permute-start(f32[6,3,8,256]{3,2,1,0:T(8,128)S(1)} %slice_bitcast_fusion), channel_id=1, source_target_pairs={{0,3},{1,0},{2,1},{3,2},{4,7},{5,4},{6,5},{7,6},{8,11},{9,8},{10,9... | collective-permute-start | bytes 442376 | tf_op jit(solution)/shard_map/ppermute | solution.py:460
  22.3 0.0 collective-permute-start.9
  22.3 3.7 %collective-permute-start.6 = (f32[4,3,8,256]{3,2,1,0:T(8,128)S(1)}, f32[4,3,8,256]{3,2,1,0:T(8,128)S(1)}, u32[]{:S(2)}, u32[]{:S(2)}) collective-permute-start(f32[4,3,8,256]{3,2,1,0:T(8,128)S(1)} %slice_bitcast_fusion.2), channel_id=1, source_target_pairs={{0,12},{1,13},{2,14},{3,15},{4,0},{5,1},{6,2},{7,3},{8,4},{9,5},{1... | collective-permute-start | bytes 294920 | tf_op jit(solution)/shard_map/ppermute | solution.py:460
  26.0 0.0 collective-permute-start.5
  26.0 0.7 phases.1
  26.7 1.4 %waves.4 = (bf16[4,48,1536]{2,1,0:T(8,128)(2,1)S(1)}, bf16[4,48,1536]{2,1,0:T(8,128)(2,1)S(1)}, bf16[4,48,1536]{2,1,0:T(8,128)(2,1)S(1)}, bf16[4,48,1536]{2,1,0:T(8,128)(2,1)S(1)}) custom-call(f32[2,6,3,8,256]{4,3,2,1,0:T(8,128)S(1)} %collective-permute-done.7.refs_0_, f32[2,6,3,8,256]{4,3,2,1,0:T(8,128)S(1)} %collective-permute-done.8.refs_1_, ...), custom_call_target="tpu_custom_call" | custom-call | flops 20000000 | bytes 4000000 | tf_op jit(solution)/shard_map/waves/pallas_call | solution.py:176
  28.2 0.0 collective-permute-done.10.refs_1_
  28.2 0.0 collective-permute-done.9.refs_0_
  28.2 0.7 waves.5
  28.9 0.0 collective-permute-done.6.refs_3_
  28.9 3.1 %collective-permute-done.5.refs_2_ = f32[4,3,8,256]{3,2,1,0:T(8,128)S(1)} collective-permute-done((f32[4,3,8,256]{3,2,1,0:T(8,128)S(1)}, f32[4,3,8,256]{3,2,1,0:T(8,128)S(1)}, u32[]{:S(2)}, u32[]{:S(2)}) %collective-permute-start.5) | collective-permute-done | bytes 98336 | tf_op jit(solution)/shard_map/ppermute | solution.py:460
  32.1 2.6 %elementals.1 = f32[2,2,3,8,128]{4,3,2,1,0:T(8,128)S(1)} custom-call(s32[3]{0:T(128)S(1)} %copy-done.5, f32[2,4,3,8,256]{4,3,2,1,0:T(8,128)S(1)} %pack.1.refs_0_, f32[2,4,3,8,256]{4,3,2,1,0:T(8,128)S(1)} %collective-permute-done.refs_1_, f32[4,3,8,256]{3,2,1,0:T(8,128)S(1)} %collective-permute-done.5.refs_2_, ...), custom_call_target="tpu_custom_call" | custom-call | flops 1000000000 | bytes 3000000 | tf_op jit(solution)/shard_map/elementals/pallas_call | solution.py:239
  34.7 0.1 collective-permute-start.12
  34.8 6.2 %collective-permute-start.13 = (f32[2,3,8,128]{3,2,1,0:T(8,128)S(1)}, f32[2,3,8,128]{3,2,1,0:T(8,128)S(1)}, u32[]{:S(2)}, u32[]{:S(2)}) collective-permute-start(f32[2,3,8,128]{3,2,1,0:T(8,128)S(1)} %get-tuple-element.124), channel_id=1, source_target_pairs={{0,192},{64,128},{128,64},{192,0},{1,193},{65,129},{129,65},{193,1... | collective-permute-start | bytes 73736 | tf_op jit(solution)/shard_map/ppermute | solution.py:491
  41.0 0.0 collective-permute-start.11
  41.0 1.8 %collective-permute-done.13 = f32[2,3,8,128]{3,2,1,0:T(8,128)S(1)} collective-permute-done((f32[2,3,8,128]{3,2,1,0:T(8,128)S(1)}, f32[2,3,8,128]{3,2,1,0:T(8,128)S(1)}, u32[]{:S(2)}, u32[]{:S(2)}) %collective-permute-start.13) | collective-permute-done | bytes 24608 | tf_op jit(solution)/shard_map/ppermute | solution.py:491
  42.8 0.0 collective-permute-done.11
  42.8 0.9 collective-permute-start.16
  43.7 0.7 collective-permute-start.15
  44.5 2.3 %collective-permute-start.14 = (f32[2,3,8,128]{3,2,1,0:T(8,128)S(1)}, f32[2,3,8,128]{3,2,1,0:T(8,128)S(1)}, u32[]{:S(2)}, u32[]{:S(2)}) collective-permute-start(f32[2,3,8,128]{3,2,1,0:T(8,128)S(1)} %add_add_fusion), channel_id=1, source_target_pairs={{0,4},{1,5},{2,6},{3,7},{4,8},{5,9},{6,10},{7,11},{8,12},{9,13},{1... | collective-permute-start | bytes 73736 | tf_op jit(solution)/shard_map/ppermute | solution.py:494
  48.0 1.3 %prepare.1 = (bf16[256,1024]{1,0:T(8,128)(2,1)S(1)}, bf16[256,1024]{1,0:T(8,128)(2,1)S(1)}, bf16[512,1024]{1,0:T(8,128)(2,1)S(1)}, bf16[512,1024]{1,0:T(8,128)(2...) custom-call(s32[1]{0:T(128)S(6)} %copy.19.ins_time, ...), custom_call_target="tpu_custom_call" | custom-call | flops 100000000 | bytes 8000000 | tf_op jit(solution)/shard_map/prepare/pallas_call | solution.py:323
  49.3 1.0 %collective-permute-done.15 = f32[2,3,8,128]{3,2,1,0:T(8,128)S(1)} collective-permute-done((f32[2,3,8,128]{3,2,1,0:T(8,128)S(1)}, f32[2,3,8,128]{3,2,1,0:T(8,128)S(1)}, u32[]{:S(2)}, u32[]{:S(2)}) %collective-permute-start.15) | collective-permute-done | bytes 24608 | tf_op jit(solution)/shard_map/ppermute | solution.py:494
  50.3 0.3 collective-permute-start.18
  50.6 1.6 %collective-permute-start.17 = (f32[4,2,3,8,128]{4,3,2,1,0:T(8,128)S(1)}, f32[4,2,3,8,128]{4,3,2,1,0:T(8,128)S(1)}, u32[]{:S(2)}, u32[]{:S(2)}) collective-permute-start(f32[4,2,3,8,128]{4,3,2,1,0:T(8,128)S(1)} %get-tuple-element.122), channel_id=1, source_target_pairs={{0,1},{1,2},{2,3},{3,0},{4,5},{5,6},{6,7},{7,4},{8,9},{9,10},{10,1... | collective-permute-start | bytes 294920 | tf_op jit(solution)/shard_map/ppermute | solution.py:498
  52.2 1.1 %collective-permute-start.19 = (f32[4,2,3,8,128]{4,3,2,1,0:T(8,128)S(1)}, f32[4,2,3,8,128]{4,3,2,1,0:T(8,128)S(1)}, u32[]{:S(2)}, u32[]{:S(2)}) collective-permute-start(f32[4,2,3,8,128]{4,3,2,1,0:T(8,128)S(1)} %get-tuple-element.122), channel_id=1, source_target_pairs={{0,3},{1,0},{2,1},{3,2},{4,7},{5,4},{6,5},{7,6},{8,11},{9,8},{10,9... | collective-permute-start | bytes 294920 | tf_op jit(solution)/shard_map/ppermute | solution.py:498
  53.3 2.2 %collective-permute-done.18 = f32[4,2,3,8,128]{4,3,2,1,0:T(8,128)S(1)} collective-permute-done((f32[4,2,3,8,128]{4,3,2,1,0:T(8,128)S(1)}, f32[4,2,3,8,128]{4,3,2,1,0:T(8,128)S(1)}, u32[]{:S(2)}, u32[]{:S(2)}) %collective-permute-start.18) | collective-permute-done | bytes 98336 | tf_op jit(solution)/shard_map/ppermute | solution.py:498
  55.5 0.8 collective-permute-done.17
  56.3 0.0 collective-permute-done.19
  56.4 4.9 %collective-permute-start.20 = (f32[4,4,2,3,8,128]{5,4,3,2,1,0:T(8,128)S(1)}, f32[4,4,2,3,8,128]{5,4,3,2,1,0:T(8,128)S(1)}, u32[]{:S(2)}, u32[]{:S(2)}) collective-permute-start(f32[4,4,2,3,8,128]{5,4,3,2,1,0:T(8,128)S(1)} %pad_maximum_fusion.mine), channel_id=1, source_target_pairs={{0,64},{64,0},{128,192},{192,128},{1,65},{65,1},{129,193},{193,129... | collective-permute-start | bytes 1179656 | tf_op jit(solution)/shard_map/ppermute | solution.py:499
  61.2 1.3 %collective-permute-done.20.others = f32[4,4,2,3,8,128]{5,4,3,2,1,0:T(8,128)S(1)} collective-permute-done((f32[4,4,2,3,8,128]{5,4,3,2,1,0:T(8,128)S(1)}, f32[4,4,2,3,8,128]{5,4,3,2,1,0:T(8,128)S(1)}, u32[]{:S(2)}, u32[]{:S(2)}) %collective-permute-start.20) | collective-permute-done | bytes 393248 | tf_op jit(solution)/shard_map/ppermute | solution.py:499
  62.6 3.3 %left.1 = (bf16[1024,768]{1,0:T(8,128)(2,1)S(1)}, bf16[1024,768]{1,0:T(8,128)(2,1)S(1)}, f32[128,768]{1,0:T(8,128)S(1)}, f32[128,768]{1,0:T(8,128)S(1)}) custom-call(f32[4,4,2,3,8,128]{5,4,3,2,1,0:T(8,128)S(1)} %pad_maximum_fusion.mine, f32[4,4,2,3,8,128]{5,4,3,2,1,0:T(8,128)S(1)} %collective-permute-done.20.others, ...), custom_call_target="tpu_custom_call" | custom-call | flops 1000000000 | bytes 4000000 | tf_op jit(solution)/shard_map/left/pallas_call | solution.py:374
  65.9 1.4 %collective-permute-start.21 = (f32[128,768]{1,0:T(8,128)S(1)}, f32[128,768]{1,0:T(8,128)S(1)}, u32[]{:S(2)}, u32[]{:S(2)}) collective-permute-start(f32[128,768]{1,0:T(8,128)S(1)} %get-tuple-element.114), channel_id=1, source_target_pairs={{0,16},{16,32},{32,48},{48,0},{1,17},{17,33},{33,49},{49,1},{2,18}... | collective-permute-start | bytes 1179656 | tf_op jit(solution)/shard_map/ppermute | solution.py:506
  67.3 1.5 %collective-permute-start.25 = (f32[128,768]{1,0:T(8,128)S(1)}, f32[128,768]{1,0:T(8,128)S(1)}, u32[]{:S(2)}, u32[]{:S(2)}) collective-permute-start(f32[128,768]{1,0:T(8,128)S(1)} %get-tuple-element.118), channel_id=1, source_target_pairs={{0,48},{16,0},{32,16},{48,32},{1,49},{17,1},{33,17},{49,33},{2,50}... | collective-permute-start | bytes 1179656 | tf_op jit(solution)/shard_map/ppermute | solution.py:509
  68.8 2.6 %right.2 = (f32[128,768]{1,0:T(8,128)S(1)}, f32[128,768]{1,0:T(8,128)S(1)}, f32[128,768]{1,0:T(8,128)S(1)}, f32[128,768]{1,0:T(8,128)S(1)}) custom-call(bf16[512,1024]{1,0:T(8,128)(2,1)S(1)} %get-tuple-element.94.src_hi, bf16[512,1024]{1,0:T(8,128)(2,1)S(1)} %get-tuple-element.95.src_lo, bf16[1024,768]{1,0:T(8,128)(2,1)S(1)} %get-tuple-element.103.left_hi, ...), custom_call_target="tpu_custom_call" | custom-call | flops 1000000000 | bytes 5000000 | tf_op jit(solution)/shard_map/right/pallas_call | solution.py:397
  71.4 1.4 %right.3 = (f32[128,768]{1,0:T(8,128)S(1)}, f32[128,768]{1,0:T(8,128)S(1)}) custom-call(bf16[256,1024]{1,0:T(8,128)(2,1)S(1)} %get-tuple-element.107.src_hi, bf16[256,1024]{1,0:T(8,128)(2,1)S(1)} %get-tuple-element.108.src_lo, bf16[1024,768]{1,0:T(8,128)(2,1)S(1)} %get-tuple-element.103.left_hi, bf16[1024,768]{1,0:T(8,128)(2,1)S(1)} %get-tuple-element.104.left_lo), custom_call_target="tpu_custom_call" | custom-call | flops 1000000000 | bytes 5000000 | tf_op jit(solution)/shard_map/right/pallas_call | solution.py:397
  72.8 0.1 collective-permute-start.23
  72.9 2.7 %collective-permute-start.24 = (f32[128,768]{1,0:T(8,128)S(1)}, f32[128,768]{1,0:T(8,128)S(1)}, u32[]{:S(2)}, u32[]{:S(2)}) collective-permute-start(f32[128,768]{1,0:T(8,128)S(1)} %get-tuple-element.116), channel_id=1, source_target_pairs={{0,48},{16,0},{32,16},{48,32},{1,49},{17,1},{33,17},{49,33},{2,50}... | collective-permute-start | bytes 1179656 | tf_op jit(solution)/shard_map/ppermute | solution.py:509
  75.6 2.1 %collective-permute-done.21.second = f32[128,768]{1,0:T(8,128)S(1)} collective-permute-done((f32[128,768]{1,0:T(8,128)S(1)}, f32[128,768]{1,0:T(8,128)S(1)}, u32[]{:S(2)}, u32[]{:S(2)}) %collective-permute-start.21) | collective-permute-done | bytes 393248 | tf_op jit(solution)/shard_map/ppermute | solution.py:506
  77.7 0.1 collective-permute-start.22
  77.9 2.7 %collective-permute-start.26 = (f32[128,768]{1,0:T(8,128)S(1)}, f32[128,768]{1,0:T(8,128)S(1)}, u32[]{:S(2)}, u32[]{:S(2)}) collective-permute-start(f32[128,768]{1,0:T(8,128)S(1)} %relay.3), channel_id=1, source_target_pairs={{0,48},{16,0},{32,16},{48,32},{1,49},{17,1},{33,17},{49,33},{2,50}... | collective-permute-start | bytes 1179656 | tf_op jit(solution)/shard_map/ppermute | solution.py:509
  80.6 5.5 %collective-permute-done.23.refs_3_ = f32[128,768]{1,0:T(8,128)S(1)} collective-permute-done((f32[128,768]{1,0:T(8,128)S(1)}, f32[128,768]{1,0:T(8,128)S(1)}, u32[]{:S(2)}, u32[]{:S(2)}) %collective-permute-start.23) | collective-permute-done | bytes 393248 | tf_op jit(solution)/shard_map/ppermute | solution.py:506
  86.1 0.0 collective-permute-done.24.refs_4_
  86.1 8.4 %collective-permute-done.22.refs_2_ = f32[128,768]{1,0:T(8,128)S(1)} collective-permute-done((f32[128,768]{1,0:T(8,128)S(1)}, f32[128,768]{1,0:T(8,128)S(1)}, u32[]{:S(2)}, u32[]{:S(2)}) %collective-permute-start.22) | collective-permute-done | bytes 393248 | tf_op jit(solution)/shard_map/ppermute | solution.py:506
  94.5 0.0 collective-permute-done.26.refs_5_
  94.5 1.4 %final.1 = f32[128,6,2,128]{3,2,1,0:T(2,128)} custom-call(f32[128,768]{1,0:T(8,128)S(1)} %get-tuple-element.111.refs_0_, f32[128,768]{1,0:T(8,128)S(1)} %get-tuple-element.112.refs_1_, f32[128,768]{1,0:T(8,128)S(1)} %collective-permute-done.22.refs_2_, f32[128,768]{1,0:T(8,128)S(1)} %collective-permute-done.23.refs_3_, ...), custom_call_target="tpu_custom_call" | custom-call | tf_op jit(solution)/shard_map/final/pallas_call | solution.py:433
  (29 shorter events, 0.2 us)
Async XLA Ops:
  0.0 26.7 %copy-start.1 = (f32[1,3,2,3,3,4,256]{6,5,4,3,2,1,0:T(4,128)S(1)}, f32[1,3,2,3,3,4,256]{6,5,4,3,2,1,0:T(4,128)}, u32[]{:S(2)}) copy-start(f32[1,3,2,3,3,4,256]{6,5,4,3,2,1,0:T(4,128)} %param.9) | copy-start | bytes 663556
  0.0 1.0 %copy-start.4 = (f32[1,2,3,8,4,256]{5,4,3,2,1,0:T(4,128)S(1)}, f32[1,2,3,8,4,256]{5,4,3,2,1,0:T(4,128)}, u32[]{:S(2)}) copy-start(f32[1,2,3,8,4,256]{5,4,3,2,1,0:T(4,128)} %param.8) | copy-start | bytes 589828
  1.0 25.1 %copy-start.5 = (s32[3]{0:T(128)S(1)}, s32[3]{0:T(128)}, u32[]{:S(2)}) copy-start(s32[3]{0:T(128)} %directions.3) | copy-start | bytes 40
  1.0 25.1 %copy-start.6 = (s32[2,3]{1,0:T(2,128)S(1)}, s32[2,3]{1,0:T(2,128)}, u32[]{:S(2)}) copy-start(s32[2,3]{1,0:T(2,128)} %momenta.1) | copy-start | bytes 76
  1.3 8.2 %collective-permute-start.2 = (f32[2,1,3,8,256]{4,3,2,1,0:T(8,128)S(1)}, f32[2,1,3,8,256]{4,3,2,1,0:T(8,128)S(1)}, u32[]{:S(2)}, u32[]{:S(2)}) collective-permute-start(f32[2,1,3,8,256]{4,3,2,1,0:T(8,128)S(1)} %get-tuple-element.119), channel_id=1, source_target_pairs={{0,64},{64,128},{128,192},{192,0},{1,65},{65,129},{129,193},{193,1... | collective-permute-start | bytes 147464 | tf_op jit(solution)/shard_map/ppermute | solution.py:467
  4.4 5.1 %collective-permute-start.3 = (f32[2,1,3,8,256]{4,3,2,1,0:T(8,128)S(1)}, f32[2,1,3,8,256]{4,3,2,1,0:T(8,128)S(1)}, u32[]{:S(2)}, u32[]{:S(2)}) collective-permute-start(f32[2,1,3,8,256]{4,3,2,1,0:T(8,128)S(1)} %get-tuple-element.120), channel_id=1, source_target_pairs={{0,192},{64,0},{128,64},{192,128},{1,193},{65,1},{129,65},{193,129... | collective-permute-start | bytes 147464 | tf_op jit(solution)/shard_map/ppermute | solution.py:468
  4.7 13.3 %collective-permute-start.1 = (f32[2,4,3,8,256]{4,3,2,1,0:T(8,128)S(1)}, f32[2,4,3,8,256]{4,3,2,1,0:T(8,128)S(1)}, u32[]{:S(2)}, u32[]{:S(2)}) collective-permute-start(f32[2,4,3,8,256]{4,3,2,1,0:T(8,128)S(1)} %pack.1.refs_0_), channel_id=1, source_target_pairs={{0,12},{1,13},{2,14},{3,15},{4,0},{5,1},{6,2},{7,3},{8,4},{9,5},{1... | collective-permute-start | bytes 589832 | tf_op jit(solution)/shard_map/ppermute | solution.py:456
  9.5 10.2 %collective-permute-start = (f32[2,4,3,8,256]{4,3,2,1,0:T(8,128)S(1)}, f32[2,4,3,8,256]{4,3,2,1,0:T(8,128)S(1)}, u32[]{:S(2)}, u32[]{:S(2)}) collective-permute-start(f32[2,4,3,8,256]{4,3,2,1,0:T(8,128)S(1)} %pack.1.refs_0_), channel_id=1, source_target_pairs={{0,4},{1,5},{2,6},{3,7},{4,8},{5,9},{6,10},{7,11},{8,12},{9,13},{1... | collective-permute-start | bytes 589832 | tf_op jit(solution)/shard_map/ppermute | solution.py:456
  9.6 10.1 %collective-permute-start.8 = (f32[2,6,3,8,256]{4,3,2,1,0:T(8,128)S(1)}, f32[2,6,3,8,256]{4,3,2,1,0:T(8,128)S(1)}, u32[]{:S(2)}, u32[]{:S(2)}) collective-permute-start(f32[2,6,3,8,256]{4,3,2,1,0:T(8,128)S(1)} %pad_maximum_fusion.1.refs_0_), channel_id=1, source_target_pairs={{0,3},{1,0},{2,1},{3,2},{4,7},{5,4},{6,5},{7,6},{8,11},{9,8},{10,9... | collective-permute-start | bytes 884744 | tf_op jit(solution)/shard_map/ppermute | solution.py:456
  12.1 8.0 %collective-permute-start.7 = (f32[2,6,3,8,256]{4,3,2,1,0:T(8,128)S(1)}, f32[2,6,3,8,256]{4,3,2,1,0:T(8,128)S(1)}, u32[]{:S(2)}, u32[]{:S(2)}) collective-permute-start(f32[2,6,3,8,256]{4,3,2,1,0:T(8,128)S(1)} %pad_maximum_fusion.1.refs_0_), channel_id=1, source_target_pairs={{0,1},{1,2},{2,3},{3,0},{4,5},{5,6},{6,7},{7,4},{8,9},{9,10},{10,1... | collective-permute-start | bytes 884744 | tf_op jit(solution)/shard_map/ppermute | solution.py:456
  13.1 3.3 %collective-permute-start.4 = (f32[18,256]{1,0:T(8,128)S(1)}, f32[18,256]{1,0:T(8,128)S(1)}, u32[]{:S(2)}, u32[]{:S(2)}) collective-permute-start(f32[18,256]{1,0:T(8,128)S(1)} %bitcast.47), channel_id=1, source_target_pairs={{0,64},{64,128},{128,192},{192,0},{1,65},{65,129},{129,193},{193,1... | collective-permute-start | bytes 55304 | tf_op jit(solution)/shard_map/ppermute | solution.py:472
  16.4 0.9 copy-start
  20.2 8.0 %collective-permute-start.10 = (f32[6,3,8,256]{3,2,1,0:T(8,128)S(1)}, f32[6,3,8,256]{3,2,1,0:T(8,128)S(1)}, u32[]{:S(2)}, u32[]{:S(2)}) collective-permute-start(f32[6,3,8,256]{3,2,1,0:T(8,128)S(1)} %slice_bitcast_fusion), channel_id=1, source_target_pairs={{0,3},{1,0},{2,1},{3,2},{4,7},{5,4},{6,5},{7,6},{8,11},{9,8},{10,9... | collective-permute-start | bytes 442376 | tf_op jit(solution)/shard_map/ppermute | solution.py:460
  22.3 5.8 %collective-permute-start.9 = (f32[6,3,8,256]{3,2,1,0:T(8,128)S(1)}, f32[6,3,8,256]{3,2,1,0:T(8,128)S(1)}, u32[]{:S(2)}, u32[]{:S(2)}) collective-permute-start(f32[6,3,8,256]{3,2,1,0:T(8,128)S(1)} %slice_bitcast_fusion.1), channel_id=1, source_target_pairs={{0,1},{1,2},{2,3},{3,0},{4,5},{5,6},{6,7},{7,4},{8,9},{9,10},{10,1... | collective-permute-start | bytes 442376 | tf_op jit(solution)/shard_map/ppermute | solution.py:460
  22.3 6.6 %collective-permute-start.6 = (f32[4,3,8,256]{3,2,1,0:T(8,128)S(1)}, f32[4,3,8,256]{3,2,1,0:T(8,128)S(1)}, u32[]{:S(2)}, u32[]{:S(2)}) collective-permute-start(f32[4,3,8,256]{3,2,1,0:T(8,128)S(1)} %slice_bitcast_fusion.2), channel_id=1, source_target_pairs={{0,12},{1,13},{2,14},{3,15},{4,0},{5,1},{6,2},{7,3},{8,4},{9,5},{1... | collective-permute-start | bytes 294920 | tf_op jit(solution)/shard_map/ppermute | solution.py:460
  26.0 6.0 %collective-permute-start.5 = (f32[4,3,8,256]{3,2,1,0:T(8,128)S(1)}, f32[4,3,8,256]{3,2,1,0:T(8,128)S(1)}, u32[]{:S(2)}, u32[]{:S(2)}) collective-permute-start(f32[4,3,8,256]{3,2,1,0:T(8,128)S(1)} %slice_bitcast_fusion.3), channel_id=1, source_target_pairs={{0,4},{1,5},{2,6},{3,7},{4,8},{5,9},{6,10},{7,11},{8,12},{9,13},{1... | collective-permute-start | bytes 294920 | tf_op jit(solution)/shard_map/ppermute | solution.py:460
  32.1 16.0 %copy-start.2 = (f32[1,2,512,512]{3,2,1,0:T(8,128)S(1)}, f32[1,2,512,512]{3,2,1,0:T(8,128)}, u32[]{:S(2)}) copy-start(f32[1,2,512,512]{3,2,1,0:T(8,128)} %param.15) | copy-start | bytes 6291460
  32.1 16.0 %copy-start.3 = (f32[1,1,2,128,512]{4,3,2,1,0:T(8,128)S(1)}, f32[1,1,2,128,512]{4,3,2,1,0:T(8,128)}, u32[]{:S(2)}) copy-start(f32[1,1,2,128,512]{4,3,2,1,0:T(8,128)} %param.14) | copy-start | bytes 1572868
  34.7 6.3 %collective-permute-start.12 = (f32[2,3,8,128]{3,2,1,0:T(8,128)S(1)}, f32[2,3,8,128]{3,2,1,0:T(8,128)S(1)}, u32[]{:S(2)}, u32[]{:S(2)}) collective-permute-start(f32[2,3,8,128]{3,2,1,0:T(8,128)S(1)} %get-tuple-element.123), channel_id=1, source_target_pairs={{0,128},{64,192},{128,0},{192,64},{1,129},{65,193},{129,1},{193,65... | collective-permute-start | bytes 73736 | tf_op jit(solution)/shard_map/ppermute | solution.py:490
  34.8 8.0 %collective-permute-start.13 = (f32[2,3,8,128]{3,2,1,0:T(8,128)S(1)}, f32[2,3,8,128]{3,2,1,0:T(8,128)S(1)}, u32[]{:S(2)}, u32[]{:S(2)}) collective-permute-start(f32[2,3,8,128]{3,2,1,0:T(8,128)S(1)} %get-tuple-element.124), channel_id=1, source_target_pairs={{0,192},{64,128},{128,64},{192,0},{1,193},{65,129},{129,65},{193,1... | collective-permute-start | bytes 73736 | tf_op jit(solution)/shard_map/ppermute | solution.py:491
  41.0 1.8 %collective-permute-start.11 = (f32[2,3,8,128]{3,2,1,0:T(8,128)S(1)}, f32[2,3,8,128]{3,2,1,0:T(8,128)S(1)}, u32[]{:S(2)}, u32[]{:S(2)}) collective-permute-start(f32[2,3,8,128]{3,2,1,0:T(8,128)S(1)} %get-tuple-element.124), channel_id=1, source_target_pairs={{0,64},{64,0},{128,192},{192,128},{1,65},{65,1},{129,193},{193,129... | collective-permute-start | bytes 73736 | tf_op jit(solution)/shard_map/ppermute | solution.py:489
  42.8 6.5 %collective-permute-start.16 = (f32[2,3,8,128]{3,2,1,0:T(8,128)S(1)}, f32[2,3,8,128]{3,2,1,0:T(8,128)S(1)}, u32[]{:S(2)}, u32[]{:S(2)}) collective-permute-start(f32[2,3,8,128]{3,2,1,0:T(8,128)S(1)} %add_add_fusion), channel_id=1, source_target_pairs={{0,12},{1,13},{2,14},{3,15},{4,0},{5,1},{6,2},{7,3},{8,4},{9,5},{1... | collective-permute-start | bytes 73736 | tf_op jit(solution)/shard_map/ppermute | solution.py:494
  43.7 6.6 %collective-permute-start.15 = (f32[2,3,8,128]{3,2,1,0:T(8,128)S(1)}, f32[2,3,8,128]{3,2,1,0:T(8,128)S(1)}, u32[]{:S(2)}, u32[]{:S(2)}) collective-permute-start(f32[2,3,8,128]{3,2,1,0:T(8,128)S(1)} %add_add_fusion), channel_id=1, source_target_pairs={{0,8},{1,9},{2,10},{3,11},{4,12},{5,13},{6,14},{7,15},{8,0},{9,1},... | collective-permute-start | bytes 73736 | tf_op jit(solution)/shard_map/ppermute | solution.py:494
  44.5 5.9 %collective-permute-start.14 = (f32[2,3,8,128]{3,2,1,0:T(8,128)S(1)}, f32[2,3,8,128]{3,2,1,0:T(8,128)S(1)}, u32[]{:S(2)}, u32[]{:S(2)}) collective-permute-start(f32[2,3,8,128]{3,2,1,0:T(8,128)S(1)} %add_add_fusion), channel_id=1, source_target_pairs={{0,4},{1,5},{2,6},{3,7},{4,8},{5,9},{6,10},{7,11},{8,12},{9,13},{1... | collective-permute-start | bytes 73736 | tf_op jit(solution)/shard_map/ppermute | solution.py:494
  50.3 5.2 %collective-permute-start.18 = (f32[4,2,3,8,128]{4,3,2,1,0:T(8,128)S(1)}, f32[4,2,3,8,128]{4,3,2,1,0:T(8,128)S(1)}, u32[]{:S(2)}, u32[]{:S(2)}) collective-permute-start(f32[4,2,3,8,128]{4,3,2,1,0:T(8,128)S(1)} %get-tuple-element.122), channel_id=1, source_target_pairs={{0,2},{1,3},{2,0},{3,1},{4,6},{5,7},{6,4},{7,5},{8,10},{9,11},{10,... | collective-permute-start | bytes 294920 | tf_op jit(solution)/shard_map/ppermute | solution.py:498
  50.6 5.7 %collective-permute-start.17 = (f32[4,2,3,8,128]{4,3,2,1,0:T(8,128)S(1)}, f32[4,2,3,8,128]{4,3,2,1,0:T(8,128)S(1)}, u32[]{:S(2)}, u32[]{:S(2)}) collective-permute-start(f32[4,2,3,8,128]{4,3,2,1,0:T(8,128)S(1)} %get-tuple-element.122), channel_id=1, source_target_pairs={{0,1},{1,2},{2,3},{3,0},{4,5},{5,6},{6,7},{7,4},{8,9},{9,10},{10,1... | collective-permute-start | bytes 294920 | tf_op jit(solution)/shard_map/ppermute | solution.py:498
  52.2 4.2 %collective-permute-start.19 = (f32[4,2,3,8,128]{4,3,2,1,0:T(8,128)S(1)}, f32[4,2,3,8,128]{4,3,2,1,0:T(8,128)S(1)}, u32[]{:S(2)}, u32[]{:S(2)}) collective-permute-start(f32[4,2,3,8,128]{4,3,2,1,0:T(8,128)S(1)} %get-tuple-element.122), channel_id=1, source_target_pairs={{0,3},{1,0},{2,1},{3,2},{4,7},{5,4},{6,5},{7,6},{8,11},{9,8},{10,9... | collective-permute-start | bytes 294920 | tf_op jit(solution)/shard_map/ppermute | solution.py:498
  56.4 6.2 %collective-permute-start.20 = (f32[4,4,2,3,8,128]{5,4,3,2,1,0:T(8,128)S(1)}, f32[4,4,2,3,8,128]{5,4,3,2,1,0:T(8,128)S(1)}, u32[]{:S(2)}, u32[]{:S(2)}) collective-permute-start(f32[4,4,2,3,8,128]{5,4,3,2,1,0:T(8,128)S(1)} %pad_maximum_fusion.mine), channel_id=1, source_target_pairs={{0,64},{64,0},{128,192},{192,128},{1,65},{65,1},{129,193},{193,129... | collective-permute-start | bytes 1179656 | tf_op jit(solution)/shard_map/ppermute | solution.py:499
  65.9 11.7 %collective-permute-start.21 = (f32[128,768]{1,0:T(8,128)S(1)}, f32[128,768]{1,0:T(8,128)S(1)}, u32[]{:S(2)}, u32[]{:S(2)}) collective-permute-start(f32[128,768]{1,0:T(8,128)S(1)} %get-tuple-element.114), channel_id=1, source_target_pairs={{0,16},{16,32},{32,48},{48,0},{1,17},{17,33},{33,49},{49,1},{2,18}... | collective-permute-start | bytes 1179656 | tf_op jit(solution)/shard_map/ppermute | solution.py:506
  67.3 10.5 %collective-permute-start.25 = (f32[128,768]{1,0:T(8,128)S(1)}, f32[128,768]{1,0:T(8,128)S(1)}, u32[]{:S(2)}, u32[]{:S(2)}) collective-permute-start(f32[128,768]{1,0:T(8,128)S(1)} %get-tuple-element.118), channel_id=1, source_target_pairs={{0,48},{16,0},{32,16},{48,32},{1,49},{17,1},{33,17},{49,33},{2,50}... | collective-permute-start | bytes 1179656 | tf_op jit(solution)/shard_map/ppermute | solution.py:509
  72.8 13.3 %collective-permute-start.23 = (f32[128,768]{1,0:T(8,128)S(1)}, f32[128,768]{1,0:T(8,128)S(1)}, u32[]{:S(2)}, u32[]{:S(2)}) collective-permute-start(f32[128,768]{1,0:T(8,128)S(1)} %get-tuple-element.115), channel_id=1, source_target_pairs={{0,16},{16,32},{32,48},{48,0},{1,17},{17,33},{33,49},{49,1},{2,18}... | collective-permute-start | bytes 1179656 | tf_op jit(solution)/shard_map/ppermute | solution.py:506
  72.9 13.2 %collective-permute-start.24 = (f32[128,768]{1,0:T(8,128)S(1)}, f32[128,768]{1,0:T(8,128)S(1)}, u32[]{:S(2)}, u32[]{:S(2)}) collective-permute-start(f32[128,768]{1,0:T(8,128)S(1)} %get-tuple-element.116), channel_id=1, source_target_pairs={{0,48},{16,0},{32,16},{48,32},{1,49},{17,1},{33,17},{49,33},{2,50}... | collective-permute-start | bytes 1179656 | tf_op jit(solution)/shard_map/ppermute | solution.py:509
  77.7 16.8 %collective-permute-start.22 = (f32[128,768]{1,0:T(8,128)S(1)}, f32[128,768]{1,0:T(8,128)S(1)}, u32[]{:S(2)}, u32[]{:S(2)}) collective-permute-start(f32[128,768]{1,0:T(8,128)S(1)} %relay.2), channel_id=1, source_target_pairs={{0,16},{16,32},{32,48},{48,0},{1,17},{17,33},{33,49},{49,1},{2,18}... | collective-permute-start | bytes 1179656 | tf_op jit(solution)/shard_map/ppermute | solution.py:506
  77.9 16.7 %collective-permute-start.26 = (f32[128,768]{1,0:T(8,128)S(1)}, f32[128,768]{1,0:T(8,128)S(1)}, u32[]{:S(2)}, u32[]{:S(2)}) collective-permute-start(f32[128,768]{1,0:T(8,128)S(1)} %relay.3), channel_id=1, source_target_pairs={{0,48},{16,0},{32,16},{48,32},{1,49},{17,1},{33,17},{49,33},{2,50}... | collective-permute-start | bytes 1179656 | tf_op jit(solution)/shard_map/ppermute | solution.py:509
